TPU v7x, 32 devices: a whole 2x2x4 slice. The times are simulated.
32 devices in a mesh: gx: 8 (over y, x, core), gy: 4 (over z).
Axes of the slice: x: 2, y: 2, z: 4, core: 2. Of those that a mesh axis runs over, the one named last changes fastest.
Arguments:
- adjoint_start: float32 [2, 4, 2048, 1024], P(None, None, 'gx', 'gy'), may hold values from -6 to 6
- viscosity: float32 [4, 2048, 1024], P(None, 'gx', 'gy'), may hold values from 0.25 to 4
- base_velocity: float32 [2, 2048, 1024], P(None, 'gx', 'gy'), may hold values from -6 to 6
- surface_velocity: float32 [2, 2048, 1024], P(None, 'gx', 'gy'), may hold values from -6 to 6
- ice_mask: int32 [16, 8], P('gx', 'gy'), may hold values 0 or 1
- log_friction: float32 [2048, 1024], P(('gx', 'gy')), may hold values from -1 to 1
- observed_velocity: float32 [2, 2048, 1024], P(None, ('gx', 'gy')), may hold values from -6 to 6
- obs_weight: float32 [2, 2048, 1024], P(None, ('gx', 'gy')), may hold values from 0.2 to 2
Outputs:
- gradient: float32 [2048, 1024], P(('gx', 'gy'))
- adjoint: float32 [2, 4, 2048, 1024], P(None, None, 'gx', 'gy')
All inputs are finite; a program needn't handle non-finite values. No bound on the sum of `ice_mask` on one device may be relied on, other than what follows from the above.
Results may differ from a plain program's by a relative error of at most 0.00002.
Values sent between devices are 32-bit elements; how exact they have to be, the bound alone decides.
No kernel may reach another device: no remote copies, remote signals or barrier semaphores. Data moves between devices by JAX's collectives and lax.ppermute only.
A program may use at most 128 MiB of HBM per device.

v0:
```python
import functools

import jax
import jax.numpy as jnp
from jax import lax
from jax.experimental import pallas as pl
from jax.experimental.pallas import tpu as pltpu
from jax.sharding import PartitionSpec as P

SWEEPS = 4
DAMPING = 0.8
VERTICAL = 2.0
COUPLING = 3.0
TIKHONOV = 0.25

LAYERS = 4
LANES = 128
ROWS = 8
TILE = 256
FRAME = TILE + 2 * ROWS
HALF = TILE // 2
BLOCKS = TILE // ROWS
FIRST = 4
STEPS = BLOCKS + 1
TILE_FIELDS = 15
RIM_FIELDS = 20
VMEM_BYTES = 56 * 1024 * 1024


def lane_index():
    return lax.broadcasted_iota(jnp.int32, (ROWS, LANES), 1)


def roll_to(x, shift):
    shift = shift % LANES
    return x if shift == 0 else pltpu.roll(x, shift, 1)


def after(x, lane):
    a, b, c = (roll_to(v, -1) for v in x)
    last = lane == LANES - 1
    return jnp.where(last, b, a), jnp.where(last, c, b), jnp.where(last, a, c)


def before(x, lane):
    a, b, c = (roll_to(v, 1) for v in x)
    first = lane == 0
    return jnp.where(first, c, a), jnp.where(first, a, b), jnp.where(first, b, c)


def rim_slot(array, block, strip_blocks):
    position = array * strip_blocks + block
    return position // 16, position % 16


def rim_tiles(strip_rows):
    return -(-5 * (strip_rows // ROWS) // 16)


def control_rows(strip_rows):
    return 2 * strip_rows + 64 + ROWS * rim_tiles(strip_rows)


def pack_strips(n, strip_rows, logf, obs, weight, *outs):
    controls, datas = outs[:n], outs[n:]
    me = lax.axis_index("gy")
    lane = lane_index()
    blocks = strip_rows // ROWS
    edge = jnp.where(me == 0, 0, strip_rows - ROWS)
    edge = pl.multiple_of(edge, ROWS)
    strips = [logf.at[...], obs.at[0], obs.at[1], weight.at[0], weight.at[1]]
    width = n * TILE
    for k in range(n):
        to = lax.rem(me + k, n)
        column = pl.multiple_of(to * TILE, TILE)
        left = pl.multiple_of(jnp.maximum(column - LANES, 0), LANES)
        right = pl.multiple_of(jnp.minimum(column + TILE, width - LANES), LANES)
        control, data = controls[k], datas[k]
        for t in range(2):
            columns = pl.ds(column + t * LANES, LANES)
            control[pl.ds(t * strip_rows, strip_rows), :] = logf[:, columns]
            for a in range(4):
                data[a, t] = strips[a + 1][:, columns]
                control[pl.ds(2 * strip_rows + (a * 2 + t) * ROWS, ROWS), :] = strips[a + 1][pl.ds(edge, ROWS), columns]
        packed = [jnp.zeros((ROWS, LANES), jnp.float32) for _ in range(rim_tiles(strip_rows))]
        for a in range(5):
            for b in range(blocks):
                part, slot = rim_slot(a, b, blocks)
                rows = pl.ds(b * ROWS, ROWS)
                both = jnp.where(lane < 64, strips[a][rows, pl.ds(right, LANES)], strips[a][rows, pl.ds(left, LANES)])
                packed[part] = jnp.where(lane // 8 == slot, roll_to(both, 8 * slot + 4), packed[part])
        for part, value in enumerate(packed):
            control[pl.ds(2 * strip_rows + 64 + part * ROWS, ROWS), :] = value


def tile_field(a, adjoint, viscosity, surface):
    if a < 8:
        return adjoint.at[a]
    if a < 12:
        return viscosity.at[a - 8]
    return surface.at[a - 12]


def pack_columns(mask, adjoint, viscosity, surface, up, down):
    lane = lane_index()

    def step(r, carry):
        to_up = jnp.zeros((ROWS, LANES), jnp.float32)
        to_down = jnp.zeros((ROWS, LANES), jnp.float32)
        for h in range(2):
            rows = pl.ds(pl.multiple_of(h * HALF + r * ROWS, ROWS), ROWS)
            for a in range(TILE_FIELDS):
                slot = h * TILE_FIELDS + a
                here = lane // 4 == slot
                if a == TILE_FIELDS - 1:
                    low = mask[h, 0].astype(jnp.float32)
                    high = mask[h, 1].astype(jnp.float32)
                    to_up = jnp.where(here, high, to_up)
                    to_down = jnp.where(here, low, to_down)
                else:
                    field = tile_field(a, adjoint, viscosity, surface)
                    to_up = jnp.where(here, roll_to(field[rows, LANES:], 4 * slot + 4), to_up)
                    to_down = jnp.where(here, roll_to(field[rows, :LANES], 4 * slot), to_down)
        rows = pl.ds(pl.multiple_of(r * ROWS, ROWS), ROWS)
        up[rows, :] = to_up
        down[rows, :] = to_down
        return carry

    lax.fori_loop(0, HALF // ROWS, step, 0)


def side_columns(lane, from_left, from_right, slot):
    left = roll_to(from_left, -(4 * slot + 4))
    right = roll_to(from_right, -4 * slot)
    return jnp.where(lane < 4, right, jnp.where(lane >= LANES - 4, left, 0.0))


def strip_columns(lane, packed, slot):
    value = roll_to(packed, -(8 * slot + 4))
    return jnp.where(jnp.logical_or(lane < 4, lane >= LANES - 4), value, 0.0)


def pack_rows(n, strip_rows, mask, adjoint, viscosity, surface, from_left, from_right, *rest):
    controls, (up, down) = rest[:n], rest[n:]
    me = lax.axis_index("gy")
    lane = lane_index()
    blocks = strip_rows // ROWS
    for message, h, row, owner in ((up, 1, TILE - ROWS, n - 1), (down, 0, 0, 0)):
        rows = pl.ds(row, ROWS)
        packed_rows = pl.ds(row - h * HALF, ROWS)
        left, right = from_left[packed_rows, :], from_right[packed_rows, :]
        for a in range(TILE_FIELDS):
            for t in range(2):
                if a == TILE_FIELDS - 1:
                    message[a, t] = jnp.full((ROWS, LANES), mask[h, t].astype(jnp.float32))
                else:
                    message[a, t] = tile_field(a, adjoint, viscosity, surface)[rows, t * LANES : (t + 1) * LANES]
            message[a, 2] = side_columns(lane, left, right, h * TILE_FIELDS + a)
        block = blocks - 1 if h else 0
        for k in range(n):

            @pl.when(lax.rem(me - k + n, n) == owner)
            def _():
                control = controls[k]
                for a in range(5):
                    for t in range(2):
                        if a == 0:
                            start = t * strip_rows + block * ROWS
                        else:
                            start = 2 * strip_rows + ((a - 1) * 2 + t) * ROWS
                        message[TILE_FIELDS + a, t] = control[pl.ds(start, ROWS), :]
                    part, slot = rim_slot(a, block, blocks)
                    packed = control[pl.ds(2 * strip_rows + 64 + part * ROWS, ROWS), :]
                    message[TILE_FIELDS + a, 2] = strip_columns(lane, packed, slot)


E_, N_, S_, U_, V_, K0_, K1_, I0_, I1_ = range(9)


def coefficients(coef, visc, fric, ice, lane):
    def step(i, carry):
        r = FIRST + i * ROWS
        rows, east, west = pl.ds(r, ROWS), pl.ds(r + 1, ROWS), pl.ds(r - 1, ROWS)
        cells = [ice[t, rows, :] for t in range(3)]
        layers = [[visc[l, t, rows, :] for t in range(3)] for l in range(LAYERS)]
        for l in range(LAYERS):
            centre = layers[l]
            north, south = after(centre, lane), before(centre, lane)
            for t in range(3):
                c = centre[t]
                e = 0.5 * (c + visc[l, t, east, :])
                w = 0.5 * (c + visc[l, t, west, :])
                nf = 0.5 * (c + north[t])
                sf = 0.5 * (c + south[t])
                coef[l, E_, t, rows, :] = e
                coef[l, N_, t, rows, :] = nf
                coef[l, S_, t, rows, :] = sf
                vertical = None
                if l < LAYERS - 1:
                    u = (0.5 * VERTICAL) * (c + layers[l + 1][t])
                    coef[l, U_, t, rows, :] = u
                    vertical = u
                if l > 0:
                    lower = (0.5 * VERTICAL) * (c + layers[l - 1][t])
                    vertical = lower if vertical is None else vertical + lower
                if l == 0:
                    vertical = vertical + fric[t, rows, :]
                coef[l, V_, t, rows, :] = (0.25 * COUPLING) * c
                rest = COUPLING * c + (1.0 - cells[t])
                ew, ns = e + w, nf + sf
                for c_, ax, ay in ((0, 4.0, 1.0), (1, 1.0, 4.0)):
                    own = (ax * ew if ax != 1.0 else ew) + (ay * ns if ay != 1.0 else ns) + vertical
                    inverse = DAMPING * cells[t] / (own + rest)
                    coef[l, I0_ + c_, t, rows, :] = inverse
                    coef[l, K0_ + c_, t, rows, :] = cells[t] - own * inverse
        return carry

    lax.fori_loop(0, STEPS, step, 0)


def sweep_layer(coef, old, new, l, lane, force=None):
    def step(i, carry):
        r = FIRST + i * ROWS
        rows, east, west = pl.ds(r, ROWS), pl.ds(r + 1, ROWS), pl.ds(r - 1, ROWS)
        e = [coef[l, E_, t, rows, :] for t in range(3)]
        w = [coef[l, E_, t, west, :] for t in range(3)]
        fluxes, mixes = [], []
        for c in range(2):
            m = [old[c * LAYERS + l, t, rows, :] for t in range(3)]
            me = [old[c * LAYERS + l, t, east, :] for t in range(3)]
            mw = [old[c * LAYERS + l, t, west, :] for t in range(3)]
            mn, ms = after(m, lane), before(m, lane)
            across = [me[t] - mw[t] for t in range(3)]
            an, as_ = after(across, lane), before(across, lane)
            mixes.append([an[t] - as_[t] for t in range(3)])
            flux = []
            for t in range(3):
                x = e[t] * me[t] + w[t] * mw[t]
                y = coef[l, N_, t, rows, :] * mn[t] + coef[l, S_, t, rows, :] * ms[t]
                total = 4.0 * x + y if c == 0 else x + 4.0 * y
                if l < LAYERS - 1:
                    total = total + coef[l, U_, t, rows, :] * old[c * LAYERS + l + 1, t, rows, :]
                if l > 0:
                    total = total + coef[l - 1, U_, t, rows, :] * old[c * LAYERS + l - 1, t, rows, :]
                if force is not None:
                    total = total + force[c, t, rows, :]
                flux.append((total, m[t]))
            fluxes.append(flux)
        for c in range(2):
            for t in range(3):
                total, m = fluxes[c][t]
                total = total + coef[l, V_, t, rows, :] * mixes[1 - c][t]
                new[c * LAYERS + l, t, rows, :] = (
                    coef[l, K0_ + c, t, rows, :] * m + coef[l, I0_ + c, t, rows, :] * total
                )
        return carry

    lax.fori_loop(0, STEPS, step, 0)


def sweeps_kernel(n, strip_rows, mask, adjoint, viscosity, surface, base, from_left, from_right, above, below, *rest):
    controls, datas = rest[:n], rest[n : 2 * n]
    grads, out = rest[2 * n : 3 * n], rest[3 * n]
    state, other, visc, surf, ice, logf, fric, given, bed, coef, force, grad, packed, sems = rest[3 * n + 1 :]
    me, mx = lax.axis_index("gy"), lax.axis_index("gx")
    size_x = lax.axis_size("gx")
    lane = lane_index()
    blocks = strip_rows // ROWS
    main = pl.ds(ROWS, TILE)
    copies = []

    def start(source, target):
        copy = pltpu.make_async_copy(source, target, sems.at[len(copies)])
        copy.start()
        copies.append(copy)

    for t in range(2):
        columns = pl.ds(t * LANES, LANES)
        start(adjoint.at[:, :, columns], state.at[:, t, main, :])
        start(viscosity.at[:, :, columns], visc.at[:, t, main, :])
        start(surface.at[:, :, columns], surf.at[:, t, main, :])
        start(base.at[:, :, columns], bed.at[:, t])
    for message, row in ((above, 0), (below, ROWS + TILE)):
        rows = pl.ds(row, ROWS)
        start(message.at[0:8], state.at[:, :, rows, :])
        start(message.at[8:12], visc.at[:, :, rows, :])
        start(message.at[12:14], surf.at[:, :, rows, :])
        start(message.at[14], ice.at[:, rows, :])
        start(message.at[15], logf.at[:, rows, :])
        start(message.at[16:20], given.at[:, :, rows, :])
    for k in range(n):
        source = lax.rem(me - k + n, n)
        rows = pl.ds(pl.multiple_of(ROWS + source * strip_rows, ROWS), strip_rows)
        start(controls[k].at[0:strip_rows], logf.at[0, rows, :])
        start(controls[k].at[strip_rows : 2 * strip_rows], logf.at[1, rows, :])
        start(controls[k].at[2 * strip_rows + 64 :], packed.at[k])
        start(datas[k], given.at[:, 0:2, rows, :])
    for copy in copies:
        copy.wait()

    for h in range(2):
        for t in range(2):
            ice[t, pl.ds(ROWS + h * HALF, HALF), :] = jnp.full((HALF, LANES), mask[h, t].astype(jnp.float32))

    def sides(r, carry):
        rows = pl.ds(pl.multiple_of(r * ROWS, ROWS), ROWS)
        left, right = from_left[rows, :], from_right[rows, :]
        for h in range(2):
            to = pl.ds(pl.multiple_of(ROWS + h * HALF + r * ROWS, ROWS), ROWS)
            for a in range(TILE_FIELDS):
                value = side_columns(lane, left, right, h * TILE_FIELDS + a)
                if a < 8:
                    state[a, 2, to, :] = value
                elif a < 12:
                    visc[a - 8, 2, to, :] = value
                elif a < 14:
                    surf[a - 12, 2, to, :] = value
                else:
                    ice[2, to, :] = value
        return carry

    lax.fori_loop(0, HALF // ROWS, sides, 0)
    for k in range(n):
        source = lax.rem(me - k + n, n)
        for a in range(5):
            for b in range(blocks):
                part, slot = rim_slot(a, b, blocks)
                value = strip_columns(lane, packed[k, pl.ds(part * ROWS, ROWS), :], slot)
                to = pl.ds(pl.multiple_of(ROWS + source * strip_rows + b * ROWS, ROWS), ROWS)
                if a == 0:
                    logf[2, to, :] = value
                else:
                    given[a - 1, 2, to, :] = value

    def fields(i, carry):
        rows = pl.ds(pl.multiple_of(i * ROWS, ROWS), ROWS)
        for t in range(3):
            fric[t, rows, :] = jnp.exp(logf[t, rows, :])
            for c in range(2):
                force[c, t, rows, :] = given[2 + c, t, rows, :] * (given[c, t, rows, :] - surf[c, t, rows, :])
        return carry

    lax.fori_loop(0, FRAME // ROWS, fields, 0)
    coefficients(coef, visc, fric, ice, lane)
    old, new = state, other
    for _ in range(SWEEPS):
        for l in range(LAYERS):
            sweep_layer(coef, old, new, l, lane, force if l == LAYERS - 1 else None)
        old, new = new, old
    outs = []
    for t in range(2):
        copy = pltpu.make_async_copy(old.at[:, t, main, :], out.at[:, :, pl.ds(t * LANES, LANES)], sems.at[t])
        copy.start()
        outs.append(copy)

    def finish(i, carry):
        r = pl.multiple_of(i * ROWS, ROWS)
        rows, east, west = pl.ds(r + ROWS, ROWS), pl.ds(r + ROWS + 1, ROWS), pl.ds(r + ROWS - 1, ROWS)
        centre = [logf[t, rows, :] for t in range(3)]
        north, south = after(centre, lane), before(centre, lane)
        row = lax.broadcasted_iota(jnp.int32, (ROWS, LANES), 0) + r
        in_west = jnp.logical_or(row != 0, mx != 0)
        in_east = jnp.logical_or(row != TILE - 1, mx != size_x - 1)
        in_south = jnp.logical_or(lane != 0, me != 0)
        in_north = jnp.logical_or(lane != LANES - 1, me != n - 1)
        for t in range(2):
            c = centre[t]
            smooth = jnp.where(in_west, c - logf[t, west, :], 0.0) + jnp.where(in_east, c - logf[t, east, :], 0.0)
            below_ = c - south[t]
            above_ = c - north[t]
            smooth = smooth + (jnp.where(in_south, below_, 0.0) if t == 0 else below_)
            smooth = smooth + (jnp.where(in_north, above_, 0.0) if t == 1 else above_)
            inner = pl.ds(r, ROWS)
            basal = fric[t, rows, :] * (
                bed[0, t, inner, :] * old[0, t, rows, :] + bed[1, t, inner, :] * old[LAYERS, t, rows, :]
            )
            grad[t, inner, :] = basal + TIKHONOV * smooth
        return carry

    lax.fori_loop(0, BLOCKS, finish, 0)
    for k in range(n):
        to = lax.rem(me + k, n)
        rows = pl.ds(pl.multiple_of(to * strip_rows, ROWS), strip_rows)
        copy = pltpu.make_async_copy(grad.at[:, rows, :], grads[k], sems.at[2 + k])
        copy.start()
        outs.append(copy)
    for copy in outs:
        copy.wait()


def unpack_gradient(n, *refs):
    parts, out = refs[:n], refs[n]
    me = lax.axis_index("gy")
    for k in range(n):
        source = lax.rem(me - k + n, n)
        for t in range(2):
            out[:, pl.ds(pl.multiple_of(source * TILE + t * LANES, LANES), LANES)] = parts[k][t]


def f32(*shape):
    return jax.ShapeDtypeStruct(shape, jnp.float32)


def per_device(
    adjoint_start,
    viscosity,
    base_velocity,
    surface_velocity,
    ice_mask,
    log_friction,
    observed_velocity,
    obs_weight,
):
    n = lax.axis_size("gy")
    size_x = lax.axis_size("gx")
    strip_rows = log_friction.shape[0]
    vmem = pl.BlockSpec(memory_space=pltpu.VMEM)
    smem = pl.BlockSpec(memory_space=pltpu.SMEM)
    anywhere = pl.BlockSpec(memory_space=pl.ANY)
    params = pltpu.CompilerParams(vmem_limit_bytes=VMEM_BYTES)
    adjoint = adjoint_start.reshape((2 * LAYERS, TILE, TILE))

    def ring(k):
        return [(i, (i + k) % n) for i in range(n)]

    def line(size, k):
        return [(i, i + k) for i in range(size) if 0 <= i + k < size]

    packed = pl.pallas_call(
        functools.partial(pack_strips, n, strip_rows),
        out_shape=[f32(control_rows(strip_rows), LANES)] * n + [f32(4, 2, strip_rows, LANES)] * n,
        in_specs=[vmem] * 3,
        out_specs=[vmem] * (2 * n),
        compiler_params=params,
    )(log_friction, observed_velocity, obs_weight)
    controls, datas = packed[:n], packed[n:]
    controls = [controls[0]] + [lax.ppermute(controls[k], "gy", ring(k)) for k in range(1, n)]
    datas = [datas[0]] + [lax.ppermute(datas[k], "gy", ring(k)) for k in range(1, n)]

    columns_up, columns_down = pl.pallas_call(
        pack_columns,
        out_shape=[f32(HALF, LANES)] * 2,
        in_specs=[smem, vmem, vmem, vmem],
        out_specs=[vmem] * 2,
        compiler_params=params,
    )(ice_mask, adjoint, viscosity, surface_velocity)
    from_left = lax.ppermute(columns_up, "gy", line(n, 1))
    from_right = lax.ppermute(columns_down, "gy", line(n, -1))

    rows_up, rows_down = pl.pallas_call(
        functools.partial(pack_rows, n, strip_rows),
        out_shape=[f32(RIM_FIELDS, 3, ROWS, LANES)] * 2,
        in_specs=[smem] + [vmem] * (5 + n),
        out_specs=[vmem] * 2,
        compiler_params=params,
    )(ice_mask, adjoint, viscosity, surface_velocity, from_left, from_right, *controls)
    above = lax.ppermute(rows_up, "gx", line(size_x, 1))
    below = lax.ppermute(rows_down, "gx", line(size_x, -1))

    def frames(*leading):
        return pltpu.VMEM(leading + (3, FRAME, LANES), jnp.float32)

    *grads, out = pl.pallas_call(
        functools.partial(sweeps_kernel, n, strip_rows),
        out_shape=[f32(2, strip_rows, LANES)] * n + [f32(2 * LAYERS, TILE, TILE)],
        in_specs=[smem] + [anywhere] * 4 + [vmem] * 2 + [anywhere] * (2 + 2 * n),
        out_specs=[anywhere] * (n + 1),
        scratch_shapes=[
            frames(8),
            frames(8),
            frames(4),
            frames(2),
            frames(),
            frames(),
            frames(),
            frames(4),
            pltpu.VMEM((2, 2, TILE, LANES), jnp.float32),
            frames(LAYERS, 9),
            frames(2),
            pltpu.VMEM((2, TILE, LANES), jnp.float32),
            pltpu.VMEM((n, ROWS * rim_tiles(strip_rows), LANES), jnp.float32),
            pltpu.SemaphoreType.DMA((20 + 4 * n,)),
        ],
        compiler_params=params,
    )(
        ice_mask,
        adjoint,
        viscosity,
        surface_velocity,
        base_velocity,
        from_left,
        from_right,
        above,
        below,
        *controls,
        *datas,
    )
    parts = [grads[0]] + [lax.ppermute(grads[k], "gy", ring(k)) for k in range(1, n)]
    gradient = pl.pallas_call(
        functools.partial(unpack_gradient, n),
        out_shape=f32(strip_rows, n * TILE),
        in_specs=[vmem] * n,
        out_specs=vmem,
        compiler_params=params,
    )(*parts)
    return gradient, out.reshape(adjoint_start.shape)


def solution(mesh):
    placed = (
        P(None, None, "gx", "gy"),
        P(None, "gx", "gy"),
        P(None, "gx", "gy"),
        P(None, "gx", "gy"),
        P("gx", "gy"),
        P(("gx", "gy"), None),
        P(None, ("gx", "gy"), None),
        P(None, ("gx", "gy"), None),
    )
    return jax.shard_map(
        per_device,
        mesh=mesh,
        in_specs=placed,
        out_specs=(P(("gx", "gy"), None), P(None, None, "gx", "gy")),
        check_vma=False,
    )
```

profile of v0, /device:TPU:1, one launch (start us, length us, event | category | flops | bytes accessed | tf_op | source)
XLA Modules:
  0.0 123.8 jit_solution(3981512491862543143)
XLA Ops:
  0.6 2.8 %shard_map.96 = (f32[216,128]{1,0:T(8,128)}, f32[216,128]{1,0:T(8,128)}, f32[216,128]{1,0:T(8,128)}, f32[216,128]{1,0:T(8,128)}, f32[4,2,64,128]{3,2,1,0:T(8,128...) custom-call(f32[64,1024]{1,0:T(8,128)} %logf.1, f32[2,64,1024]{2,1,0:T(8,128)} %obs.1, ...), custom_call_target="tpu_custom_call" | custom-call | tf_op jit(solution)/shard_map/pallas_call | solution.py:429
  3.4 0.0 copy-start.13
  3.4 2.2 %collective-permute-start.2 = (f32[216,128]{1,0:T(8,128)}, f32[216,128]{1,0:T(8,128)S(1)}, u32[]{:S(2)}, u32[]{:S(2)}) collective-permute-start(f32[216,128]{1,0:T(8,128)} %get-tuple-element.22), channel_id=1, source_target_pairs={{0,1},{1,2},{2,3},{3,0},{4,5},{5,6},{6,7},{7,4},{8,9},{9,10},{10,1... | collective-permute-start | bytes 331784 | tf_op jit(solution)/shard_map/ppermute | solution.py:437
  5.6 2.3 %collective-permute-start.3 = (f32[216,128]{1,0:T(8,128)}, f32[216,128]{1,0:T(8,128)S(1)}, u32[]{:S(2)}, u32[]{:S(2)}) collective-permute-start(f32[216,128]{1,0:T(8,128)} %get-tuple-element.23), channel_id=1, source_target_pairs={{0,2},{1,3},{2,0},{3,1},{4,6},{5,7},{6,4},{7,5},{8,10},{9,11},{10,... | collective-permute-start | bytes 331784 | tf_op jit(solution)/shard_map/ppermute | solution.py:437
  7.9 1.1 collective-permute-start.4
  9.0 4.7 %shard_map.95 = (f32[128,128]{1,0:T(8,128)}, f32[128,128]{1,0:T(8,128)}) custom-call(s32[2,2]{1,0:T(2,128)} %mask.5, f32[8,256,256]{2,1,0:T(8,128)} %bitcast.2, f32[4,256,256]{2,1,0:T(8,128)} %viscosity.5, f32[2,256,256]{2,1,0:T(8,128)} %surface.5), custom_call_target="tpu_custom_call" | custom-call | tf_op jit(solution)/shard_map/pallas_call | solution.py:440
  13.7 2.3 %collective-permute-start = (f32[128,128]{1,0:T(8,128)}, f32[128,128]{1,0:T(8,128)S(1)}, u32[]{:S(2)}, u32[]{:S(2)}) collective-permute-start(f32[128,128]{1,0:T(8,128)} %get-tuple-element.19), channel_id=1, source_target_pairs={{0,1},{1,2},{2,3},{4,5},{5,6},{6,7},{8,9},{9,10},{10,11},{12,13},{... | collective-permute-start | bytes 196616 | tf_op jit(solution)/shard_map/ppermute | solution.py:447
  15.9 1.3 %collective-permute-start.1 = (f32[128,128]{1,0:T(8,128)}, f32[128,128]{1,0:T(8,128)S(1)}, u32[]{:S(2)}, u32[]{:S(2)}) collective-permute-start(f32[128,128]{1,0:T(8,128)} %get-tuple-element.20), channel_id=1, source_target_pairs={{1,0},{2,1},{3,2},{5,4},{6,5},{7,6},{9,8},{10,9},{11,10},{13,12},{... | collective-permute-start | bytes 196616 | tf_op jit(solution)/shard_map/ppermute | solution.py:448
  17.2 0.3 collective-permute-done.from_left
  17.6 0.0 copy-done.15
  17.6 1.8 %collective-permute-start.7 = (f32[4,2,64,128]{3,2,1,0:T(8,128)S(1)}, f32[4,2,64,128]{3,2,1,0:T(8,128)S(1)}, u32[]{:S(2)}, u32[]{:S(2)}) collective-permute-start(f32[4,2,64,128]{3,2,1,0:T(8,128)S(1)} %copy-done.15), channel_id=1, source_target_pairs={{0,1},{1,2},{2,3},{3,0},{4,5},{5,6},{6,7},{7,4},{8,9},{9,10},{10,1... | collective-permute-start | bytes 786440 | tf_op jit(solution)/shard_map/ppermute | solution.py:438
  19.4 1.8 %collective-permute-done.1.from_right = f32[128,128]{1,0:T(8,128)S(1)} collective-permute-done((f32[128,128]{1,0:T(8,128)}, f32[128,128]{1,0:T(8,128)S(1)}, u32[]{:S(2)}, u32[]{:S(2)}) %collective-permute-start.1) | collective-permute-done | bytes 65568 | tf_op jit(solution)/shard_map/ppermute | solution.py:448
  21.2 0.0 copy-done.14
  21.2 0.1 collective-permute-start.8
  21.2 0.0 collective-permute-done.2.rest_1_
  21.2 0.0 copy-done.13
  21.2 2.4 %collective-permute-start.9 = (f32[4,2,64,128]{3,2,1,0:T(8,128)S(1)}, f32[4,2,64,128]{3,2,1,0:T(8,128)S(1)}, u32[]{:S(2)}, u32[]{:S(2)}) collective-permute-start(f32[4,2,64,128]{3,2,1,0:T(8,128)S(1)} %copy-done.13), channel_id=1, source_target_pairs={{0,3},{1,0},{2,1},{3,2},{4,7},{5,4},{6,5},{7,6},{8,11},{9,8},{10,9... | collective-permute-start | bytes 786440 | tf_op jit(solution)/shard_map/ppermute | solution.py:438
  23.7 0.0 collective-permute-done.3.rest_2_
  23.7 0.0 collective-permute-done.4.rest_3_
  23.7 0.0 copy-start.2
  23.7 0.0 copy-done.3
  23.7 0.0 copy-done.4
  23.7 0.0 copy-done
  23.7 0.6 copy-done.1
  24.3 0.1 copy-done.2
  24.4 3.2 %shard_map.97 = (f32[20,3,8,128]{3,2,1,0:T(8,128)}, f32[20,3,8,128]{3,2,1,0:T(8,128)}) custom-call(s32[2,2]{1,0:T(2,128)} %mask.5, f32[8,256,256]{2,1,0:T(8,128)} %bitcast.3, f32[4,256,256]{2,1,0:T(8,128)} %viscosity.5, f32[2,256,256]{2,1,0:T(8,128)} %surface.5, f32[128,128]{1,0:T(8,128)} %copy-done.3, f32[128,128]{1,0:T(8,128)} %copy-done.4, ...), custom_call_target="tpu_custom_call" | custom-call | tf_op jit(solution)/shard_map/pallas_call | solution.py:450
  27.6 6.9 %collective-permute-start.5 = (f32[20,3,8,128]{3,2,1,0:T(8,128)}, f32[20,3,8,128]{3,2,1,0:T(8,128)S(1)}, u32[]{:S(2)}, u32[]{:S(2)}) collective-permute-start(f32[20,3,8,128]{3,2,1,0:T(8,128)} %get-tuple-element.25), channel_id=1, source_target_pairs={{0,4},{4,8},{8,12},{12,16},{16,20},{20,24},{24,28},{1,5},{5,9},{9,... | collective-permute-start | bytes 737288 | tf_op jit(solution)/shard_map/ppermute | solution.py:457
  34.5 1.9 %collective-permute-start.6 = (f32[20,3,8,128]{3,2,1,0:T(8,128)}, f32[20,3,8,128]{3,2,1,0:T(8,128)S(1)}, u32[]{:S(2)}, u32[]{:S(2)}) collective-permute-start(f32[20,3,8,128]{3,2,1,0:T(8,128)} %get-tuple-element.26), channel_id=1, source_target_pairs={{4,0},{8,4},{12,8},{16,12},{20,16},{24,20},{28,24},{5,1},{9,5},{13... | collective-permute-start | bytes 737288 | tf_op jit(solution)/shard_map/ppermute | solution.py:458
  36.4 0.0 collective-permute-done.7.rest_5_
  36.4 0.0 copy-start.5
  36.4 3.3 %collective-permute-done.8.rest_6_ = f32[4,2,64,128]{3,2,1,0:T(8,128)S(1)} collective-permute-done((f32[4,2,64,128]{3,2,1,0:T(8,128)S(1)}, f32[4,2,64,128]{3,2,1,0:T(8,128)S(1)}, u32[]{:S(2)}, u32[]{:S(2)}) %collective-permute-start.8) | collective-permute-done | bytes 262176 | tf_op jit(solution)/shard_map/ppermute | solution.py:438
  39.7 0.0 collective-permute-done.9.rest_7_
  39.7 0.0 collective-permute-done.5.above
  39.7 0.0 copy-start.8
  39.7 2.4 %collective-permute-done.6.below = f32[20,3,8,128]{3,2,1,0:T(8,128)S(1)} collective-permute-done((f32[20,3,8,128]{3,2,1,0:T(8,128)}, f32[20,3,8,128]{3,2,1,0:T(8,128)S(1)}, u32[]{:S(2)}, u32[]{:S(2)}) %collective-permute-start.6) | collective-permute-done | bytes 245792 | tf_op jit(solution)/shard_map/ppermute | solution.py:458
  42.2 0.0 copy-done.5
  42.2 0.0 copy-done.8
  42.2 0.7 copy-done.9
  42.9 68.6 %shard_map.98 = (f32[2,64,128]{2,1,0:T(8,128)}, f32[2,64,128]{2,1,0:T(8,128)}, f32[2,64,128]{2,1,0:T(8,128)}, f32[2,64,128]{2,1,0:T(8,128)}, f32[8,256,256]{2,1,0:T(8,128)}) custom-call(s32[2,2]{1,0:T(2,128)} %mask.5, f32[8,256,256]{2,1,0:T(8,128)} %bitcast.4, f32[4,256,256]{2,1,0:T(8,128)} %viscosity.5, f32[2,256,256]{2,1,0:T(8,128)} %surface.5, ...), custom_call_target="tpu_custom_call" | custom-call | tf_op jit(solution)/shard_map/pallas_call | solution.py:463
  111.5 3.7 %collective-permute-start.10 = (f32[2,64,128]{2,1,0:T(8,128)}, f32[2,64,128]{2,1,0:T(8,128)S(1)}, u32[]{:S(2)}, u32[]{:S(2)}) collective-permute-start(f32[2,64,128]{2,1,0:T(8,128)} %get-tuple-element.32), channel_id=1, source_target_pairs={{0,1},{1,2},{2,3},{3,0},{4,5},{5,6},{6,7},{7,4},{8,9},{9,10},{10,1... | collective-permute-start | bytes 196616 | tf_op jit(solution)/shard_map/ppermute | solution.py:498
  115.2 0.6 collective-permute-start.11
  115.8 1.6 %collective-permute-start.12 = (f32[2,64,128]{2,1,0:T(8,128)}, f32[2,64,128]{2,1,0:T(8,128)S(1)}, u32[]{:S(2)}, u32[]{:S(2)}) collective-permute-start(f32[2,64,128]{2,1,0:T(8,128)} %get-tuple-element.34), channel_id=1, source_target_pairs={{0,3},{1,0},{2,1},{3,2},{4,7},{5,4},{6,5},{7,6},{8,11},{9,8},{10,9... | collective-permute-start | bytes 196616 | tf_op jit(solution)/shard_map/ppermute | solution.py:498
  117.4 0.7 collective-permute-done.10.refs_1_
  118.1 3.4 %collective-permute-done.11.refs_2_ = f32[2,64,128]{2,1,0:T(8,128)S(1)} collective-permute-done((f32[2,64,128]{2,1,0:T(8,128)}, f32[2,64,128]{2,1,0:T(8,128)S(1)}, u32[]{:S(2)}, u32[]{:S(2)}) %collective-permute-start.11) | collective-permute-done | bytes 65568 | tf_op jit(solution)/shard_map/ppermute | solution.py:498
  121.5 0.0 collective-permute-done.12.refs_3_
  121.5 0.6 copy-done.11
  122.1 0.0 copy-done.12
  122.1 1.7 %shard_map.99 = f32[64,1024]{1,0:T(8,128)} custom-call(f32[2,64,128]{2,1,0:T(8,128)} %get-tuple-element.31.refs_0_, f32[2,64,128]{2,1,0:T(8,128)} %copy-done.10, f32[2,64,128]{2,1,0:T(8,128)} %copy-done.11, f32[2,64,128]{2,1,0:T(8,128)} %copy-done.12), custom_call_target="tpu_custom_call" | custom-call | tf_op jit(solution)/shard_map/pallas_call | solution.py:499
  (15 shorter events, 0.0 us)
Async XLA Ops:
  3.4 14.2 %copy-start.15 = (f32[4,2,64,128]{3,2,1,0:T(8,128)S(1)}, f32[4,2,64,128]{3,2,1,0:T(8,128)}, u32[]{:S(2)}) copy-start(f32[4,2,64,128]{3,2,1,0:T(8,128)} %get-tuple-element.28) | copy-start | bytes 786436
  3.4 17.8 %copy-start.14 = (f32[4,2,64,128]{3,2,1,0:T(8,128)S(1)}, f32[4,2,64,128]{3,2,1,0:T(8,128)}, u32[]{:S(2)}) copy-start(f32[4,2,64,128]{3,2,1,0:T(8,128)} %get-tuple-element.29) | copy-start | bytes 786436
  3.4 17.9 %copy-start.13 = (f32[4,2,64,128]{3,2,1,0:T(8,128)S(1)}, f32[4,2,64,128]{3,2,1,0:T(8,128)}, u32[]{:S(2)}) copy-start(f32[4,2,64,128]{3,2,1,0:T(8,128)} %get-tuple-element.30) | copy-start | bytes 786436
  3.4 17.8 %collective-permute-start.2 = (f32[216,128]{1,0:T(8,128)}, f32[216,128]{1,0:T(8,128)S(1)}, u32[]{:S(2)}, u32[]{:S(2)}) collective-permute-start(f32[216,128]{1,0:T(8,128)} %get-tuple-element.22), channel_id=1, source_target_pairs={{0,1},{1,2},{2,3},{3,0},{4,5},{5,6},{6,7},{7,4},{8,9},{9,10},{10,1... | collective-permute-start | bytes 331784 | tf_op jit(solution)/shard_map/ppermute | solution.py:437
  5.6 18.1 %collective-permute-start.3 = (f32[216,128]{1,0:T(8,128)}, f32[216,128]{1,0:T(8,128)S(1)}, u32[]{:S(2)}, u32[]{:S(2)}) collective-permute-start(f32[216,128]{1,0:T(8,128)} %get-tuple-element.23), channel_id=1, source_target_pairs={{0,2},{1,3},{2,0},{3,1},{4,6},{5,7},{6,4},{7,5},{8,10},{9,11},{10,... | collective-permute-start | bytes 331784 | tf_op jit(solution)/shard_map/ppermute | solution.py:437
  7.9 15.8 %collective-permute-start.4 = (f32[216,128]{1,0:T(8,128)}, f32[216,128]{1,0:T(8,128)S(1)}, u32[]{:S(2)}, u32[]{:S(2)}) collective-permute-start(f32[216,128]{1,0:T(8,128)} %get-tuple-element.24), channel_id=1, source_target_pairs={{0,3},{1,0},{2,1},{3,2},{4,7},{5,4},{6,5},{7,6},{8,11},{9,8},{10,9... | collective-permute-start | bytes 331784 | tf_op jit(solution)/shard_map/ppermute | solution.py:437
  13.7 3.9 %collective-permute-start = (f32[128,128]{1,0:T(8,128)}, f32[128,128]{1,0:T(8,128)S(1)}, u32[]{:S(2)}, u32[]{:S(2)}) collective-permute-start(f32[128,128]{1,0:T(8,128)} %get-tuple-element.19), channel_id=1, source_target_pairs={{0,1},{1,2},{2,3},{4,5},{5,6},{6,7},{8,9},{9,10},{10,11},{12,13},{... | collective-permute-start | bytes 196616 | tf_op jit(solution)/shard_map/ppermute | solution.py:447
  15.9 5.2 %collective-permute-start.1 = (f32[128,128]{1,0:T(8,128)}, f32[128,128]{1,0:T(8,128)S(1)}, u32[]{:S(2)}, u32[]{:S(2)}) collective-permute-start(f32[128,128]{1,0:T(8,128)} %get-tuple-element.20), channel_id=1, source_target_pairs={{1,0},{2,1},{3,2},{5,4},{6,5},{7,6},{9,8},{10,9},{11,10},{13,12},{... | collective-permute-start | bytes 196616 | tf_op jit(solution)/shard_map/ppermute | solution.py:448
  17.6 6.1 %copy-start.3 = (f32[128,128]{1,0:T(8,128)}, f32[128,128]{1,0:T(8,128)S(1)}, u32[]{:S(2)}) copy-start(f32[128,128]{1,0:T(8,128)S(1)} %collective-permute-done.from_left) | copy-start | bytes 196612
  17.6 18.8 %collective-permute-start.7 = (f32[4,2,64,128]{3,2,1,0:T(8,128)S(1)}, f32[4,2,64,128]{3,2,1,0:T(8,128)S(1)}, u32[]{:S(2)}, u32[]{:S(2)}) collective-permute-start(f32[4,2,64,128]{3,2,1,0:T(8,128)S(1)} %copy-done.15), channel_id=1, source_target_pairs={{0,1},{1,2},{2,3},{3,0},{4,5},{5,6},{6,7},{7,4},{8,9},{9,10},{10,1... | collective-permute-start | bytes 786440 | tf_op jit(solution)/shard_map/ppermute | solution.py:438
  21.2 2.5 %copy-start.4 = (f32[128,128]{1,0:T(8,128)}, f32[128,128]{1,0:T(8,128)S(1)}, u32[]{:S(2)}) copy-start(f32[128,128]{1,0:T(8,128)S(1)} %collective-permute-done.1.from_right) | copy-start | bytes 196612
  21.2 18.5 %collective-permute-start.8 = (f32[4,2,64,128]{3,2,1,0:T(8,128)S(1)}, f32[4,2,64,128]{3,2,1,0:T(8,128)S(1)}, u32[]{:S(2)}, u32[]{:S(2)}) collective-permute-start(f32[4,2,64,128]{3,2,1,0:T(8,128)S(1)} %copy-done.14), channel_id=1, source_target_pairs={{0,2},{1,3},{2,0},{3,1},{4,6},{5,7},{6,4},{7,5},{8,10},{9,11},{10,... | collective-permute-start | bytes 786440 | tf_op jit(solution)/shard_map/ppermute | solution.py:438
  21.2 2.5 %copy-start = (f32[216,128]{1,0:T(8,128)}, f32[216,128]{1,0:T(8,128)S(1)}, u32[]{:S(2)}) copy-start(f32[216,128]{1,0:T(8,128)S(1)} %collective-permute-done.2.rest_1_) | copy-start | bytes 331780
  21.2 18.5 %collective-permute-start.9 = (f32[4,2,64,128]{3,2,1,0:T(8,128)S(1)}, f32[4,2,64,128]{3,2,1,0:T(8,128)S(1)}, u32[]{:S(2)}, u32[]{:S(2)}) collective-permute-start(f32[4,2,64,128]{3,2,1,0:T(8,128)S(1)} %copy-done.13), channel_id=1, source_target_pairs={{0,3},{1,0},{2,1},{3,2},{4,7},{5,4},{6,5},{7,6},{8,11},{9,8},{10,9... | collective-permute-start | bytes 786440 | tf_op jit(solution)/shard_map/ppermute | solution.py:438
  23.7 0.6 copy-start.1
  23.7 0.7 copy-start.2
  27.6 12.1 %collective-permute-start.5 = (f32[20,3,8,128]{3,2,1,0:T(8,128)}, f32[20,3,8,128]{3,2,1,0:T(8,128)S(1)}, u32[]{:S(2)}, u32[]{:S(2)}) collective-permute-start(f32[20,3,8,128]{3,2,1,0:T(8,128)} %get-tuple-element.25), channel_id=1, source_target_pairs={{0,4},{4,8},{8,12},{12,16},{16,20},{20,24},{24,28},{1,5},{5,9},{9,... | collective-permute-start | bytes 737288 | tf_op jit(solution)/shard_map/ppermute | solution.py:457
  34.5 7.7 %collective-permute-start.6 = (f32[20,3,8,128]{3,2,1,0:T(8,128)}, f32[20,3,8,128]{3,2,1,0:T(8,128)S(1)}, u32[]{:S(2)}, u32[]{:S(2)}) collective-permute-start(f32[20,3,8,128]{3,2,1,0:T(8,128)} %get-tuple-element.26), channel_id=1, source_target_pairs={{4,0},{8,4},{12,8},{16,12},{20,16},{24,20},{28,24},{5,1},{9,5},{13... | collective-permute-start | bytes 737288 | tf_op jit(solution)/shard_map/ppermute | solution.py:458
  36.4 5.8 %copy-start.5 = (f32[4,2,64,128]{3,2,1,0:T(8,128)}, f32[4,2,64,128]{3,2,1,0:T(8,128)S(1)}, u32[]{:S(2)}) copy-start(f32[4,2,64,128]{3,2,1,0:T(8,128)S(1)} %collective-permute-done.7.rest_5_) | copy-start | bytes 786436
  39.7 2.5 %copy-start.6 = (f32[4,2,64,128]{3,2,1,0:T(8,128)}, f32[4,2,64,128]{3,2,1,0:T(8,128)S(1)}, u32[]{:S(2)}) copy-start(f32[4,2,64,128]{3,2,1,0:T(8,128)S(1)} %collective-permute-done.8.rest_6_) | copy-start | bytes 786436
  39.7 2.5 %copy-start.7 = (f32[4,2,64,128]{3,2,1,0:T(8,128)}, f32[4,2,64,128]{3,2,1,0:T(8,128)S(1)}, u32[]{:S(2)}) copy-start(f32[4,2,64,128]{3,2,1,0:T(8,128)S(1)} %collective-permute-done.9.rest_7_) | copy-start | bytes 786436
  39.7 2.5 %copy-start.8 = (f32[20,3,8,128]{3,2,1,0:T(8,128)}, f32[20,3,8,128]{3,2,1,0:T(8,128)S(1)}, u32[]{:S(2)}) copy-start(f32[20,3,8,128]{3,2,1,0:T(8,128)S(1)} %collective-permute-done.5.above) | copy-start | bytes 737284
  42.2 0.7 copy-start.9
  111.5 6.6 %collective-permute-start.10 = (f32[2,64,128]{2,1,0:T(8,128)}, f32[2,64,128]{2,1,0:T(8,128)S(1)}, u32[]{:S(2)}, u32[]{:S(2)}) collective-permute-start(f32[2,64,128]{2,1,0:T(8,128)} %get-tuple-element.32), channel_id=1, source_target_pairs={{0,1},{1,2},{2,3},{3,0},{4,5},{5,6},{6,7},{7,4},{8,9},{9,10},{10,1... | collective-permute-start | bytes 196616 | tf_op jit(solution)/shard_map/ppermute | solution.py:498
  115.2 6.3 %collective-permute-start.11 = (f32[2,64,128]{2,1,0:T(8,128)}, f32[2,64,128]{2,1,0:T(8,128)S(1)}, u32[]{:S(2)}, u32[]{:S(2)}) collective-permute-start(f32[2,64,128]{2,1,0:T(8,128)} %get-tuple-element.33), channel_id=1, source_target_pairs={{0,2},{1,3},{2,0},{3,1},{4,6},{5,7},{6,4},{7,5},{8,10},{9,11},{10,... | collective-permute-start | bytes 196616 | tf_op jit(solution)/shard_map/ppermute | solution.py:498
  115.8 5.7 %collective-permute-start.12 = (f32[2,64,128]{2,1,0:T(8,128)}, f32[2,64,128]{2,1,0:T(8,128)S(1)}, u32[]{:S(2)}, u32[]{:S(2)}) collective-permute-start(f32[2,64,128]{2,1,0:T(8,128)} %get-tuple-element.34), channel_id=1, source_target_pairs={{0,3},{1,0},{2,1},{3,2},{4,7},{5,4},{6,5},{7,6},{8,11},{9,8},{10,9... | collective-permute-start | bytes 196616 | tf_op jit(solution)/shard_map/ppermute | solution.py:498
  118.1 3.4 %copy-start.10 = (f32[2,64,128]{2,1,0:T(8,128)}, f32[2,64,128]{2,1,0:T(8,128)S(1)}, u32[]{:S(2)}) copy-start(f32[2,64,128]{2,1,0:T(8,128)S(1)} %collective-permute-done.10.refs_1_) | copy-start | bytes 196612
  121.5 0.6 copy-start.11
  121.5 0.6 copy-start.12
where the time goes:
time: 125 us; the launch traced here: 124 us
  Pallas kernels  81 us (65%)
  starting transfers between devices  28.1 us (22%)
  waiting for transfers between devices  12 us (10%)
  local copies, waits for them, and re-layouts  2.01 us (2%)
    pallas_call x1, Pallas kernels, per_device(): pl.pallas_call(functools.partial(sweeps_kernel, n, strip_rows), out_shape...  68.6 us
    ppermute x1, starting transfers between devices, per_device(): above = lax.ppermute(rows_up, 'gx', line(size_x, 1))  6.86 us
    ppermute x3, starting transfers between devices, per_device(): lax.ppermute(grads[k], 'gy', ring(k))  5.87 us
    ppermute x3, starting transfers between devices, per_device(): lax.ppermute(controls[k], 'gy', ring(k))  5.56 us
    pallas_call x1, Pallas kernels, per_device(): pl.pallas_call(pack_columns, out_shape=[f32(HALF, LANES)] * 2, in_specs=[...  4.69 us
    ppermute x3, starting transfers between devices, per_device(): lax.ppermute(datas[k], 'gy', ring(k))  4.32 us
    ppermute x3, waiting for transfers between devices, per_device(): lax.ppermute(grads[k], 'gy', ring(k))  4.1 us
    ppermute x3, waiting for transfers between devices, per_device(): lax.ppermute(datas[k], 'gy', ring(k))  3.32 us
  transfers between devices with their start and end apart: 13, of which 6 were waited for; matrix products, arithmetic and copies ran while one was open for 0% of the time, Pallas kernels for 6%

commit v1 on v0

--- a/solution.py
+++ b/solution.py
@@ -126,7 +126,7 @@
         down[rows, :] = to_down
         return carry
 
-    lax.fori_loop(0, HALF // ROWS, step, 0)
+    lax.fori_loop(0, HALF // ROWS, step, 0, unroll=4)
 
 
 def side_columns(lane, from_left, from_right, slot):
@@ -215,7 +215,7 @@
                     coef[l, K0_ + c_, t, rows, :] = cells[t] - own * inverse
         return carry
 
-    lax.fori_loop(0, STEPS, step, 0)
+    lax.fori_loop(0, STEPS, step, 0, unroll=STEPS)
 
 
 def sweep_layer(coef, old, new, l, lane, force=None):
@@ -255,7 +255,7 @@
                 )
         return carry
 
-    lax.fori_loop(0, STEPS, step, 0)
+    lax.fori_loop(0, STEPS, step, 0, unroll=STEPS)
 
 
 def sweeps_kernel(n, strip_rows, mask, adjoint, viscosity, surface, base, from_left, from_right, above, below, *rest):
@@ -319,7 +319,7 @@
                     ice[2, to, :] = value
         return carry
 
-    lax.fori_loop(0, HALF // ROWS, sides, 0)
+    lax.fori_loop(0, HALF // ROWS, sides, 0, unroll=4)
     for k in range(n):
         source = lax.rem(me - k + n, n)
         for a in range(5):
@@ -340,7 +340,7 @@
                 force[c, t, rows, :] = given[2 + c, t, rows, :] * (given[c, t, rows, :] - surf[c, t, rows, :])
         return carry
 
-    lax.fori_loop(0, FRAME // ROWS, fields, 0)
+    lax.fori_loop(0, FRAME // ROWS, fields, 0, unroll=True)
     coefficients(coef, visc, fric, ice, lane)
     old, new = state, other
     for _ in range(SWEEPS):
@@ -377,7 +377,7 @@
             grad[t, inner, :] = basal + TIKHONOV * smooth
         return carry
 
-    lax.fori_loop(0, BLOCKS, finish, 0)
+    lax.fori_loop(0, BLOCKS, finish, 0, unroll=8)
     for k in range(n):
         to = lax.rem(me + k, n)
         rows = pl.ds(pl.multiple_of(to * strip_rows, ROWS), strip_rows)

time: 125 us -> 78.1 us (0.62)
  Pallas kernels: 81 us -> 33.9 us
    pallas_call x1, Pallas kernels: 68.6 us -> 22.4 us  [per_device(): pl.pallas_call(functools.partial(sweeps_kernel, n, strip_rows), out_shape...]
  transfers between devices with their start and end apart: 13 -> 13, of which waited for: 6 -> 6; matrix products, arithmetic and copies ran while one was open for 0% -> 0% of each run, Pallas kernels for 6% -> 9%
where the time goes in v1:
time: 78.1 us; the launch traced here: 76.8 us
  Pallas kernels  33.9 us (43%)
  starting transfers between devices  28.2 us (36%)
  waiting for transfers between devices  11.8 us (15%)
  local copies, waits for them, and re-layouts  2.01 us (3%)
    pallas_call x1, Pallas kernels, per_device(): pl.pallas_call(functools.partial(sweeps_kernel, n, strip_rows), out_shape...  22.4 us
    ppermute x1, starting transfers between devices, per_device(): above = lax.ppermute(rows_up, 'gx', line(size_x, 1))  6.86 us
    ppermute x3, starting transfers between devices, per_device(): lax.ppermute(grads[k], 'gy', ring(k))  5.87 us
    ppermute x3, starting transfers between devices, per_device(): lax.ppermute(controls[k], 'gy', ring(k))  5.56 us
    ppermute x3, starting transfers between devices, per_device(): lax.ppermute(datas[k], 'gy', ring(k))  4.46 us
    ppermute x3, waiting for transfers between devices, per_device(): lax.ppermute(grads[k], 'gy', ring(k))  4.1 us
    pallas_call x1, Pallas kernels, per_device(): pl.pallas_call(pack_columns, out_shape=[f32(HALF, LANES)] * 2, in_specs=[...  3.85 us
    ppermute x3, waiting for transfers between devices, per_device(): lax.ppermute(datas[k], 'gy', ring(k))  3.32 us
  transfers between devices with their start and end apart: 13, of which 6 were waited for; matrix products, arithmetic and copies ran while one was open for 0% of the time, Pallas kernels for 9%

profile of v1, /device:TPU:1, one launch (start us, length us, event | category | flops | bytes accessed | tf_op | source)
XLA Modules:
  0.0 76.8 jit_solution(11835506888643706334)
XLA Ops:
  0.6 2.8 %shard_map.96 = (f32[216,128]{1,0:T(8,128)}, f32[216,128]{1,0:T(8,128)}, f32[216,128]{1,0:T(8,128)}, f32[216,128]{1,0:T(8,128)}, f32[4,2,64,128]{3,2,1,0:T(8,128...) custom-call(f32[64,1024]{1,0:T(8,128)} %logf.1, f32[2,64,1024]{2,1,0:T(8,128)} %obs.1, ...), custom_call_target="tpu_custom_call" | custom-call | tf_op jit(solution)/shard_map/pallas_call | solution.py:429
  3.4 0.0 copy-start.13
  3.4 2.2 %collective-permute-start.2 = (f32[216,128]{1,0:T(8,128)}, f32[216,128]{1,0:T(8,128)S(1)}, u32[]{:S(2)}, u32[]{:S(2)}) collective-permute-start(f32[216,128]{1,0:T(8,128)} %get-tuple-element.22), channel_id=1, source_target_pairs={{0,1},{1,2},{2,3},{3,0},{4,5},{5,6},{6,7},{7,4},{8,9},{9,10},{10,1... | collective-permute-start | bytes 331784 | tf_op jit(solution)/shard_map/ppermute | solution.py:437
  5.6 2.3 %collective-permute-start.3 = (f32[216,128]{1,0:T(8,128)}, f32[216,128]{1,0:T(8,128)S(1)}, u32[]{:S(2)}, u32[]{:S(2)}) collective-permute-start(f32[216,128]{1,0:T(8,128)} %get-tuple-element.23), channel_id=1, source_target_pairs={{0,2},{1,3},{2,0},{3,1},{4,6},{5,7},{6,4},{7,5},{8,10},{9,11},{10,... | collective-permute-start | bytes 331784 | tf_op jit(solution)/shard_map/ppermute | solution.py:437
  7.9 1.1 %collective-permute-start.4 = (f32[216,128]{1,0:T(8,128)}, f32[216,128]{1,0:T(8,128)S(1)}, u32[]{:S(2)}, u32[]{:S(2)}) collective-permute-start(f32[216,128]{1,0:T(8,128)} %get-tuple-element.24), channel_id=1, source_target_pairs={{0,3},{1,0},{2,1},{3,2},{4,7},{5,4},{6,5},{7,6},{8,11},{9,8},{10,9... | collective-permute-start | bytes 331784 | tf_op jit(solution)/shard_map/ppermute | solution.py:437
  9.0 3.8 %shard_map.95 = (f32[128,128]{1,0:T(8,128)}, f32[128,128]{1,0:T(8,128)}) custom-call(s32[2,2]{1,0:T(2,128)} %mask.5, f32[8,256,256]{2,1,0:T(8,128)} %bitcast.2, f32[4,256,256]{2,1,0:T(8,128)} %viscosity.5, f32[2,256,256]{2,1,0:T(8,128)} %surface.5), custom_call_target="tpu_custom_call" | custom-call | tf_op jit(solution)/shard_map/pallas_call | solution.py:440
  12.8 2.3 %collective-permute-start = (f32[128,128]{1,0:T(8,128)}, f32[128,128]{1,0:T(8,128)S(1)}, u32[]{:S(2)}, u32[]{:S(2)}) collective-permute-start(f32[128,128]{1,0:T(8,128)} %get-tuple-element.19), channel_id=1, source_target_pairs={{0,1},{1,2},{2,3},{4,5},{5,6},{6,7},{8,9},{9,10},{10,11},{12,13},{... | collective-permute-start | bytes 196616 | tf_op jit(solution)/shard_map/ppermute | solution.py:447
  15.1 1.3 %collective-permute-start.1 = (f32[128,128]{1,0:T(8,128)}, f32[128,128]{1,0:T(8,128)S(1)}, u32[]{:S(2)}, u32[]{:S(2)}) collective-permute-start(f32[128,128]{1,0:T(8,128)} %get-tuple-element.20), channel_id=1, source_target_pairs={{1,0},{2,1},{3,2},{5,4},{6,5},{7,6},{9,8},{10,9},{11,10},{13,12},{... | collective-permute-start | bytes 196616 | tf_op jit(solution)/shard_map/ppermute | solution.py:448
  16.4 0.3 collective-permute-done.from_left
  16.7 0.0 copy-done.15
  16.7 2.0 %collective-permute-start.7 = (f32[4,2,64,128]{3,2,1,0:T(8,128)S(1)}, f32[4,2,64,128]{3,2,1,0:T(8,128)S(1)}, u32[]{:S(2)}, u32[]{:S(2)}) collective-permute-start(f32[4,2,64,128]{3,2,1,0:T(8,128)S(1)} %copy-done.15), channel_id=1, source_target_pairs={{0,1},{1,2},{2,3},{3,0},{4,5},{5,6},{6,7},{7,4},{8,9},{9,10},{10,1... | collective-permute-start | bytes 786440 | tf_op jit(solution)/shard_map/ppermute | solution.py:438
  18.7 1.6 %collective-permute-done.1.from_right = f32[128,128]{1,0:T(8,128)S(1)} collective-permute-done((f32[128,128]{1,0:T(8,128)}, f32[128,128]{1,0:T(8,128)S(1)}, u32[]{:S(2)}, u32[]{:S(2)}) %collective-permute-start.1) | collective-permute-done | bytes 65568 | tf_op jit(solution)/shard_map/ppermute | solution.py:448
  20.3 0.0 copy-done.14
  20.3 0.1 collective-permute-start.8
  20.4 0.0 collective-permute-done.2.rest_1_
  20.4 0.0 copy-done.13
  20.4 2.4 %collective-permute-start.9 = (f32[4,2,64,128]{3,2,1,0:T(8,128)S(1)}, f32[4,2,64,128]{3,2,1,0:T(8,128)S(1)}, u32[]{:S(2)}, u32[]{:S(2)}) collective-permute-start(f32[4,2,64,128]{3,2,1,0:T(8,128)S(1)} %copy-done.13), channel_id=1, source_target_pairs={{0,3},{1,0},{2,1},{3,2},{4,7},{5,4},{6,5},{7,6},{8,11},{9,8},{10,9... | collective-permute-start | bytes 786440 | tf_op jit(solution)/shard_map/ppermute | solution.py:438
  22.8 0.0 collective-permute-done.3.rest_2_
  22.8 0.0 collective-permute-done.4.rest_3_
  22.8 0.0 copy-start.2
  22.8 0.0 copy-done.3
  22.9 0.0 copy-done.4
  22.9 0.0 copy-done
  22.9 0.6 copy-done.1
  23.5 0.1 copy-done.2
  23.5 3.2 %shard_map.97 = (f32[20,3,8,128]{3,2,1,0:T(8,128)}, f32[20,3,8,128]{3,2,1,0:T(8,128)}) custom-call(s32[2,2]{1,0:T(2,128)} %mask.5, f32[8,256,256]{2,1,0:T(8,128)} %bitcast.3, f32[4,256,256]{2,1,0:T(8,128)} %viscosity.5, f32[2,256,256]{2,1,0:T(8,128)} %surface.5, f32[128,128]{1,0:T(8,128)} %copy-done.3, f32[128,128]{1,0:T(8,128)} %copy-done.4, ...), custom_call_target="tpu_custom_call" | custom-call | tf_op jit(solution)/shard_map/pallas_call | solution.py:450
  26.7 6.9 %collective-permute-start.5 = (f32[20,3,8,128]{3,2,1,0:T(8,128)}, f32[20,3,8,128]{3,2,1,0:T(8,128)S(1)}, u32[]{:S(2)}, u32[]{:S(2)}) collective-permute-start(f32[20,3,8,128]{3,2,1,0:T(8,128)} %get-tuple-element.25), channel_id=1, source_target_pairs={{0,4},{4,8},{8,12},{12,16},{16,20},{20,24},{24,28},{1,5},{5,9},{9,... | collective-permute-start | bytes 737288 | tf_op jit(solution)/shard_map/ppermute | solution.py:457
  33.6 1.9 %collective-permute-start.6 = (f32[20,3,8,128]{3,2,1,0:T(8,128)}, f32[20,3,8,128]{3,2,1,0:T(8,128)S(1)}, u32[]{:S(2)}, u32[]{:S(2)}) collective-permute-start(f32[20,3,8,128]{3,2,1,0:T(8,128)} %get-tuple-element.26), channel_id=1, source_target_pairs={{4,0},{8,4},{12,8},{16,12},{20,16},{24,20},{28,24},{5,1},{9,5},{13... | collective-permute-start | bytes 737288 | tf_op jit(solution)/shard_map/ppermute | solution.py:458
  35.5 0.0 collective-permute-done.7.rest_5_
  35.5 0.0 copy-start.5
  35.6 3.3 %collective-permute-done.8.rest_6_ = f32[4,2,64,128]{3,2,1,0:T(8,128)S(1)} collective-permute-done((f32[4,2,64,128]{3,2,1,0:T(8,128)S(1)}, f32[4,2,64,128]{3,2,1,0:T(8,128)S(1)}, u32[]{:S(2)}, u32[]{:S(2)}) %collective-permute-start.8) | collective-permute-done | bytes 262176 | tf_op jit(solution)/shard_map/ppermute | solution.py:438
  38.9 0.0 collective-permute-done.9.rest_7_
  38.9 0.0 collective-permute-done.5.above
  38.9 0.0 copy-start.8
  38.9 2.4 %collective-permute-done.6.below = f32[20,3,8,128]{3,2,1,0:T(8,128)S(1)} collective-permute-done((f32[20,3,8,128]{3,2,1,0:T(8,128)}, f32[20,3,8,128]{3,2,1,0:T(8,128)S(1)}, u32[]{:S(2)}, u32[]{:S(2)}) %collective-permute-start.6) | collective-permute-done | bytes 245792 | tf_op jit(solution)/shard_map/ppermute | solution.py:458
  41.3 0.0 copy-done.5
  41.3 0.0 copy-done.6
  41.4 0.7 copy-done.9
  42.0 22.4 %shard_map.98 = (f32[2,64,128]{2,1,0:T(8,128)}, f32[2,64,128]{2,1,0:T(8,128)}, f32[2,64,128]{2,1,0:T(8,128)}, f32[2,64,128]{2,1,0:T(8,128)}, f32[8,256,256]{2,1,0:T(8,128)}) custom-call(s32[2,2]{1,0:T(2,128)} %mask.5, f32[8,256,256]{2,1,0:T(8,128)} %bitcast.4, f32[4,256,256]{2,1,0:T(8,128)} %viscosity.5, f32[2,256,256]{2,1,0:T(8,128)} %surface.5, ...), custom_call_target="tpu_custom_call" | custom-call | tf_op jit(solution)/shard_map/pallas_call | solution.py:463
  64.5 3.7 %collective-permute-start.10 = (f32[2,64,128]{2,1,0:T(8,128)}, f32[2,64,128]{2,1,0:T(8,128)S(1)}, u32[]{:S(2)}, u32[]{:S(2)}) collective-permute-start(f32[2,64,128]{2,1,0:T(8,128)} %get-tuple-element.32), channel_id=1, source_target_pairs={{0,1},{1,2},{2,3},{3,0},{4,5},{5,6},{6,7},{7,4},{8,9},{9,10},{10,1... | collective-permute-start | bytes 196616 | tf_op jit(solution)/shard_map/ppermute | solution.py:498
  68.2 0.5 collective-permute-start.11
  68.7 1.6 %collective-permute-start.12 = (f32[2,64,128]{2,1,0:T(8,128)}, f32[2,64,128]{2,1,0:T(8,128)S(1)}, u32[]{:S(2)}, u32[]{:S(2)}) collective-permute-start(f32[2,64,128]{2,1,0:T(8,128)} %get-tuple-element.34), channel_id=1, source_target_pairs={{0,3},{1,0},{2,1},{3,2},{4,7},{5,4},{6,5},{7,6},{8,11},{9,8},{10,9... | collective-permute-start | bytes 196616 | tf_op jit(solution)/shard_map/ppermute | solution.py:498
  70.4 0.3 collective-permute-done.10.refs_1_
  70.7 3.8 %collective-permute-done.11.refs_2_ = f32[2,64,128]{2,1,0:T(8,128)S(1)} collective-permute-done((f32[2,64,128]{2,1,0:T(8,128)}, f32[2,64,128]{2,1,0:T(8,128)S(1)}, u32[]{:S(2)}, u32[]{:S(2)}) %collective-permute-start.11) | collective-permute-done | bytes 65568 | tf_op jit(solution)/shard_map/ppermute | solution.py:498
  74.5 0.0 collective-permute-done.12.refs_3_
  74.5 0.6 copy-done.11
  75.1 0.0 copy-done.12
  75.1 1.7 %shard_map.99 = f32[64,1024]{1,0:T(8,128)} custom-call(f32[2,64,128]{2,1,0:T(8,128)} %get-tuple-element.31.refs_0_, f32[2,64,128]{2,1,0:T(8,128)} %copy-done.10, f32[2,64,128]{2,1,0:T(8,128)} %copy-done.11, f32[2,64,128]{2,1,0:T(8,128)} %copy-done.12), custom_call_target="tpu_custom_call" | custom-call | tf_op jit(solution)/shard_map/pallas_call | solution.py:499
  (15 shorter events, 0.0 us)
Async XLA Ops:
  3.4 13.4 %copy-start.15 = (f32[4,2,64,128]{3,2,1,0:T(8,128)S(1)}, f32[4,2,64,128]{3,2,1,0:T(8,128)}, u32[]{:S(2)}) copy-start(f32[4,2,64,128]{3,2,1,0:T(8,128)} %get-tuple-element.28) | copy-start | bytes 786436
  3.4 16.9 %copy-start.14 = (f32[4,2,64,128]{3,2,1,0:T(8,128)S(1)}, f32[4,2,64,128]{3,2,1,0:T(8,128)}, u32[]{:S(2)}) copy-start(f32[4,2,64,128]{3,2,1,0:T(8,128)} %get-tuple-element.29) | copy-start | bytes 786436
  3.4 17.0 %copy-start.13 = (f32[4,2,64,128]{3,2,1,0:T(8,128)S(1)}, f32[4,2,64,128]{3,2,1,0:T(8,128)}, u32[]{:S(2)}) copy-start(f32[4,2,64,128]{3,2,1,0:T(8,128)} %get-tuple-element.30) | copy-start | bytes 786436
  3.4 17.0 %collective-permute-start.2 = (f32[216,128]{1,0:T(8,128)}, f32[216,128]{1,0:T(8,128)S(1)}, u32[]{:S(2)}, u32[]{:S(2)}) collective-permute-start(f32[216,128]{1,0:T(8,128)} %get-tuple-element.22), channel_id=1, source_target_pairs={{0,1},{1,2},{2,3},{3,0},{4,5},{5,6},{6,7},{7,4},{8,9},{9,10},{10,1... | collective-permute-start | bytes 331784 | tf_op jit(solution)/shard_map/ppermute | solution.py:437
  5.6 17.2 %collective-permute-start.3 = (f32[216,128]{1,0:T(8,128)}, f32[216,128]{1,0:T(8,128)S(1)}, u32[]{:S(2)}, u32[]{:S(2)}) collective-permute-start(f32[216,128]{1,0:T(8,128)} %get-tuple-element.23), channel_id=1, source_target_pairs={{0,2},{1,3},{2,0},{3,1},{4,6},{5,7},{6,4},{7,5},{8,10},{9,11},{10,... | collective-permute-start | bytes 331784 | tf_op jit(solution)/shard_map/ppermute | solution.py:437
  7.9 14.9 %collective-permute-start.4 = (f32[216,128]{1,0:T(8,128)}, f32[216,128]{1,0:T(8,128)S(1)}, u32[]{:S(2)}, u32[]{:S(2)}) collective-permute-start(f32[216,128]{1,0:T(8,128)} %get-tuple-element.24), channel_id=1, source_target_pairs={{0,3},{1,0},{2,1},{3,2},{4,7},{5,4},{6,5},{7,6},{8,11},{9,8},{10,9... | collective-permute-start | bytes 331784 | tf_op jit(solution)/shard_map/ppermute | solution.py:437
  12.8 3.9 %collective-permute-start = (f32[128,128]{1,0:T(8,128)}, f32[128,128]{1,0:T(8,128)S(1)}, u32[]{:S(2)}, u32[]{:S(2)}) collective-permute-start(f32[128,128]{1,0:T(8,128)} %get-tuple-element.19), channel_id=1, source_target_pairs={{0,1},{1,2},{2,3},{4,5},{5,6},{6,7},{8,9},{9,10},{10,11},{12,13},{... | collective-permute-start | bytes 196616 | tf_op jit(solution)/shard_map/ppermute | solution.py:447
  15.1 5.2 %collective-permute-start.1 = (f32[128,128]{1,0:T(8,128)}, f32[128,128]{1,0:T(8,128)S(1)}, u32[]{:S(2)}, u32[]{:S(2)}) collective-permute-start(f32[128,128]{1,0:T(8,128)} %get-tuple-element.20), channel_id=1, source_target_pairs={{1,0},{2,1},{3,2},{5,4},{6,5},{7,6},{9,8},{10,9},{11,10},{13,12},{... | collective-permute-start | bytes 196616 | tf_op jit(solution)/shard_map/ppermute | solution.py:448
  16.7 6.1 %copy-start.3 = (f32[128,128]{1,0:T(8,128)}, f32[128,128]{1,0:T(8,128)S(1)}, u32[]{:S(2)}) copy-start(f32[128,128]{1,0:T(8,128)S(1)} %collective-permute-done.from_left) | copy-start | bytes 196612
  16.7 18.8 %collective-permute-start.7 = (f32[4,2,64,128]{3,2,1,0:T(8,128)S(1)}, f32[4,2,64,128]{3,2,1,0:T(8,128)S(1)}, u32[]{:S(2)}, u32[]{:S(2)}) collective-permute-start(f32[4,2,64,128]{3,2,1,0:T(8,128)S(1)} %copy-done.15), channel_id=1, source_target_pairs={{0,1},{1,2},{2,3},{3,0},{4,5},{5,6},{6,7},{7,4},{8,9},{9,10},{10,1... | collective-permute-start | bytes 786440 | tf_op jit(solution)/shard_map/ppermute | solution.py:438
  20.3 2.5 %copy-start.4 = (f32[128,128]{1,0:T(8,128)}, f32[128,128]{1,0:T(8,128)S(1)}, u32[]{:S(2)}) copy-start(f32[128,128]{1,0:T(8,128)S(1)} %collective-permute-done.1.from_right) | copy-start | bytes 196612
  20.3 18.5 %collective-permute-start.8 = (f32[4,2,64,128]{3,2,1,0:T(8,128)S(1)}, f32[4,2,64,128]{3,2,1,0:T(8,128)S(1)}, u32[]{:S(2)}, u32[]{:S(2)}) collective-permute-start(f32[4,2,64,128]{3,2,1,0:T(8,128)S(1)} %copy-done.14), channel_id=1, source_target_pairs={{0,2},{1,3},{2,0},{3,1},{4,6},{5,7},{6,4},{7,5},{8,10},{9,11},{10,... | collective-permute-start | bytes 786440 | tf_op jit(solution)/shard_map/ppermute | solution.py:438
  20.4 2.5 %copy-start = (f32[216,128]{1,0:T(8,128)}, f32[216,128]{1,0:T(8,128)S(1)}, u32[]{:S(2)}) copy-start(f32[216,128]{1,0:T(8,128)S(1)} %collective-permute-done.2.rest_1_) | copy-start | bytes 331780
  20.4 18.5 %collective-permute-start.9 = (f32[4,2,64,128]{3,2,1,0:T(8,128)S(1)}, f32[4,2,64,128]{3,2,1,0:T(8,128)S(1)}, u32[]{:S(2)}, u32[]{:S(2)}) collective-permute-start(f32[4,2,64,128]{3,2,1,0:T(8,128)S(1)} %copy-done.13), channel_id=1, source_target_pairs={{0,3},{1,0},{2,1},{3,2},{4,7},{5,4},{6,5},{7,6},{8,11},{9,8},{10,9... | collective-permute-start | bytes 786440 | tf_op jit(solution)/shard_map/ppermute | solution.py:438
  22.8 0.6 copy-start.1
  22.8 0.7 copy-start.2
  26.7 12.1 %collective-permute-start.5 = (f32[20,3,8,128]{3,2,1,0:T(8,128)}, f32[20,3,8,128]{3,2,1,0:T(8,128)S(1)}, u32[]{:S(2)}, u32[]{:S(2)}) collective-permute-start(f32[20,3,8,128]{3,2,1,0:T(8,128)} %get-tuple-element.25), channel_id=1, source_target_pairs={{0,4},{4,8},{8,12},{12,16},{16,20},{20,24},{24,28},{1,5},{5,9},{9,... | collective-permute-start | bytes 737288 | tf_op jit(solution)/shard_map/ppermute | solution.py:457
  33.6 7.7 %collective-permute-start.6 = (f32[20,3,8,128]{3,2,1,0:T(8,128)}, f32[20,3,8,128]{3,2,1,0:T(8,128)S(1)}, u32[]{:S(2)}, u32[]{:S(2)}) collective-permute-start(f32[20,3,8,128]{3,2,1,0:T(8,128)} %get-tuple-element.26), channel_id=1, source_target_pairs={{4,0},{8,4},{12,8},{16,12},{20,16},{24,20},{28,24},{5,1},{9,5},{13... | collective-permute-start | bytes 737288 | tf_op jit(solution)/shard_map/ppermute | solution.py:458
  35.5 5.8 %copy-start.5 = (f32[4,2,64,128]{3,2,1,0:T(8,128)}, f32[4,2,64,128]{3,2,1,0:T(8,128)S(1)}, u32[]{:S(2)}) copy-start(f32[4,2,64,128]{3,2,1,0:T(8,128)S(1)} %collective-permute-done.7.rest_5_) | copy-start | bytes 786436
  38.9 2.5 %copy-start.6 = (f32[4,2,64,128]{3,2,1,0:T(8,128)}, f32[4,2,64,128]{3,2,1,0:T(8,128)S(1)}, u32[]{:S(2)}) copy-start(f32[4,2,64,128]{3,2,1,0:T(8,128)S(1)} %collective-permute-done.8.rest_6_) | copy-start | bytes 786436
  38.9 2.5 %copy-start.7 = (f32[4,2,64,128]{3,2,1,0:T(8,128)}, f32[4,2,64,128]{3,2,1,0:T(8,128)S(1)}, u32[]{:S(2)}) copy-start(f32[4,2,64,128]{3,2,1,0:T(8,128)S(1)} %collective-permute-done.9.rest_7_) | copy-start | bytes 786436
  38.9 2.5 %copy-start.8 = (f32[20,3,8,128]{3,2,1,0:T(8,128)}, f32[20,3,8,128]{3,2,1,0:T(8,128)S(1)}, u32[]{:S(2)}) copy-start(f32[20,3,8,128]{3,2,1,0:T(8,128)S(1)} %collective-permute-done.5.above) | copy-start | bytes 737284
  41.3 0.7 copy-start.9
  64.5 6.2 %collective-permute-start.10 = (f32[2,64,128]{2,1,0:T(8,128)}, f32[2,64,128]{2,1,0:T(8,128)S(1)}, u32[]{:S(2)}, u32[]{:S(2)}) collective-permute-start(f32[2,64,128]{2,1,0:T(8,128)} %get-tuple-element.32), channel_id=1, source_target_pairs={{0,1},{1,2},{2,3},{3,0},{4,5},{5,6},{6,7},{7,4},{8,9},{9,10},{10,1... | collective-permute-start | bytes 196616 | tf_op jit(solution)/shard_map/ppermute | solution.py:498
  68.2 6.3 %collective-permute-start.11 = (f32[2,64,128]{2,1,0:T(8,128)}, f32[2,64,128]{2,1,0:T(8,128)S(1)}, u32[]{:S(2)}, u32[]{:S(2)}) collective-permute-start(f32[2,64,128]{2,1,0:T(8,128)} %get-tuple-element.33), channel_id=1, source_target_pairs={{0,2},{1,3},{2,0},{3,1},{4,6},{5,7},{6,4},{7,5},{8,10},{9,11},{10,... | collective-permute-start | bytes 196616 | tf_op jit(solution)/shard_map/ppermute | solution.py:498
  68.7 5.7 %collective-permute-start.12 = (f32[2,64,128]{2,1,0:T(8,128)}, f32[2,64,128]{2,1,0:T(8,128)S(1)}, u32[]{:S(2)}, u32[]{:S(2)}) collective-permute-start(f32[2,64,128]{2,1,0:T(8,128)} %get-tuple-element.34), channel_id=1, source_target_pairs={{0,3},{1,0},{2,1},{3,2},{4,7},{5,4},{6,5},{7,6},{8,11},{9,8},{10,9... | collective-permute-start | bytes 196616 | tf_op jit(solution)/shard_map/ppermute | solution.py:498
  70.7 3.8 %copy-start.10 = (f32[2,64,128]{2,1,0:T(8,128)}, f32[2,64,128]{2,1,0:T(8,128)S(1)}, u32[]{:S(2)}) copy-start(f32[2,64,128]{2,1,0:T(8,128)S(1)} %collective-permute-done.10.refs_1_) | copy-start | bytes 196612
  74.5 0.6 copy-start.11
  74.5 0.6 copy-start.12

commit v2 on v1

v2 whole, which is shorter than its diff:
```python
import functools

import jax
import jax.numpy as jnp
from jax import lax
from jax.experimental import pallas as pl
from jax.experimental.pallas import tpu as pltpu
from jax.sharding import PartitionSpec as P

SWEEPS = 4
DAMPING = 0.8
VERTICAL = 2.0
COUPLING = 3.0
TIKHONOV = 0.25

LAYERS = 4
LANES = 128
ROWS = 8
TILE = 256
FRAME = TILE + 2 * ROWS
HALF = TILE // 2
BLOCKS = TILE // ROWS
FIRST = 4
STEPS = BLOCKS + 1
TILE_FIELDS = 15
RIM_FIELDS = 20
PAIRS = RIM_FIELDS // 2
EDGE_ROWS = 4 * ROWS
MIB = 1024 * 1024


def row_index():
    return lax.broadcasted_iota(jnp.int32, (ROWS, LANES), 0)


def lane_index():
    return lax.broadcasted_iota(jnp.int32, (ROWS, LANES), 1)


def roll_to(x, shift):
    shift = shift % LANES
    return x if shift == 0 else pltpu.roll(x, shift, 1)


def after(x, lane):
    a, b, c = (roll_to(v, -1) for v in x)
    last = lane == LANES - 1
    return jnp.where(last, b, a), jnp.where(last, c, b), jnp.where(last, a, c)


def before(x, lane):
    a, b, c = (roll_to(v, 1) for v in x)
    first = lane == 0
    return jnp.where(first, c, a), jnp.where(first, a, b), jnp.where(first, b, c)


def rim_slot(array, block, strip_blocks):
    position = array * strip_blocks + block
    return position // 16, position % 16


def rim_tiles(strip_rows):
    return -(-5 * (strip_rows // ROWS) // 16)


def control_rows(strip_rows):
    return 2 * strip_rows + EDGE_ROWS + ROWS * rim_tiles(strip_rows)


def pack_strips(n, strip_rows, logf, obs, weight, controls, datas):
    me = lax.axis_index("gy")
    lane = lane_index()
    blocks = strip_rows // ROWS
    edge = pl.multiple_of(jnp.where(me == 0, 0, strip_rows - ROWS), ROWS)
    own = (row_index() < 4) == (me == 0)
    strips = [logf.at[...], obs.at[0], obs.at[1], weight.at[0], weight.at[1]]
    width = n * TILE
    for k in range(n):
        to = lax.rem(me + k, n)
        column = pl.multiple_of(to * TILE, TILE)
        left = pl.multiple_of(jnp.maximum(column - LANES, 0), LANES)
        right = pl.multiple_of(jnp.minimum(column + TILE, width - LANES), LANES)
        control, data = controls[k], datas[k]
        for t in range(2):
            columns = pl.ds(column + t * LANES, LANES)
            control[pl.ds(t * strip_rows, strip_rows), :] = logf[:, columns]
            for a in range(4):
                data[a, t] = strips[a + 1][:, columns]
            for a in range(2):
                ends = [strips[a + i][pl.ds(edge, ROWS), columns] for i in (1, 3)]
                both = jnp.where(own, ends[0], pltpu.roll(ends[1], 4, 0))
                control[pl.ds(2 * strip_rows + (a * 2 + t) * ROWS, ROWS), :] = both
        packed = [jnp.zeros((ROWS, LANES), jnp.float32) for _ in range(rim_tiles(strip_rows))]
        for a in range(5):
            for b in range(blocks):
                part, slot = rim_slot(a, b, blocks)
                rows = pl.ds(b * ROWS, ROWS)
                both = jnp.where(lane < 64, strips[a][rows, pl.ds(right, LANES)], strips[a][rows, pl.ds(left, LANES)])
                packed[part] = jnp.where(lane // 8 == slot, roll_to(both, 8 * slot + 4), packed[part])
        for part, value in enumerate(packed):
            control[pl.ds(2 * strip_rows + EDGE_ROWS + part * ROWS, ROWS), :] = value


def tile_field(a, adjoint, viscosity, surface):
    if a < 8:
        return adjoint.at[a]
    if a < 12:
        return viscosity.at[a - 8]
    return surface.at[a - 12]


def pack_columns(mask, adjoint, viscosity, surface, up, down, first):
    lane = lane_index()

    def step(r, carry):
        to_up = jnp.zeros((ROWS, LANES), jnp.float32)
        to_down = jnp.zeros((ROWS, LANES), jnp.float32)
        for h in range(2):
            rows = pl.ds(pl.multiple_of(h * HALF + r * ROWS, ROWS), ROWS)
            for a in range(TILE_FIELDS):
                slot = h * TILE_FIELDS + a
                here = lane // 4 == slot
                if a == TILE_FIELDS - 1:
                    low = mask[h, 0].astype(jnp.float32)
                    high = mask[h, 1].astype(jnp.float32)
                    to_up = jnp.where(here, high, to_up)
                    to_down = jnp.where(here, low, to_down)
                else:
                    field = tile_field(a, adjoint, viscosity, surface)
                    to_up = jnp.where(here, roll_to(field[rows, LANES:], 4 * slot + 4), to_up)
                    to_down = jnp.where(here, roll_to(field[rows, :LANES], 4 * slot), to_down)
        rows = pl.ds(pl.multiple_of(first + r * ROWS, ROWS), ROWS)
        up[rows, :] = to_up
        down[rows, :] = to_down
        return carry

    lax.fori_loop(0, HALF // ROWS, step, 0, unroll=4)


def start_copies(sems, pairs):
    copies = [pltpu.make_async_copy(source, target, sems.at[i]) for i, (source, target) in enumerate(pairs)]
    for copy in copies:
        copy.start()
    return copies


def pack_kernel(n, strip_rows, mask, logf, obs, weight, adjoint, viscosity, surface, *rest):
    controls, datas = rest[:n], rest[n : 2 * n]
    logf_in, obs_in, weight_in, adjoint_in, viscosity_in, surface_in, sems = rest[2 * n :]
    copies = start_copies(
        sems,
        [
            (logf, logf_in),
            (obs, obs_in),
            (weight, weight_in),
            (adjoint, adjoint_in),
            (viscosity, viscosity_in),
            (surface, surface_in),
        ],
    )
    for copy in copies[:3]:
        copy.wait()
    pack_strips(n, strip_rows, logf_in, obs_in, weight_in, controls, datas)
    for copy in copies[3:]:
        copy.wait()
    pack_columns(
        mask, adjoint_in, viscosity_in, surface_in, controls[1], controls[n - 1], control_rows(strip_rows)
    )


def side_columns(lane, from_left, from_right, slot):
    left = roll_to(from_left, -(4 * slot + 4))
    right = roll_to(from_right, -4 * slot)
    return jnp.where(lane < 4, right, jnp.where(lane >= LANES - 4, left, 0.0))


def strip_columns(lane, packed, slot):
    value = roll_to(packed, -(8 * slot + 4))
    return jnp.where(jnp.logical_or(lane < 4, lane >= LANES - 4), value, 0.0)


def sides_at(n, strip_rows, controls, row):
    me = lax.axis_index("gy")
    rows = pl.ds(pl.multiple_of(control_rows(strip_rows) + row, ROWS), ROWS)
    left = jnp.where(me > 0, controls[1][rows, :], 0.0)
    right = jnp.where(me < n - 1, controls[n - 1][rows, :], 0.0)
    return left, right


def pack_rows(n, strip_rows, mask, adjoint, viscosity, surface, *rest):
    controls, (up, down, adjoint_in, viscosity_in, surface_in, rim, sems) = rest[:n], rest[n:]
    me = lax.axis_index("gy")
    lane, sub = lane_index(), row_index()
    blocks = strip_rows // ROWS
    copies = []
    for h, row in ((0, 0), (1, TILE - ROWS)):
        rows = pl.ds(row, ROWS)
        copies += [
            (adjoint.at[:, rows, :], adjoint_in.at[h]),
            (viscosity.at[:, rows, :], viscosity_in.at[h]),
            (surface.at[:, rows, :], surface_in.at[h]),
        ]
    copies = start_copies(sems, copies)
    for h, owner in ((1, n - 1), (0, 0)):
        block = blocks - 1 if h else 0
        for k in range(n):

            @pl.when(lax.rem(me - k + n, n) == owner)
            def _():
                control = controls[k]
                for a in range(5):
                    for t in range(2):
                        if a == 0:
                            rim[h, a, t] = control[pl.ds(t * strip_rows + block * ROWS, ROWS), :]
                            continue
                        both = control[pl.ds(2 * strip_rows + ((a - 1) % 2 * 2 + t) * ROWS, ROWS), :]
                        rim[h, a, t] = both if a < 3 else pltpu.roll(both, 4, 0)
                    part, slot = rim_slot(a, block, blocks)
                    packed = control[pl.ds(2 * strip_rows + EDGE_ROWS + part * ROWS, ROWS), :]
                    rim[h, a, 2] = strip_columns(lane, packed, slot)

    for copy in copies:
        copy.wait()
    for message, h in ((up, 1), (down, 0)):
        left, right = sides_at(n, strip_rows, controls, h * (HALF - ROWS))

        def field(a, t):
            if a >= TILE_FIELDS:
                return rim[h, a - TILE_FIELDS, t]
            if t == 2:
                return side_columns(lane, left, right, h * TILE_FIELDS + a)
            if a == TILE_FIELDS - 1:
                return jnp.full((ROWS, LANES), mask[h, t].astype(jnp.float32))
            return tile_field(a, adjoint_in.at[h], viscosity_in.at[h], surface_in.at[h])[:, t * LANES : (t + 1) * LANES]

        own = sub >= 4 if h else sub < 4
        for a in range(PAIRS):
            for t in range(3):
                message[a, t] = jnp.where(own, field(a, t), pltpu.roll(field(a + PAIRS, t), 4, 0))


def rim_rows(message, a, t):
    if a < PAIRS:
        return message[a, t]
    return pltpu.roll(message[a - PAIRS, t], 4, 0)


E_, N_, S_, U_, V_, K0_, K1_, I0_, I1_ = range(9)


def coefficients(coef, visc, ice, lane, fric=None):
    def step(i, carry):
        r = FIRST + i * ROWS
        rows, east, west = pl.ds(r, ROWS), pl.ds(r + 1, ROWS), pl.ds(r - 1, ROWS)
        cells = [ice[t, rows, :] for t in range(3)]
        layers = [[visc[l, t, rows, :] for t in range(3)] for l in range(LAYERS)]
        for l in range(LAYERS):
            centre = layers[l]
            if l == 0 and fric is None:
                for t in range(3):
                    coef[l, U_, t, rows, :] = (0.5 * VERTICAL) * (centre[t] + layers[l + 1][t])
                continue
            north, south = after(centre, lane), before(centre, lane)
            for t in range(3):
                c = centre[t]
                e = 0.5 * (c + visc[l, t, east, :])
                w = 0.5 * (c + visc[l, t, west, :])
                nf = 0.5 * (c + north[t])
                sf = 0.5 * (c + south[t])
                coef[l, E_, t, rows, :] = e
                coef[l, N_, t, rows, :] = nf
                coef[l, S_, t, rows, :] = sf
                vertical = None
                if l < LAYERS - 1:
                    u = (0.5 * VERTICAL) * (c + layers[l + 1][t])
                    coef[l, U_, t, rows, :] = u
                    vertical = u
                if l > 0:
                    lower = (0.5 * VERTICAL) * (c + layers[l - 1][t])
                    vertical = lower if vertical is None else vertical + lower
                if l == 0:
                    vertical = vertical + fric[t, rows, :]
                coef[l, V_, t, rows, :] = (0.25 * COUPLING) * c
                rest = COUPLING * c + (1.0 - cells[t])
                ew, ns = e + w, nf + sf
                for c_, ax, ay in ((0, 4.0, 1.0), (1, 1.0, 4.0)):
                    own = (ax * ew if ax != 1.0 else ew) + (ay * ns if ay != 1.0 else ns) + vertical
                    inverse = DAMPING * cells[t] / (own + rest)
                    coef[l, I0_ + c_, t, rows, :] = inverse
                    coef[l, K0_ + c_, t, rows, :] = cells[t] - own * inverse
        return carry

    lax.fori_loop(0, STEPS, step, 0, unroll=STEPS)


def sweep_layer(coef, old, new, l, lane, force=None, last=False):
    first, steps, tiles = (ROWS, BLOCKS, 2) if last else (FIRST, STEPS, 3)

    def step(i, carry):
        r = first + i * ROWS
        rows, east, west = pl.ds(r, ROWS), pl.ds(r + 1, ROWS), pl.ds(r - 1, ROWS)
        e = [coef[l, E_, t, rows, :] for t in range(tiles)]
        w = [coef[l, E_, t, west, :] for t in range(tiles)]
        fluxes, mixes = [], []
        for c in range(2):
            m = [old[c * LAYERS + l, t, rows, :] for t in range(3)]
            me = [old[c * LAYERS + l, t, east, :] for t in range(3)]
            mw = [old[c * LAYERS + l, t, west, :] for t in range(3)]
            mn, ms = after(m, lane), before(m, lane)
            across = [me[t] - mw[t] for t in range(3)]
            an, as_ = after(across, lane), before(across, lane)
            mixes.append([an[t] - as_[t] for t in range(tiles)])
            flux = []
            for t in range(tiles):
                x = e[t] * me[t] + w[t] * mw[t]
                y = coef[l, N_, t, rows, :] * mn[t] + coef[l, S_, t, rows, :] * ms[t]
                total = 4.0 * x + y if c == 0 else x + 4.0 * y
                if l < LAYERS - 1:
                    total = total + coef[l, U_, t, rows, :] * old[c * LAYERS + l + 1, t, rows, :]
                if l > 0:
                    total = total + coef[l - 1, U_, t, rows, :] * old[c * LAYERS + l - 1, t, rows, :]
                if force is not None:
                    total = total + force[c, t, rows, :]
                flux.append((total, m[t]))
            fluxes.append(flux)
        for c in range(2):
            for t in range(tiles):
                total, m = fluxes[c][t]
                total = total + coef[l, V_, t, rows, :] * mixes[1 - c][t]
                new[c * LAYERS + l, t, rows, :] = (
                    coef[l, K0_ + c, t, rows, :] * m + coef[l, I0_ + c, t, rows, :] * total
                )
        return carry

    lax.fori_loop(0, steps, step, 0, unroll=steps)


def before_forcing(n, strip_rows, mask, adjoint, viscosity, base, above, below, *rest):
    controls = rest[:n]
    terms, first, second, third, fourth, visc_out, ice_out = rest[n : n + 7]
    s0, s1, s2, s3, s4, visc, ice, logf, fric, bed, coef, terms_in, reach, packed, sems = rest[n + 7 :]
    me, mx = lax.axis_index("gy"), lax.axis_index("gx")
    size_x = lax.axis_size("gx")
    lane = lane_index()
    blocks = strip_rows // ROWS
    main = pl.ds(ROWS, TILE)
    pairs = []
    for t in range(2):
        columns = pl.ds(t * LANES, LANES)
        pairs += [
            (adjoint.at[:, :, columns], s0.at[:, t, main, :]),
            (viscosity.at[:, :, columns], visc.at[:, t, main, :]),
            (base.at[:, :, columns], bed.at[:, t]),
        ]
    for k in range(n):
        source = lax.rem(me - k + n, n)
        rows = pl.ds(pl.multiple_of(ROWS + source * strip_rows, ROWS), strip_rows)
        tail = pl.ds(2 * strip_rows + EDGE_ROWS, ROWS * rim_tiles(strip_rows))
        pairs += [
            (controls[k].at[0:strip_rows], logf.at[0, rows, :]),
            (controls[k].at[strip_rows : 2 * strip_rows], logf.at[1, rows, :]),
            (controls[k].at[tail], packed.at[k]),
        ]
    copies = start_copies(sems, pairs)

    for h in range(2):
        for t in range(2):
            ice[t, pl.ds(ROWS + h * HALF, HALF), :] = jnp.full((HALF, LANES), mask[h, t].astype(jnp.float32))
    for message, row in ((above, 0), (below, ROWS + TILE)):
        rows = pl.ds(row, ROWS)
        for t in range(3):
            for a in range(8):
                s0[a, t, rows, :] = rim_rows(message, a, t)
            for a in range(4):
                visc[a, t, rows, :] = rim_rows(message, 8 + a, t)
            ice[t, rows, :] = rim_rows(message, 14, t)
            logf[t, rows, :] = rim_rows(message, 15, t)

    def sides(r, carry):
        left, right = sides_at(n, strip_rows, controls, r * ROWS)
        for h in range(2):
            to = pl.ds(pl.multiple_of(ROWS + h * HALF + r * ROWS, ROWS), ROWS)
            for a in range(TILE_FIELDS):
                slot = h * TILE_FIELDS + a
                if a < 8:
                    s0[a, 2, to, :] = side_columns(lane, left, right, slot)
                elif a < 12:
                    visc[a - 8, 2, to, :] = side_columns(lane, left, right, slot)
                elif a == 14:
                    ice[2, to, :] = side_columns(lane, left, right, slot)
        return carry

    lax.fori_loop(0, HALF // ROWS, sides, 0, unroll=4)
    for copy in copies:
        copy.wait()
    for k in range(n):
        source = lax.rem(me - k + n, n)
        for b in range(blocks):
            part, slot = rim_slot(0, b, blocks)
            to = pl.ds(pl.multiple_of(ROWS + source * strip_rows + b * ROWS, ROWS), ROWS)
            logf[2, to, :] = strip_columns(lane, packed[k, pl.ds(part * ROWS, ROWS), :], slot)
    for i in range(FRAME // ROWS):
        rows = pl.ds(i * ROWS, ROWS)
        for t in range(3):
            fric[t, rows, :] = jnp.exp(logf[t, rows, :])
    coefficients(coef, visc, ice, lane, fric)

    outs = [(visc, visc_out), (ice, ice_out)]
    for l in range(LAYERS):
        sweep_layer(coef, s0, s1, l, lane)
    outs += [(s1.at[pl.ds(c * LAYERS + 2, 2)], first.at[c]) for c in range(2)]
    for l in range(3):
        sweep_layer(coef, s1, s2, l, lane)
    outs += [(s2.at[pl.ds(c * LAYERS + 1, 2)], second.at[c]) for c in range(2)]
    for l in range(2):
        sweep_layer(coef, s2, s3, l, lane)
    outs += [(s3.at[pl.ds(c * LAYERS, 2)], third.at[c]) for c in range(2)]
    copies = start_copies(sems, outs)
    sweep_layer(coef, s3, s4, 0, lane, last=True)

    def finish(i, carry):
        r = pl.multiple_of(i * ROWS, ROWS)
        rows, east, west = pl.ds(r + ROWS, ROWS), pl.ds(r + ROWS + 1, ROWS), pl.ds(r + ROWS - 1, ROWS)
        centre = [logf[t, rows, :] for t in range(3)]
        north, south = after(centre, lane), before(centre, lane)
        row = row_index() + r
        in_west = jnp.logical_or(row != 0, mx != 0)
        in_east = jnp.logical_or(row != TILE - 1, mx != size_x - 1)
        in_south = jnp.logical_or(lane != 0, me != 0)
        in_north = jnp.logical_or(lane != LANES - 1, me != n - 1)
        inner = pl.ds(r, ROWS)
        for t in range(2):
            c = centre[t]
            smooth = jnp.where(in_west, c - logf[t, west, :], 0.0) + jnp.where(in_east, c - logf[t, east, :], 0.0)
            left, right = c - south[t], c - north[t]
            smooth = smooth + (jnp.where(in_south, left, 0.0) if t == 0 else left)
            smooth = smooth + (jnp.where(in_north, right, 0.0) if t == 1 else right)
            total = TIKHONOV * smooth
            for component in range(2):
                along = coef[LAYERS - 1, I0_ + component, t, rows, :]
                for l in (2, 1, 0):
                    along = along * (coef[l, I0_ + component, t, rows, :] * coef[l, U_, t, rows, :])
                reach[component, t, inner, :] = along
                weight = fric[t, rows, :] * bed[component, t, inner, :]
                total = total + weight * s4[component * LAYERS, t, rows, :]
                terms_in[1 + component, t, inner, :] = weight * along
            terms_in[0, t, inner, :] = total
        return carry

    lax.fori_loop(0, BLOCKS, finish, 0, unroll=8)
    used = len(copies)
    more = [(terms_in, terms), (reach, fourth.at[1])]
    more += [(s4.at[c * LAYERS, pl.ds(0, 2), main, :], fourth.at[0, c]) for c in range(2)]
    for copy in copies + start_copies(sems.at[pl.ds(used, len(more))], more):
        copy.wait()


def gradient_kernel(n, strip_rows, terms, surface, *rest):
    datas, grads = rest[:n], rest[n:]
    me = lax.axis_index("gy")
    for k in range(n):
        source = lax.rem(me - k + n, n)
        for b in range(strip_rows // ROWS):
            rows = pl.ds(pl.multiple_of(source * strip_rows + b * ROWS, ROWS), ROWS)
            part = pl.ds(b * ROWS, ROWS)
            for t in range(2):
                total = terms[0, t, rows, :]
                for c in range(2):
                    force = datas[k][2 + c, t, part, :] * (
                        datas[k][c, t, part, :] - surface[c, rows, t * LANES : (t + 1) * LANES]
                    )
                    total = total + terms[1 + c, t, rows, :] * force
                grads[k][t, part, :] = total


def after_forcing(n, strip_rows, surface, above, below, first, second, third, fourth, visc_in, ice_in, *rest):
    controls, datas, out = rest[:n], rest[n : 2 * n], rest[2 * n]
    s1, s2, s3, s4, visc, ice, bottom, surf, given, coef, force, packed, sems = rest[2 * n + 1 :]
    me = lax.axis_index("gy")
    lane = lane_index()
    blocks = strip_rows // ROWS
    main = pl.ds(ROWS, TILE)
    pairs = [(visc_in, visc), (ice_in, ice)]
    for t in range(2):
        pairs += [(surface.at[:, :, pl.ds(t * LANES, LANES)], surf.at[:, t, main, :])]
    for k in range(n):
        source = lax.rem(me - k + n, n)
        rows = pl.ds(pl.multiple_of(ROWS + source * strip_rows, ROWS), strip_rows)
        tail = pl.ds(2 * strip_rows + EDGE_ROWS, ROWS * rim_tiles(strip_rows))
        pairs += [(datas[k], given.at[:, 0:2, rows, :]), (controls[k].at[tail], packed.at[k])]
    early = len(pairs)
    pairs += [(first.at[c], s1.at[pl.ds(c * LAYERS + 2, 2)]) for c in range(2)]
    pairs += [(second.at[c], s2.at[pl.ds(c * LAYERS + 1, 2)]) for c in range(2)]
    pairs += [(third.at[c], s3.at[pl.ds(c * LAYERS, 2)]) for c in range(2)]
    pairs += [(fourth, bottom)]
    copies = start_copies(sems, pairs)
    for message, row in ((above, 0), (below, ROWS + TILE)):
        rows = pl.ds(row, ROWS)
        for t in range(3):
            for c in range(2):
                surf[c, t, rows, :] = rim_rows(message, 12 + c, t)
            for a in range(4):
                given[a, t, rows, :] = rim_rows(message, 16 + a, t)

    def sides(r, carry):
        left, right = sides_at(n, strip_rows, controls, r * ROWS)
        for h in range(2):
            to = pl.ds(pl.multiple_of(ROWS + h * HALF + r * ROWS, ROWS), ROWS)
            for c in range(2):
                surf[c, 2, to, :] = side_columns(lane, left, right, h * TILE_FIELDS + 12 + c)
        return carry

    lax.fori_loop(0, HALF // ROWS, sides, 0, unroll=4)
    for copy in copies[:early]:
        copy.wait()
    for k in range(n):
        source = lax.rem(me - k + n, n)
        for a in range(1, 5):
            for b in range(blocks):
                part, slot = rim_slot(a, b, blocks)
                to = pl.ds(pl.multiple_of(ROWS + source * strip_rows + b * ROWS, ROWS), ROWS)
                given[a - 1, 2, to, :] = strip_columns(lane, packed[k, pl.ds(part * ROWS, ROWS), :], slot)
    coefficients(coef, visc, ice, lane)
    for copy in copies[early:]:
        copy.wait()

    def add_forcing(i, carry):
        rows = pl.ds(FIRST + i * ROWS, ROWS)
        for t in range(3):
            for c in range(2):
                value = given[2 + c, t, rows, :] * (given[c, t, rows, :] - surf[c, t, rows, :])
                force[c, t, rows, :] = value
                value = coef[3, I0_ + c, t, rows, :] * value
                s1[c * LAYERS + 3, t, rows, :] = s1[c * LAYERS + 3, t, rows, :] + value
                value = coef[2, I0_ + c, t, rows, :] * (coef[2, U_, t, rows, :] * value)
                s2[c * LAYERS + 2, t, rows, :] = s2[c * LAYERS + 2, t, rows, :] + value
                value = coef[1, I0_ + c, t, rows, :] * (coef[1, U_, t, rows, :] * value)
                s3[c * LAYERS + 1, t, rows, :] = s3[c * LAYERS + 1, t, rows, :] + value
        return carry

    lax.fori_loop(0, STEPS, add_forcing, 0, unroll=11)
    for i in range(BLOCKS):
        rows, inner = pl.ds(ROWS + i * ROWS, ROWS), pl.ds(i * ROWS, ROWS)
        for t in range(2):
            for c in range(2):
                s4[c * LAYERS, t, rows, :] = bottom[0, c, t, inner, :] + bottom[1, c, t, inner, :] * force[c, t, rows, :]
    sweep_layer(coef, s1, s2, 3, lane, force)
    sweep_layer(coef, s2, s3, 2, lane)
    sweep_layer(coef, s2, s3, 3, lane, force)
    for l in (1, 2, 3):
        sweep_layer(coef, s3, s4, l, lane, force if l == 3 else None, last=True)
    outs = [(s4.at[:, t, main, :], out.at[:, :, pl.ds(t * LANES, LANES)]) for t in range(2)]
    for copy in start_copies(sems, outs):
        copy.wait()


def unpack_gradient(n, *refs):
    parts, out = refs[:n], refs[n]
    me = lax.axis_index("gy")
    for k in range(n):
        source = lax.rem(me + k, n)
        for t in range(2):
            out[:, pl.ds(pl.multiple_of(source * TILE + t * LANES, LANES), LANES)] = parts[k][t]


def f32(*shape):
    return jax.ShapeDtypeStruct(shape, jnp.float32)


def vmem_f32(*shape):
    return pltpu.VMEM(shape, jnp.float32)


def frames(*leading):
    return vmem_f32(*leading, 3, FRAME, LANES)


def f32_frames(*leading):
    return f32(*leading, 3, FRAME, LANES)


def per_device(
    adjoint_start,
    viscosity,
    base_velocity,
    surface_velocity,
    ice_mask,
    log_friction,
    observed_velocity,
    obs_weight,
):
    n = lax.axis_size("gy")
    size_x = lax.axis_size("gx")
    strip_rows = log_friction.shape[0]
    width = n * TILE
    vmem = pl.BlockSpec(memory_space=pltpu.VMEM)
    smem = pl.BlockSpec(memory_space=pltpu.SMEM)
    anywhere = pl.BlockSpec(memory_space=pl.ANY)
    adjoint = adjoint_start.reshape((2 * LAYERS, TILE, TILE))
    rim_size = ROWS * rim_tiles(strip_rows)

    def params(mib):
        return pltpu.CompilerParams(vmem_limit_bytes=mib * MIB)

    def ring(k):
        return [(i, (i + k) % n) for i in range(n)]

    def line(size, k):
        return [(i, i + k) for i in range(size) if 0 <= i + k < size]

    def control_shape(k):
        return f32(control_rows(strip_rows) + (HALF if k in (1, n - 1) else 0), LANES)

    packed = pl.pallas_call(
        functools.partial(pack_kernel, n, strip_rows),
        out_shape=[control_shape(k) for k in range(n)] + [f32(4, 2, strip_rows, LANES)] * n,
        in_specs=[smem] + [anywhere] * 6,
        out_specs=[vmem] * (2 * n),
        scratch_shapes=[
            vmem_f32(strip_rows, width),
            vmem_f32(2, strip_rows, width),
            vmem_f32(2, strip_rows, width),
            vmem_f32(2 * LAYERS, TILE, TILE),
            vmem_f32(LAYERS, TILE, TILE),
            vmem_f32(2, TILE, TILE),
            pltpu.SemaphoreType.DMA((6,)),
        ],
        compiler_params=params(56),
    )(ice_mask, log_friction, observed_velocity, obs_weight, adjoint, viscosity, surface_velocity)
    controls, datas = packed[:n], packed[n:]
    controls = [controls[0]] + [lax.ppermute(controls[k], "gy", ring(k)) for k in range(1, n)]
    controls, datas = lax.optimization_barrier((controls, datas))
    datas = [datas[0]] + [lax.ppermute(datas[k], "gy", ring(k)) for k in range(1, n)]

    rows_up, rows_down = pl.pallas_call(
        functools.partial(pack_rows, n, strip_rows),
        out_shape=[f32(PAIRS, 3, ROWS, LANES)] * 2,
        in_specs=[smem] + [anywhere] * 3 + [vmem] * n,
        out_specs=[vmem] * 2,
        scratch_shapes=[
            vmem_f32(2, 2 * LAYERS, ROWS, TILE),
            vmem_f32(2, LAYERS, ROWS, TILE),
            vmem_f32(2, 2, ROWS, TILE),
            vmem_f32(2, 5, 3, ROWS, LANES),
            pltpu.SemaphoreType.DMA((6,)),
        ],
        compiler_params=params(4),
    )(ice_mask, adjoint, viscosity, surface_velocity, *controls)
    above = lax.ppermute(rows_up, "gx", line(size_x, 1))
    below = lax.ppermute(rows_down, "gx", line(size_x, -1))

    terms, first, second, third, fourth, visc, ice = pl.pallas_call(
        functools.partial(before_forcing, n, strip_rows),
        out_shape=[
            f32(3, 2, TILE, LANES),
            f32_frames(2, 2),
            f32_frames(2, 2),
            f32_frames(2, 2),
            f32(2, 2, 2, TILE, LANES),
            f32_frames(LAYERS),
            f32_frames(),
        ],
        in_specs=[smem] + [anywhere] * 3 + [vmem] * (2 + n),
        out_specs=[anywhere] * 7,
        scratch_shapes=[frames(8)] * 5
        + [
            frames(LAYERS),
            frames(),
            frames(),
            frames(),
            vmem_f32(2, 2, TILE, LANES),
            frames(LAYERS, 9),
            vmem_f32(3, 2, TILE, LANES),
            vmem_f32(2, 2, TILE, LANES),
            vmem_f32(n, rim_size, LANES),
            pltpu.SemaphoreType.DMA((16 + 3 * n,)),
        ],
        compiler_params=params(42),
    )(ice_mask, adjoint, viscosity, base_velocity, above, below, *controls)

    grads = pl.pallas_call(
        functools.partial(gradient_kernel, n, strip_rows),
        out_shape=[f32(2, strip_rows, LANES)] * n,
        in_specs=[vmem] * (2 + n),
        out_specs=[vmem] * n,
        compiler_params=params(6),
    )(terms, surface_velocity, *datas)
    parts = [grads[0]] + [lax.ppermute(grads[k], "gy", ring(n - k)) for k in range(1, n)]

    out = pl.pallas_call(
        functools.partial(after_forcing, n, strip_rows),
        out_shape=f32(2 * LAYERS, TILE, TILE),
        in_specs=[anywhere] + [vmem] * 2 + [anywhere] * 6 + [vmem] * n + [anywhere] * n,
        out_specs=anywhere,
        scratch_shapes=[frames(8)] * 4
        + [
            frames(LAYERS),
            frames(),
            vmem_f32(2, 2, 2, TILE, LANES),
            frames(2),
            frames(4),
            frames(LAYERS, 9),
            frames(2),
            vmem_f32(n, rim_size, LANES),
            pltpu.SemaphoreType.DMA((12 + 2 * n,)),
        ],
        compiler_params=params(42),
    )(surface_velocity, above, below, first, second, third, fourth, visc, ice, *controls, *datas)

    gradient = pl.pallas_call(
        functools.partial(unpack_gradient, n),
        out_shape=f32(strip_rows, width),
        in_specs=[vmem] * n,
        out_specs=vmem,
        compiler_params=params(4),
    )(*parts)
    return gradient, out.reshape(adjoint_start.shape)


def solution(mesh):
    placed = (
        P(None, None, "gx", "gy"),
        P(None, "gx", "gy"),
        P(None, "gx", "gy"),
        P(None, "gx", "gy"),
        P("gx", "gy"),
        P(("gx", "gy"), None),
        P(None, ("gx", "gy"), None),
        P(None, ("gx", "gy"), None),
    )
    return jax.shard_map(
        per_device,
        mesh=mesh,
        in_specs=placed,
        out_specs=(P(("gx", "gy"), None), P(None, None, "gx", "gy")),
        check_vma=False,
    )
```

time: 78.1 us -> 68.5 us (0.88); the launches traced: 76.8 us -> 68.3 us
  starting transfers between devices: 28.2 us -> 17.3 us
  waiting for transfers between devices: 11.8 us -> 16.4 us
  local copies, waits for them, and re-layouts: 2.01 us -> 0.92 us
  Pallas kernels: 33.9 us -> 32.9 us
    ppermute x3, waiting for transfers between devices: 0.01 us -> 11.8 us  [per_device(): lax.ppermute(controls[k], 'gy', ring(k))]
    ppermute x5 -> x3, starting transfers between devices: 9.45 us -> 3.28 us  [per_device(): lax.ppermute(grads[k], 'gy', ring(n - k))]
    ppermute x5 -> x3, waiting for transfers between devices: 6.04 us -> 0.01 us  [per_device(): lax.ppermute(grads[k], 'gy', ring(n - k))]
    ppermute x3, waiting for transfers between devices: 3.32 us -> 0.01 us  [per_device(): lax.ppermute(datas[k], 'gy', ring(k))]
    ppermute x1, starting transfers between devices: 6.86 us -> 4.06 us  [per_device(): above = lax.ppermute(rows_up, 'gx', line(size_x, 1))]
    pallas_call x1, Pallas kernels: 3.22 us -> 0.97 us  [per_device(): pl.pallas_call(functools.partial(pack_rows, n, strip_rows), out_shape=[f3...]
    pallas_call x3 -> x4, Pallas kernels: 29 us -> 31.2 us  [the longest x1 14.8 us: per_device(): pl.pallas_call(functools.partial(before_forcing, n, strip_rows), out_shap...]
    ppermute x1, waiting for transfers between devices: 2.44 us -> 4.55 us  [per_device(): below = lax.ppermute(rows_down, 'gx', line(size_x, -1))]
  transfers between devices with their start and end apart: 13 -> 11, of which waited for: 6 -> 2; matrix products, arithmetic and copies ran while one was open for 0% -> 0% of each run, Pallas kernels for 9% -> 38%
where the time goes in v2:
time: 68.5 us; the launch traced here: 68.3 us
  Pallas kernels  32.9 us (48%)
  starting transfers between devices  17.3 us (25%)
  waiting for transfers between devices  16.4 us (24%)
  local copies, waits for them, and re-layouts  0.92 us (1%)
  between operations  0.81 us (1%)
    pallas_call x1, Pallas kernels, per_device(): pl.pallas_call(functools.partial(before_forcing, n, strip_rows), out_shap...  14.8 us
    ppermute x3, waiting for transfers between devices, per_device(): lax.ppermute(controls[k], 'gy', ring(k))  11.8 us
    pallas_call x1, Pallas kernels, per_device(): pl.pallas_call(functools.partial(after_forcing, n, strip_rows), out_shape...  10.5 us
    pallas_call x1, Pallas kernels, per_device(): pl.pallas_call(functools.partial(pack_kernel, n, strip_rows), out_shape=[...  5.76 us
    ppermute x3, starting transfers between devices, per_device(): lax.ppermute(controls[k], 'gy', ring(k))  4.66 us
    ppermute x1, waiting for transfers between devices, per_device(): below = lax.ppermute(rows_down, 'gx', line(size_x, -1))  4.55 us
    ppermute x1, starting transfers between devices, per_device(): above = lax.ppermute(rows_up, 'gx', line(size_x, 1))  4.06 us
    ppermute x3, starting transfers between devices, per_device(): lax.ppermute(grads[k], 'gy', ring(n - k))  3.28 us
  transfers between devices with their start and end apart: 11, of which 2 were waited for; matrix products, arithmetic and copies ran while one was open for 0% of the time, Pallas kernels for 38%

profile of v2, /device:TPU:1, one launch (start us, length us, event | category | flops | bytes accessed | tf_op | source)
XLA Modules:
  0.0 68.3 jit_solution(10956497779424155442)
XLA Ops:
  0.6 0.0 copy-start
  0.6 0.0 copy-start.1
  0.7 0.0 copy-start.2
  0.7 0.0 copy-start.7
  0.7 5.8 %shard_map.95 = (f32[184,128]{1,0:T(8,128)}, f32[312,128]{1,0:T(8,128)}, f32[184,128]{1,0:T(8,128)}, f32[312,128]{1,0:T(8,128)}, f32[4,2,64,128]{3,2,1,0:T(8,128...) custom-call(s32[2,2]{1,0:T(2,128)} %mask.5, f32[64,1024]{1,0:T(8,128)} %logf.1, ...), custom_call_target="tpu_custom_call" | custom-call | tf_op jit(solution)/shard_map/pallas_call | solution.py:614
  6.4 2.2 %collective-permute-start = (f32[312,128]{1,0:T(8,128)}, f32[312,128]{1,0:T(8,128)S(1)}, u32[]{:S(2)}, u32[]{:S(2)}) collective-permute-start(f32[312,128]{1,0:T(8,128)} %get-tuple-element.32), channel_id=1, source_target_pairs={{0,1},{1,2},{2,3},{3,0},{4,5},{5,6},{6,7},{7,4},{8,9},{9,10},{10,1... | collective-permute-start | bytes 479240 | tf_op jit(solution)/shard_map/ppermute | solution.py:631
  8.6 2.1 %collective-permute-start.2 = (f32[312,128]{1,0:T(8,128)}, f32[312,128]{1,0:T(8,128)S(1)}, u32[]{:S(2)}, u32[]{:S(2)}) collective-permute-start(f32[312,128]{1,0:T(8,128)} %get-tuple-element.34), channel_id=1, source_target_pairs={{0,3},{1,0},{2,1},{3,2},{4,7},{5,4},{6,5},{7,6},{8,11},{9,8},{10,9... | collective-permute-start | bytes 479240 | tf_op jit(solution)/shard_map/ppermute | solution.py:631
  10.7 0.4 collective-permute-start.1
  11.1 11.8 %collective-permute-done.1.rest_2_ = f32[184,128]{1,0:T(8,128)S(1)} collective-permute-done((f32[184,128]{1,0:T(8,128)}, f32[184,128]{1,0:T(8,128)S(1)}, u32[]{:S(2)}, u32[]{:S(2)}) %collective-permute-start.1) | collective-permute-done | bytes 94240 | tf_op jit(solution)/shard_map/ppermute | solution.py:631
  22.9 0.0 collective-permute-done.rest_1_
  22.9 0.0 collective-permute-done.2.rest_3_
  22.9 0.0 collective-permute-start.5
  22.9 0.4 collective-permute-start.6
  23.3 2.9 %collective-permute-start.7 = (f32[4,2,64,128]{3,2,1,0:T(8,128)}, f32[4,2,64,128]{3,2,1,0:T(8,128)S(1)}, u32[]{:S(2)}, u32[]{:S(2)}) collective-permute-start(f32[4,2,64,128]{3,2,1,0:T(8,128)} %get-tuple-element.49), channel_id=1, source_target_pairs={{0,3},{1,0},{2,1},{3,2},{4,7},{5,4},{6,5},{7,6},{8,11},{9,8},{10,9... | collective-permute-start | bytes 786440 | tf_op jit(solution)/shard_map/ppermute | solution.py:633
  26.2 0.0 copy-done
  26.2 0.0 copy-done.1
  26.2 0.0 copy-done.2
  26.2 0.0 copy-done.7
  26.2 0.0 copy-start.4
  26.2 0.9 %copy-done.4 = f32[184,128]{1,0:T(8,128)S(1)} copy-done((f32[184,128]{1,0:T(8,128)S(1)}, f32[184,128]{1,0:T(8,128)}, u32[]{:S(2)}) %copy-start.4) | copy-done | bytes 94232
  27.1 0.0 copy-start.5
  27.1 0.0 copy-start.6
  27.1 1.0 %shard_map.96 = (f32[10,3,8,128]{3,2,1,0:T(8,128)S(1)}, f32[10,3,8,128]{3,2,1,0:T(8,128)S(1)}) custom-call(s32[2,2]{1,0:T(2,128)S(1)} %copy-done.7, f32[8,256,256]{2,1,0:T(8,128)S(1)} %bitcast.4, f32[4,256,256]{2,1,0:T(8,128)S(1)} %copy-done.1, f32[2,256,256]{2,1,0:T(8,128)S(1)} %copy-done.2, f32[184,128]{1,0:T(8,128)S(1)} %copy-done.4, ...), custom_call_target="tpu_custom_call" | custom-call | tf_op jit(solution)/shard_map/pallas_call | solution.py:635
  28.1 4.1 %collective-permute-start.3 = (f32[10,3,8,128]{3,2,1,0:T(8,128)S(1)}, f32[10,3,8,128]{3,2,1,0:T(8,128)S(1)}, u32[]{:S(2)}, u32[]{:S(2)}) collective-permute-start(f32[10,3,8,128]{3,2,1,0:T(8,128)S(1)} %get-tuple-element.43), channel_id=1, source_target_pairs={{0,4},{4,8},{8,12},{12,16},{16,20},{20,24},{24,28},{1,5},{5,9},{9,... | collective-permute-start | bytes 368648 | tf_op jit(solution)/shard_map/ppermute | solution.py:649
  32.1 0.0 copy-start.3
  32.1 2.1 %collective-permute-start.4 = (f32[10,3,8,128]{3,2,1,0:T(8,128)S(1)}, f32[10,3,8,128]{3,2,1,0:T(8,128)S(1)}, u32[]{:S(2)}, u32[]{:S(2)}) collective-permute-start(f32[10,3,8,128]{3,2,1,0:T(8,128)S(1)} %get-tuple-element.44), channel_id=1, source_target_pairs={{4,0},{8,4},{12,8},{16,12},{20,16},{24,20},{28,24},{5,1},{9,5},{13... | collective-permute-start | bytes 368648 | tf_op jit(solution)/shard_map/ppermute | solution.py:650
  34.2 0.0 collective-permute-done.3.above
  34.2 4.6 %collective-permute-done.4.below = f32[10,3,8,128]{3,2,1,0:T(8,128)S(1)} collective-permute-done((f32[10,3,8,128]{3,2,1,0:T(8,128)S(1)}, f32[10,3,8,128]{3,2,1,0:T(8,128)S(1)}, u32[]{:S(2)}, u32[]{:S(2)}) %collective-permute-start.4) | collective-permute-done | bytes 122912 | tf_op jit(solution)/shard_map/ppermute | solution.py:650
  38.8 0.0 copy-done.5
  38.8 0.0 copy-done.6
  38.8 14.8 %shard_map.97 = (f32[3,2,256,128]{3,2,1,0:T(8,128)S(1)}, f32[2,2,3,272,128]{4,3,2,1,0:T(8,128)S(1)}, f32[2,2,3,272,128]{4,3,2,1,0:T(8,128)S(1)}, f32[2,2,3,272,1...) custom-call(s32[2,2]{1,0:T(2,128)S(1)} %copy-done.7, ...), custom_call_target="tpu_custom_call" | custom-call | tf_op jit(solution)/shard_map/pallas_call | solution.py:652
  53.6 0.0 collective-permute-done.5.rest_1_.rest_5_
  53.6 0.0 collective-permute-done.6.rest_2_.rest_6_
  53.6 0.0 collective-permute-done.7.rest_3_.rest_7_
  53.6 0.0 copy-done.3
  53.6 0.2 shard_map.98
  53.8 0.4 collective-permute-start.8
  54.2 1.5 %collective-permute-start.9 = (f32[2,64,128]{2,1,0:T(8,128)S(1)}, f32[2,64,128]{2,1,0:T(8,128)S(1)}, u32[]{:S(2)}, u32[]{:S(2)}) collective-permute-start(f32[2,64,128]{2,1,0:T(8,128)S(1)} %get-tuple-element.52), channel_id=1, source_target_pairs={{0,2},{1,3},{2,0},{3,1},{4,6},{5,7},{6,4},{7,5},{8,10},{9,11},{10,... | collective-permute-start | bytes 196616 | tf_op jit(solution)/shard_map/ppermute | solution.py:688
  55.7 1.4 %collective-permute-start.10 = (f32[2,64,128]{2,1,0:T(8,128)S(1)}, f32[2,64,128]{2,1,0:T(8,128)S(1)}, u32[]{:S(2)}, u32[]{:S(2)}) collective-permute-start(f32[2,64,128]{2,1,0:T(8,128)S(1)} %get-tuple-element.53), channel_id=1, source_target_pairs={{0,1},{1,2},{2,3},{3,0},{4,5},{5,6},{6,7},{7,4},{8,9},{9,10},{10,1... | collective-permute-start | bytes 196616 | tf_op jit(solution)/shard_map/ppermute | solution.py:688
  57.1 10.5 %shard_map.100 = f32[8,256,256]{2,1,0:T(8,128)} custom-call(f32[2,256,256]{2,1,0:T(8,128)S(1)} %copy-done.2, f32[10,3,8,128]{3,2,1,0:T(8,128)S(1)} %collective-permute-done.3.above, f32[10,3,8,128]{3,2,1,0:T(8,128)S(1)} %collective-permute-done.4.below, f32[2,2,3,272,128]{4,3,2,1,0:T(8,128)S(1)} %get-tuple-element.54.first, ...), custom_call_target="tpu_custom_call" | custom-call | tf_op jit(solution)/shard_map/pallas_call | solution.py:690
  67.5 0.0 collective-permute-done.8.refs_1_
  67.6 0.0 collective-permute-done.9.refs_2_
  67.6 0.0 collective-permute-done.10.refs_3_
  67.6 0.8 %shard_map.99 = f32[64,1024]{1,0:T(8,128)} custom-call(f32[2,64,128]{2,1,0:T(8,128)S(1)} %get-tuple-element.50.refs_0_, f32[2,64,128]{2,1,0:T(8,128)S(1)} %collective-permute-done.8.refs_1_, f32[2,64,128]{2,1,0:T(8,128)S(1)} %collective-permute-done.9.refs_2_, f32[2,64,128]{2,1,0:T(8,128)S(1)} %collective-permute-done.10.refs_3_), custom_call_target="tpu_custom_call" | custom-call | tf_op jit(solution)/shard_map/pallas_call | solution.py:710
Async XLA Ops:
  0.6 25.5 %copy-start = (f32[2,4,256,256]{3,2,1,0:T(8,128)S(1)}, f32[2,4,256,256]{3,2,1,0:T(8,128)}, u32[]{:S(2)}) copy-start(f32[2,4,256,256]{3,2,1,0:T(8,128)} %param.8) | copy-start | bytes 6291460
  0.6 25.5 %copy-start.1 = (f32[4,256,256]{2,1,0:T(8,128)S(1)}, f32[4,256,256]{2,1,0:T(8,128)}, u32[]{:S(2)}) copy-start(f32[4,256,256]{2,1,0:T(8,128)} %viscosity.5) | copy-start | bytes 3145732
  0.7 25.5 %copy-start.2 = (f32[2,256,256]{2,1,0:T(8,128)S(1)}, f32[2,256,256]{2,1,0:T(8,128)}, u32[]{:S(2)}) copy-start(f32[2,256,256]{2,1,0:T(8,128)} %surface.7) | copy-start | bytes 1572868
  0.7 25.5 %copy-start.7 = (s32[2,2]{1,0:T(2,128)S(1)}, s32[2,2]{1,0:T(2,128)}, u32[]{:S(2)}) copy-start(s32[2,2]{1,0:T(2,128)} %mask.5) | copy-start | bytes 52
  6.4 16.5 %collective-permute-start = (f32[312,128]{1,0:T(8,128)}, f32[312,128]{1,0:T(8,128)S(1)}, u32[]{:S(2)}, u32[]{:S(2)}) collective-permute-start(f32[312,128]{1,0:T(8,128)} %get-tuple-element.32), channel_id=1, source_target_pairs={{0,1},{1,2},{2,3},{3,0},{4,5},{5,6},{6,7},{7,4},{8,9},{9,10},{10,1... | collective-permute-start | bytes 479240 | tf_op jit(solution)/shard_map/ppermute | solution.py:631
  8.6 14.3 %collective-permute-start.2 = (f32[312,128]{1,0:T(8,128)}, f32[312,128]{1,0:T(8,128)S(1)}, u32[]{:S(2)}, u32[]{:S(2)}) collective-permute-start(f32[312,128]{1,0:T(8,128)} %get-tuple-element.34), channel_id=1, source_target_pairs={{0,3},{1,0},{2,1},{3,2},{4,7},{5,4},{6,5},{7,6},{8,11},{9,8},{10,9... | collective-permute-start | bytes 479240 | tf_op jit(solution)/shard_map/ppermute | solution.py:631
  10.7 12.2 %collective-permute-start.1 = (f32[184,128]{1,0:T(8,128)}, f32[184,128]{1,0:T(8,128)S(1)}, u32[]{:S(2)}, u32[]{:S(2)}) collective-permute-start(f32[184,128]{1,0:T(8,128)} %get-tuple-element.33), channel_id=1, source_target_pairs={{0,2},{1,3},{2,0},{3,1},{4,6},{5,7},{6,4},{7,5},{8,10},{9,11},{10,... | collective-permute-start | bytes 282632 | tf_op jit(solution)/shard_map/ppermute | solution.py:631
  22.9 30.7 %collective-permute-start.5 = (f32[4,2,64,128]{3,2,1,0:T(8,128)}, f32[4,2,64,128]{3,2,1,0:T(8,128)S(1)}, u32[]{:S(2)}, u32[]{:S(2)}) collective-permute-start(f32[4,2,64,128]{3,2,1,0:T(8,128)} %get-tuple-element.47), channel_id=1, source_target_pairs={{0,1},{1,2},{2,3},{3,0},{4,5},{5,6},{6,7},{7,4},{8,9},{9,10},{10,1... | collective-permute-start | bytes 786440 | tf_op jit(solution)/shard_map/ppermute | solution.py:633
  22.9 30.7 %collective-permute-start.6 = (f32[4,2,64,128]{3,2,1,0:T(8,128)}, f32[4,2,64,128]{3,2,1,0:T(8,128)S(1)}, u32[]{:S(2)}, u32[]{:S(2)}) collective-permute-start(f32[4,2,64,128]{3,2,1,0:T(8,128)} %get-tuple-element.48), channel_id=1, source_target_pairs={{0,2},{1,3},{2,0},{3,1},{4,6},{5,7},{6,4},{7,5},{8,10},{9,11},{10,... | collective-permute-start | bytes 786440 | tf_op jit(solution)/shard_map/ppermute | solution.py:633
  23.3 30.3 %collective-permute-start.7 = (f32[4,2,64,128]{3,2,1,0:T(8,128)}, f32[4,2,64,128]{3,2,1,0:T(8,128)S(1)}, u32[]{:S(2)}, u32[]{:S(2)}) collective-permute-start(f32[4,2,64,128]{3,2,1,0:T(8,128)} %get-tuple-element.49), channel_id=1, source_target_pairs={{0,3},{1,0},{2,1},{3,2},{4,7},{5,4},{6,5},{7,6},{8,11},{9,8},{10,9... | collective-permute-start | bytes 786440 | tf_op jit(solution)/shard_map/ppermute | solution.py:633
  26.2 0.9 %copy-start.4 = (f32[184,128]{1,0:T(8,128)S(1)}, f32[184,128]{1,0:T(8,128)}, u32[]{:S(2)}) copy-start(f32[184,128]{1,0:T(8,128)} %get-tuple-element.39.rest_0_) | copy-start | bytes 282628
  27.1 11.7 %copy-start.5 = (f32[184,128]{1,0:T(8,128)S(1)}, f32[184,128]{1,0:T(8,128)}, u32[]{:S(2)}) copy-start(f32[184,128]{1,0:T(8,128)} %get-tuple-element.39.rest_0_) | copy-start | bytes 282628
  27.1 11.7 %copy-start.6 = (f32[2,256,256]{2,1,0:T(8,128)S(1)}, f32[2,256,256]{2,1,0:T(8,128)}, u32[]{:S(2)}) copy-start(f32[2,256,256]{2,1,0:T(8,128)} %base.1) | copy-start | bytes 1572868
  28.1 6.1 %collective-permute-start.3 = (f32[10,3,8,128]{3,2,1,0:T(8,128)S(1)}, f32[10,3,8,128]{3,2,1,0:T(8,128)S(1)}, u32[]{:S(2)}, u32[]{:S(2)}) collective-permute-start(f32[10,3,8,128]{3,2,1,0:T(8,128)S(1)} %get-tuple-element.43), channel_id=1, source_target_pairs={{0,4},{4,8},{8,12},{12,16},{16,20},{20,24},{24,28},{1,5},{5,9},{9,... | collective-permute-start | bytes 368648 | tf_op jit(solution)/shard_map/ppermute | solution.py:649
  32.1 21.5 %copy-start.3 = (f32[4,2,64,128]{3,2,1,0:T(8,128)S(1)}, f32[4,2,64,128]{3,2,1,0:T(8,128)}, u32[]{:S(2)}) copy-start(f32[4,2,64,128]{3,2,1,0:T(8,128)} %get-tuple-element.46.rest_0_.rest_4_) | copy-start | bytes 786436
  32.1 6.6 %collective-permute-start.4 = (f32[10,3,8,128]{3,2,1,0:T(8,128)S(1)}, f32[10,3,8,128]{3,2,1,0:T(8,128)S(1)}, u32[]{:S(2)}, u32[]{:S(2)}) collective-permute-start(f32[10,3,8,128]{3,2,1,0:T(8,128)S(1)} %get-tuple-element.44), channel_id=1, source_target_pairs={{4,0},{8,4},{12,8},{16,12},{20,16},{24,20},{28,24},{5,1},{9,5},{13... | collective-permute-start | bytes 368648 | tf_op jit(solution)/shard_map/ppermute | solution.py:650
  53.8 13.8 %collective-permute-start.8 = (f32[2,64,128]{2,1,0:T(8,128)S(1)}, f32[2,64,128]{2,1,0:T(8,128)S(1)}, u32[]{:S(2)}, u32[]{:S(2)}) collective-permute-start(f32[2,64,128]{2,1,0:T(8,128)S(1)} %get-tuple-element.51), channel_id=1, source_target_pairs={{0,3},{1,0},{2,1},{3,2},{4,7},{5,4},{6,5},{7,6},{8,11},{9,8},{10,9... | collective-permute-start | bytes 196616 | tf_op jit(solution)/shard_map/ppermute | solution.py:688
  54.2 13.4 %collective-permute-start.9 = (f32[2,64,128]{2,1,0:T(8,128)S(1)}, f32[2,64,128]{2,1,0:T(8,128)S(1)}, u32[]{:S(2)}, u32[]{:S(2)}) collective-permute-start(f32[2,64,128]{2,1,0:T(8,128)S(1)} %get-tuple-element.52), channel_id=1, source_target_pairs={{0,2},{1,3},{2,0},{3,1},{4,6},{5,7},{6,4},{7,5},{8,10},{9,11},{10,... | collective-permute-start | bytes 196616 | tf_op jit(solution)/shard_map/ppermute | solution.py:688
  55.7 11.9 %collective-permute-start.10 = (f32[2,64,128]{2,1,0:T(8,128)S(1)}, f32[2,64,128]{2,1,0:T(8,128)S(1)}, u32[]{:S(2)}, u32[]{:S(2)}) collective-permute-start(f32[2,64,128]{2,1,0:T(8,128)S(1)} %get-tuple-element.53), channel_id=1, source_target_pairs={{0,1},{1,2},{2,3},{3,0},{4,5},{5,6},{6,7},{7,4},{8,9},{9,10},{10,1... | collective-permute-start | bytes 196616 | tf_op jit(solution)/shard_map/ppermute | solution.py:688

commit v3 on v2

v3 whole, which is shorter than its diff:
```python
import functools

import jax
import jax.numpy as jnp
from jax import lax
from jax.experimental import pallas as pl
from jax.experimental.pallas import tpu as pltpu
from jax.sharding import PartitionSpec as P

SWEEPS = 4
DAMPING = 0.8
VERTICAL = 2.0
COUPLING = 3.0
TIKHONOV = 0.25

LAYERS = 4
LANES = 128
ROWS = 8
TILE = 256
FRAME = TILE + 2 * ROWS
HALF = TILE // 2
BLOCKS = TILE // ROWS
FIRST = 4
STEPS = BLOCKS + 1
TILE_FIELDS = 15
RIM_FIELDS = 20
PAIRS = RIM_FIELDS // 2
EDGE_ROWS = 4 * ROWS
MIB = 1024 * 1024


def row_index():
    return lax.broadcasted_iota(jnp.int32, (ROWS, LANES), 0)


def lane_index():
    return lax.broadcasted_iota(jnp.int32, (ROWS, LANES), 1)


def roll_to(x, shift):
    shift = shift % LANES
    return x if shift == 0 else pltpu.roll(x, shift, 1)


def after(x, lane):
    a, b, c = (roll_to(v, -1) for v in x)
    last = lane == LANES - 1
    return jnp.where(last, b, a), jnp.where(last, c, b), jnp.where(last, a, c)


def before(x, lane):
    a, b, c = (roll_to(v, 1) for v in x)
    first = lane == 0
    return jnp.where(first, c, a), jnp.where(first, a, b), jnp.where(first, b, c)


def rim_slot(array, block, strip_blocks):
    position = array * strip_blocks + block
    return position // 16, position % 16


def rim_tiles(strip_rows):
    return -(-5 * (strip_rows // ROWS) // 16)


def control_rows(strip_rows):
    return 2 * strip_rows + EDGE_ROWS + ROWS * rim_tiles(strip_rows)


def pack_strips(n, strip_rows, logf, obs, weight, controls):
    me = lax.axis_index("gy")
    lane = lane_index()
    blocks = strip_rows // ROWS
    edge = pl.multiple_of(jnp.where(me == 0, 0, strip_rows - ROWS), ROWS)
    own = (row_index() < 4) == (me == 0)
    strips = [logf.at[...], obs.at[0], obs.at[1], weight.at[0], weight.at[1]]
    width = n * TILE
    for k in range(n):
        to = lax.rem(me + k, n)
        column = pl.multiple_of(to * TILE, TILE)
        left = pl.multiple_of(jnp.maximum(column - LANES, 0), LANES)
        right = pl.multiple_of(jnp.minimum(column + TILE, width - LANES), LANES)
        control = controls[k]
        for t in range(2):
            columns = pl.ds(column + t * LANES, LANES)
            control[pl.ds(t * strip_rows, strip_rows), :] = logf[:, columns]
            for a in range(2):
                ends = [strips[a + i][pl.ds(edge, ROWS), columns] for i in (1, 3)]
                both = jnp.where(own, ends[0], pltpu.roll(ends[1], 4, 0))
                control[pl.ds(2 * strip_rows + (a * 2 + t) * ROWS, ROWS), :] = both
        packed = [jnp.zeros((ROWS, LANES), jnp.float32) for _ in range(rim_tiles(strip_rows))]
        for a in range(5):
            for b in range(blocks):
                part, slot = rim_slot(a, b, blocks)
                rows = pl.ds(b * ROWS, ROWS)
                both = jnp.where(lane < 64, strips[a][rows, pl.ds(right, LANES)], strips[a][rows, pl.ds(left, LANES)])
                packed[part] = jnp.where(lane // 8 == slot, roll_to(both, 8 * slot + 4), packed[part])
        for part, value in enumerate(packed):
            control[pl.ds(2 * strip_rows + EDGE_ROWS + part * ROWS, ROWS), :] = value


def tile_field(a, state, visc, surf):
    if a < 8:
        return state.at[a]
    if a < 12:
        return visc.at[a - 8]
    return surf.at[a - 12]


CHUNKS = 2


def pack_columns(mask, state, visc, surf, up, down, first, chunk):
    lane = lane_index()
    count = HALF // ROWS // CHUNKS
    for r in range(chunk * count, (chunk + 1) * count):
        to_up = jnp.zeros((ROWS, LANES), jnp.float32)
        to_down = jnp.zeros((ROWS, LANES), jnp.float32)
        for h in range(2):
            rows = pl.ds(ROWS + h * HALF + r * ROWS, ROWS)
            for a in range(TILE_FIELDS):
                slot = h * TILE_FIELDS + a
                here = lane // 4 == slot
                if a == TILE_FIELDS - 1:
                    low = mask[h, 0].astype(jnp.float32)
                    high = mask[h, 1].astype(jnp.float32)
                    to_up = jnp.where(here, high, to_up)
                    to_down = jnp.where(here, low, to_down)
                else:
                    field = tile_field(a, state, visc, surf)
                    to_up = jnp.where(here, roll_to(field[1, rows, :], 4 * slot + 4), to_up)
                    to_down = jnp.where(here, roll_to(field[0, rows, :], 4 * slot), to_down)
        rows = pl.ds(first + r * ROWS, ROWS)
        up[rows, :] = to_up
        down[rows, :] = to_down


def start_copies(sems, pairs):
    copies = [pltpu.make_async_copy(source, target, sems.at[i]) for i, (source, target) in enumerate(pairs)]
    for copy in copies:
        copy.start()
    return copies


def pack_kernel(n, strip_rows, mask, logf, obs, weight, adjoint, viscosity, surface, *rest):
    controls, (state, visc, surf, logf_in, obs_in, weight_in, sems) = rest[:n], rest[n:]
    pairs = [(logf, logf_in), (obs, obs_in), (weight, weight_in)]
    size = HALF // CHUNKS
    for chunk in range(CHUNKS):
        for h in range(2):
            row = h * HALF + chunk * size
            for field, frame in ((adjoint, state), (viscosity, visc), (surface, surf)):
                for t in range(2):
                    source = field.at[:, pl.ds(row, size), pl.ds(t * LANES, LANES)]
                    pairs.append((source, frame.at[:, t, pl.ds(ROWS + row, size), :]))
    copies = start_copies(sems, pairs)
    for copy in copies[:3]:
        copy.wait()
    pack_strips(n, strip_rows, logf_in, obs_in, weight_in, controls)
    first = control_rows(strip_rows)
    for chunk in range(CHUNKS):
        for copy in copies[3 + 12 * chunk : 15 + 12 * chunk]:
            copy.wait()
        pack_columns(mask, state, visc, surf, controls[1], controls[n - 1], first, chunk)


def pack_observations(n, strip_rows, obs, weight, *rest):
    datas, (obs_in, weight_in, sems) = rest[:n], rest[n:]
    me = lax.axis_index("gy")
    for copy in start_copies(sems, [(obs, obs_in), (weight, weight_in)]):
        copy.wait()
    pairs = []
    for k in range(n):
        column = pl.multiple_of(lax.rem(me + k, n) * TILE, TILE)
        for t in range(2):
            columns = pl.ds(column + t * LANES, LANES)
            pairs.append((obs_in.at[:, :, columns], datas[k].at[0:2, t]))
            pairs.append((weight_in.at[:, :, columns], datas[k].at[2:4, t]))
    for copy in start_copies(sems, pairs):
        copy.wait()


def side_columns(lane, from_left, from_right, slot):
    left = roll_to(from_left, -(4 * slot + 4))
    right = roll_to(from_right, -4 * slot)
    return jnp.where(lane < 4, right, jnp.where(lane >= LANES - 4, left, 0.0))


def strip_columns(lane, packed, slot):
    value = roll_to(packed, -(8 * slot + 4))
    return jnp.where(jnp.logical_or(lane < 4, lane >= LANES - 4), value, 0.0)


def sides_at(n, strip_rows, controls, row):
    me = lax.axis_index("gy")
    rows = pl.ds(pl.multiple_of(control_rows(strip_rows) + row, ROWS), ROWS)
    left = jnp.where(me > 0, controls[1][rows, :], 0.0)
    right = jnp.where(me < n - 1, controls[n - 1][rows, :], 0.0)
    return left, right


def pack_rows(n, strip_rows, mask, state, visc, surf, *rest):
    controls, (up, down, rim) = rest[:n], rest[n:]
    me = lax.axis_index("gy")
    lane, sub = lane_index(), row_index()
    blocks = strip_rows // ROWS
    for h, owner in ((1, n - 1), (0, 0)):
        block = blocks - 1 if h else 0
        for k in range(n):

            @pl.when(lax.rem(me - k + n, n) == owner)
            def _():
                control = controls[k]
                for a in range(5):
                    for t in range(2):
                        if a == 0:
                            rim[h, a, t] = control[pl.ds(t * strip_rows + block * ROWS, ROWS), :]
                            continue
                        both = control[pl.ds(2 * strip_rows + ((a - 1) % 2 * 2 + t) * ROWS, ROWS), :]
                        rim[h, a, t] = both if a < 3 else pltpu.roll(both, 4, 0)
                    part, slot = rim_slot(a, block, blocks)
                    packed = control[pl.ds(2 * strip_rows + EDGE_ROWS + part * ROWS, ROWS), :]
                    rim[h, a, 2] = strip_columns(lane, packed, slot)

    for message, h in ((up, 1), (down, 0)):
        left, right = sides_at(n, strip_rows, controls, h * (HALF - ROWS))

        def field(a, t):
            if a >= TILE_FIELDS:
                return rim[h, a - TILE_FIELDS, t]
            if t == 2:
                return side_columns(lane, left, right, h * TILE_FIELDS + a)
            if a == TILE_FIELDS - 1:
                return jnp.full((ROWS, LANES), mask[h, t].astype(jnp.float32))
            return tile_field(a, state, visc, surf)[t, pl.ds(TILE if h else ROWS, ROWS), :]

        own = sub >= 4 if h else sub < 4
        for a in range(PAIRS):
            for t in range(3):
                message[a, t] = jnp.where(own, field(a, t), pltpu.roll(field(a + PAIRS, t), 4, 0))


def rim_rows(message, a, t):
    if a < PAIRS:
        return message[a, t]
    return pltpu.roll(message[a - PAIRS, t], 4, 0)


E_, N_, S_, U_, V_, K0_, K1_, I0_, I1_ = range(9)


def coefficients(coef, visc, ice, fric, lane):
    def step(i, carry):
        r = FIRST + i * ROWS
        rows, east, west = pl.ds(r, ROWS), pl.ds(r + 1, ROWS), pl.ds(r - 1, ROWS)
        cells = [ice[t, rows, :] for t in range(3)]
        layers = [[visc[l, t, rows, :] for t in range(3)] for l in range(LAYERS)]
        for l in range(LAYERS):
            centre = layers[l]
            north, south = after(centre, lane), before(centre, lane)
            for t in range(3):
                c = centre[t]
                e = 0.5 * (c + visc[l, t, east, :])
                w = 0.5 * (c + visc[l, t, west, :])
                nf = 0.5 * (c + north[t])
                sf = 0.5 * (c + south[t])
                coef[l, E_, t, rows, :] = e
                coef[l, N_, t, rows, :] = nf
                coef[l, S_, t, rows, :] = sf
                vertical = None
                if l < LAYERS - 1:
                    u = (0.5 * VERTICAL) * (c + layers[l + 1][t])
                    coef[l, U_, t, rows, :] = u
                    vertical = u
                if l > 0:
                    lower = (0.5 * VERTICAL) * (c + layers[l - 1][t])
                    vertical = lower if vertical is None else vertical + lower
                if l == 0:
                    vertical = vertical + fric[t, rows, :]
                coef[l, V_, t, rows, :] = (0.25 * COUPLING) * c
                rest = COUPLING * c + (1.0 - cells[t])
                ew, ns = e + w, nf + sf
                for c_, ax, ay in ((0, 4.0, 1.0), (1, 1.0, 4.0)):
                    own = (ax * ew if ax != 1.0 else ew) + (ay * ns if ay != 1.0 else ns) + vertical
                    inverse = DAMPING * cells[t] / (own + rest)
                    coef[l, I0_ + c_, t, rows, :] = inverse
                    coef[l, K0_ + c_, t, rows, :] = cells[t] - own * inverse
        return carry

    lax.fori_loop(0, STEPS, step, 0, unroll=STEPS)


def sweep_layer(coef, old, new, l, lane, force=None, last=False):
    first, steps, tiles = (ROWS, BLOCKS, 2) if last else (FIRST, STEPS, 3)

    def step(i, carry):
        r = first + i * ROWS
        rows, east, west = pl.ds(r, ROWS), pl.ds(r + 1, ROWS), pl.ds(r - 1, ROWS)
        e = [coef[l, E_, t, rows, :] for t in range(tiles)]
        w = [coef[l, E_, t, west, :] for t in range(tiles)]
        fluxes, mixes = [], []
        for c in range(2):
            m = [old(c, l)[t, rows, :] for t in range(3)]
            me = [old(c, l)[t, east, :] for t in range(3)]
            mw = [old(c, l)[t, west, :] for t in range(3)]
            mn, ms = after(m, lane), before(m, lane)
            across = [me[t] - mw[t] for t in range(3)]
            an, as_ = after(across, lane), before(across, lane)
            mixes.append([an[t] - as_[t] for t in range(tiles)])
            flux = []
            for t in range(tiles):
                x = e[t] * me[t] + w[t] * mw[t]
                y = coef[l, N_, t, rows, :] * mn[t] + coef[l, S_, t, rows, :] * ms[t]
                total = 4.0 * x + y if c == 0 else x + 4.0 * y
                if l < LAYERS - 1:
                    total = total + coef[l, U_, t, rows, :] * old(c, l + 1)[t, rows, :]
                if l > 0:
                    total = total + coef[l - 1, U_, t, rows, :] * old(c, l - 1)[t, rows, :]
                if force is not None:
                    total = total + force[c, t, rows, :]
                flux.append((total, m[t]))
            fluxes.append(flux)
        for c in range(2):
            for t in range(tiles):
                total, m = fluxes[c][t]
                total = total + coef[l, V_, t, rows, :] * mixes[1 - c][t]
                new(c, l)[t, rows, :] = (
                    coef[l, K0_ + c, t, rows, :] * m + coef[l, I0_ + c, t, rows, :] * total
                )
        return carry

    lax.fori_loop(0, steps, step, 0, unroll=steps)


def layers_of(ref):
    return lambda c, l: ref.at[c * LAYERS + l]


def before_forcing(n, strip_rows, mask, state_in, visc_in, surf_in, base, above, below, *rest):
    controls = rest[:n]
    s0, visc, surf, coef, s1, s2, s3, bottom, terms, reach, force = rest[n : n + 11]
    ice, logf, fric, bed, sems = rest[n + 11 :]
    me, mx = lax.axis_index("gy"), lax.axis_index("gx")
    size_x = lax.axis_size("gx")
    lane = lane_index()
    blocks = strip_rows // ROWS
    copies = start_copies(sems, [(base.at[:, :, pl.ds(t * LANES, LANES)], bed.at[:, t]) for t in range(2)])

    for h in range(2):
        for t in range(2):
            ice[t, pl.ds(ROWS + h * HALF, HALF), :] = jnp.full((HALF, LANES), mask[h, t].astype(jnp.float32))
    for message, row in ((above, 0), (below, ROWS + TILE)):
        rows = pl.ds(row, ROWS)
        for t in range(3):
            for a in range(8):
                s0[a, t, rows, :] = rim_rows(message, a, t)
            for a in range(4):
                visc[a, t, rows, :] = rim_rows(message, 8 + a, t)
            ice[t, rows, :] = rim_rows(message, 14, t)
            logf[t, rows, :] = rim_rows(message, 15, t)
            for c in range(2):
                difference = rim_rows(message, 16 + c, t) - rim_rows(message, 12 + c, t)
                force[c, t, rows, :] = rim_rows(message, 18 + c, t) * difference

    def sides(r, carry):
        left, right = sides_at(n, strip_rows, controls, r * ROWS)
        for h in range(2):
            to = pl.ds(pl.multiple_of(ROWS + h * HALF + r * ROWS, ROWS), ROWS)
            for a in range(TILE_FIELDS):
                value = side_columns(lane, left, right, h * TILE_FIELDS + a)
                if a == TILE_FIELDS - 1:
                    ice[2, to, :] = value
                else:
                    tile_field(a, s0, visc, surf)[2, to, :] = value
        return carry

    lax.fori_loop(0, HALF // ROWS, sides, 0, unroll=8)
    for k in range(n):
        source = lax.rem(me - k + n, n)
        for b in range(blocks):
            to = pl.ds(pl.multiple_of(ROWS + source * strip_rows + b * ROWS, ROWS), ROWS)
            for t in range(2):
                logf[t, to, :] = controls[k][pl.ds(t * strip_rows + b * ROWS, ROWS), :]
            values = []
            for a in range(5):
                part, slot = rim_slot(a, b, blocks)
                packed = controls[k][pl.ds(2 * strip_rows + EDGE_ROWS + part * ROWS, ROWS), :]
                values.append(strip_columns(lane, packed, slot))
            logf[2, to, :] = values[0]
            for c in range(2):
                force[c, 2, to, :] = values[3 + c] * (values[1 + c] - surf[c, 2, to, :])
    for i in range(FRAME // ROWS):
        rows = pl.ds(i * ROWS, ROWS)
        for t in range(3):
            fric[t, rows, :] = jnp.exp(logf[t, rows, :])
    coefficients(coef, visc, ice, fric, lane)
    steps = [layers_of(s) for s in (s0, s1, s2, s3)] + [lambda c, l: bottom.at[c]]
    for sweep in range(SWEEPS):
        for l in range(LAYERS - sweep):
            sweep_layer(coef, steps[sweep], steps[sweep + 1], l, lane, last=sweep == SWEEPS - 1)
    for copy in copies:
        copy.wait()

    def finish(i, carry):
        r = pl.multiple_of(i * ROWS, ROWS)
        rows, east, west = pl.ds(r + ROWS, ROWS), pl.ds(r + ROWS + 1, ROWS), pl.ds(r + ROWS - 1, ROWS)
        centre = [logf[t, rows, :] for t in range(3)]
        north, south = after(centre, lane), before(centre, lane)
        row = row_index() + r
        in_west = jnp.logical_or(row != 0, mx != 0)
        in_east = jnp.logical_or(row != TILE - 1, mx != size_x - 1)
        in_south = jnp.logical_or(lane != 0, me != 0)
        in_north = jnp.logical_or(lane != LANES - 1, me != n - 1)
        inner = pl.ds(r, ROWS)
        for t in range(2):
            c = centre[t]
            smooth = jnp.where(in_west, c - logf[t, west, :], 0.0) + jnp.where(in_east, c - logf[t, east, :], 0.0)
            left, right = c - south[t], c - north[t]
            smooth = smooth + (jnp.where(in_south, left, 0.0) if t == 0 else left)
            smooth = smooth + (jnp.where(in_north, right, 0.0) if t == 1 else right)
            total = TIKHONOV * smooth
            for component in range(2):
                along = coef[LAYERS - 1, I0_ + component, t, rows, :]
                for l in (2, 1, 0):
                    along = along * (coef[l, I0_ + component, t, rows, :] * coef[l, U_, t, rows, :])
                reach[component, t, inner, :] = along
                weight = fric[t, rows, :] * bed[component, t, inner, :]
                total = total + weight * bottom[component, t, rows, :]
                terms[1 + component, t, inner, :] = weight * along
            terms[0, t, inner, :] = total
        return carry

    lax.fori_loop(0, BLOCKS, finish, 0, unroll=8)


def gradient_kernel(n, strip_rows, terms, surf, rims, *rest):
    datas, force, grads = rest[:n], rest[n], rest[n + 1 :]
    me = lax.axis_index("gy")
    for k in range(n):
        source = lax.rem(me - k + n, n)
        for b in range(strip_rows // ROWS):
            row = source * strip_rows + b * ROWS
            inner = pl.ds(pl.multiple_of(row, ROWS), ROWS)
            rows = pl.ds(pl.multiple_of(ROWS + row, ROWS), ROWS)
            part = pl.ds(b * ROWS, ROWS)
            for t in range(2):
                total = terms[0, t, inner, :]
                for c in range(2):
                    value = datas[k][2 + c, t, part, :] * (datas[k][c, t, part, :] - surf[c, t, rows, :])
                    force[c, t, rows, :] = value
                    total = total + terms[1 + c, t, inner, :] * value
                grads[k][t, part, :] = total


def after_forcing(coef, s1, s2, s3, bottom, reach, force, out, n1, n2, n3, n4, sems):
    lane = lane_index()
    copies = []

    def send(l):
        for c in range(2):
            for t in range(2):
                source = n4.at[c * LAYERS + l, t, pl.ds(ROWS, TILE), :]
                target = out.at[c * LAYERS + l, :, pl.ds(t * LANES, LANES)]
                copy = pltpu.make_async_copy(source, target, sems.at[len(copies)])
                copy.start()
                copies.append(copy)

    for i in range(BLOCKS):
        rows, inner = pl.ds(ROWS + i * ROWS, ROWS), pl.ds(i * ROWS, ROWS)
        for t in range(2):
            for c in range(2):
                n4[c * LAYERS, t, rows, :] = bottom[c, t, rows, :] + reach[c, t, inner, :] * force[c, t, rows, :]
    send(0)

    def add_forcing(i, carry):
        rows = pl.ds(FIRST + i * ROWS, ROWS)
        for t in range(3):
            for c in range(2):
                value = coef[3, I0_ + c, t, rows, :] * force[c, t, rows, :]
                n1[c, t, rows, :] = s1[c * LAYERS + 3, t, rows, :] + value
                value = coef[2, I0_ + c, t, rows, :] * (coef[2, U_, t, rows, :] * value)
                n2[2 * c, t, rows, :] = s2[c * LAYERS + 2, t, rows, :] + value
                value = coef[1, I0_ + c, t, rows, :] * (coef[1, U_, t, rows, :] * value)
                n3[3 * c, t, rows, :] = s3[c * LAYERS + 1, t, rows, :] + value
        return carry

    lax.fori_loop(0, STEPS, add_forcing, 0, unroll=STEPS)

    def first(c, l):
        return n1.at[c] if l == 3 else s1.at[c * LAYERS + l]

    def second(c, l):
        return n2.at[2 * c + l - 2] if l >= 2 else s2.at[c * LAYERS + l]

    def third(c, l):
        return n3.at[3 * c + l - 1] if l >= 1 else s3.at[c * LAYERS + l]

    sweep_layer(coef, first, second, 3, lane, force)
    sweep_layer(coef, second, third, 2, lane)
    sweep_layer(coef, second, third, 3, lane, force)
    for l in (1, 2, 3):
        sweep_layer(coef, third, layers_of(n4), l, lane, force if l == 3 else None, last=True)
        send(l)
    for copy in copies:
        copy.wait()


def unpack_gradient(n, *refs):
    parts, out = refs[:n], refs[n]
    me = lax.axis_index("gy")
    for k in range(n):
        source = lax.rem(me + k, n)
        for t in range(2):
            out[:, pl.ds(pl.multiple_of(source * TILE + t * LANES, LANES), LANES)] = parts[k][t]


def f32(*shape):
    return jax.ShapeDtypeStruct(shape, jnp.float32)


def vmem_f32(*shape):
    return pltpu.VMEM(shape, jnp.float32)


def frames(*leading):
    return vmem_f32(*leading, 3, FRAME, LANES)


def in_vmem(x):
    return pltpu.with_memory_space_constraint(x, pltpu.VMEM)


def in_hbm(x):
    return pltpu.with_memory_space_constraint(x, pltpu.HBM)


def per_device(
    adjoint_start,
    viscosity,
    base_velocity,
    surface_velocity,
    ice_mask,
    log_friction,
    observed_velocity,
    obs_weight,
):
    n = lax.axis_size("gy")
    size_x = lax.axis_size("gx")
    strip_rows = log_friction.shape[0]
    width = n * TILE
    vmem = pl.BlockSpec(memory_space=pltpu.VMEM)
    smem = pl.BlockSpec(memory_space=pltpu.SMEM)
    anywhere = pl.BlockSpec(memory_space=pl.ANY)
    ice_mask = in_hbm(ice_mask)
    adjoint = adjoint_start.reshape((2 * LAYERS, TILE, TILE))

    def params(mib):
        return pltpu.CompilerParams(vmem_limit_bytes=mib * MIB)

    def ring(k):
        return [(i, (i + k) % n) for i in range(n)]

    def line(size, k):
        return [(i, i + k) for i in range(size) if 0 <= i + k < size]

    def control_shape(k):
        return f32(control_rows(strip_rows) + (HALF if k in (1, n - 1) else 0), LANES)

    *controls, state, visc, surf = pl.pallas_call(
        functools.partial(pack_kernel, n, strip_rows),
        out_shape=[control_shape(k) for k in range(n)] + [frames(2 * LAYERS), frames(LAYERS), frames(2)],
        in_specs=[smem] + [anywhere] * 6,
        out_specs=[vmem] * (n + 3),
        scratch_shapes=[
            vmem_f32(strip_rows, width),
            vmem_f32(2, strip_rows, width),
            vmem_f32(2, strip_rows, width),
            pltpu.SemaphoreType.DMA((3 + 12 * CHUNKS,)),
        ],
        compiler_params=params(6),
    )(
        ice_mask,
        in_hbm(log_friction),
        in_hbm(observed_velocity),
        in_hbm(obs_weight),
        in_hbm(adjoint),
        in_hbm(viscosity),
        in_hbm(surface_velocity),
    )
    state, visc, surf = in_vmem(state), in_vmem(visc), in_vmem(surf)
    controls, observed_velocity, obs_weight = lax.optimization_barrier((controls, observed_velocity, obs_weight))
    datas = pl.pallas_call(
        functools.partial(pack_observations, n, strip_rows),
        out_shape=[f32(4, 2, strip_rows, LANES)] * n,
        in_specs=[anywhere] * 2,
        out_specs=[anywhere] * n,
        scratch_shapes=[vmem_f32(2, strip_rows, width)] * 2 + [pltpu.SemaphoreType.DMA((4 * n,))],
        compiler_params=params(8),
    )(in_hbm(observed_velocity), in_hbm(obs_weight))
    datas = list(datas)
    controls = [controls[0]] + [lax.ppermute(controls[k], "gy", ring(k)) for k in range(1, n)]
    controls, sent = lax.optimization_barrier((controls, datas[1:]))
    datas = [datas[0]] + [lax.ppermute(sent[k - 1], "gy", ring(k)) for k in range(1, n)]

    rows_up, rows_down = pl.pallas_call(
        functools.partial(pack_rows, n, strip_rows),
        out_shape=[f32(PAIRS, 3, ROWS, LANES)] * 2,
        in_specs=[smem] + [vmem] * (3 + n),
        out_specs=[vmem] * 2,
        scratch_shapes=[vmem_f32(2, 5, 3, ROWS, LANES)],
        compiler_params=params(4),
    )(ice_mask, state, visc, surf, *controls)
    above = lax.ppermute(rows_up, "gx", line(size_x, 1))
    below = lax.ppermute(rows_down, "gx", line(size_x, -1))

    _, _, surf, *held, force = pl.pallas_call(
        functools.partial(before_forcing, n, strip_rows),
        out_shape=[
            frames(2 * LAYERS),
            frames(LAYERS),
            frames(2),
            frames(LAYERS, 9),
            frames(2 * LAYERS),
            frames(2 * LAYERS),
            frames(2 * LAYERS),
            vmem_f32(2, 2, FRAME, LANES),
            vmem_f32(3, 2, TILE, LANES),
            vmem_f32(2, 2, TILE, LANES),
            frames(2),
        ],
        in_specs=[smem] + [vmem] * 3 + [anywhere] + [vmem] * (2 + n),
        out_specs=[vmem] * 11,
        scratch_shapes=[
            frames(),
            frames(),
            frames(),
            vmem_f32(2, 2, TILE, LANES),
            pltpu.SemaphoreType.DMA((2,)),
        ],
        input_output_aliases={1: 0, 2: 1, 3: 2},
        compiler_params=params(12),
    )(ice_mask, state, visc, surf, in_hbm(base_velocity), above, below, *controls)
    coef, s1, s2, s3, bottom, terms, reach = [in_vmem(x) for x in held]

    force, *grads = pl.pallas_call(
        functools.partial(gradient_kernel, n, strip_rows),
        out_shape=[frames(2)] + [f32(2, strip_rows, LANES)] * n,
        in_specs=[vmem] * (3 + n),
        out_specs=[vmem] * (1 + n),
        input_output_aliases={2: 0},
        compiler_params=params(6),
    )(terms, in_vmem(surf), in_vmem(force), *datas)
    parts = [grads[0]] + [lax.ppermute(grads[k], "gy", ring(n - k)) for k in range(1, n)]

    out = pl.pallas_call(
        after_forcing,
        out_shape=f32(2 * LAYERS, TILE, TILE),
        in_specs=[vmem] * 7,
        out_specs=anywhere,
        scratch_shapes=[
            frames(2),
            frames(4),
            frames(6),
            vmem_f32(2 * LAYERS, 2, FRAME, LANES),
            pltpu.SemaphoreType.DMA((16,)),
        ],
        compiler_params=params(12),
    )(coef, s1, s2, s3, bottom, reach, in_vmem(force))

    gradient = pl.pallas_call(
        functools.partial(unpack_gradient, n),
        out_shape=f32(strip_rows, width),
        in_specs=[vmem] * n,
        out_specs=vmem,
        compiler_params=params(4),
    )(*parts)
    return gradient, out.reshape(adjoint_start.shape)


def solution(mesh):
    placed = (
        P(None, None, "gx", "gy"),
        P(None, "gx", "gy"),
        P(None, "gx", "gy"),
        P(None, "gx", "gy"),
        P("gx", "gy"),
        P(("gx", "gy"), None),
        P(None, ("gx", "gy"), None),
        P(None, ("gx", "gy"), None),
    )
    return jax.shard_map(
        per_device,
        mesh=mesh,
        in_specs=placed,
        out_specs=(P(("gx", "gy"), None), P(None, None, "gx", "gy")),
        check_vma=False,
    )
```

time: 68.5 us -> 59.5 us (0.87)
  Pallas kernels: 32.9 us -> 26.9 us
  waiting for transfers between devices: 16.4 us -> 14.4 us
  local copies, waits for them, and re-layouts: 0.92 us -> 0 us
    pallas_call x1 -> x2, Pallas kernels: 10.5 us -> 7.78 us  [the longest x1 6.25 us: per_device(): pl.pallas_call(after_forcing, out_shape=f32(2 * LAYERS, TILE, TILE), in_s...]
    pallas_call x1, Pallas kernels: 5.76 us -> 3.86 us  [per_device(): pl.pallas_call(functools.partial(pack_kernel, n, strip_rows), out_shape=[...]
    ppermute x3, waiting for transfers between devices: 11.8 us -> 10 us  [per_device(): lax.ppermute(controls[k], 'gy', ring(k))]
    pallas_call x1, Pallas kernels: 14.8 us -> 13.4 us  [per_device(): pl.pallas_call(functools.partial(before_forcing, n, strip_rows), out_shap...]
    unnamed x16 -> x0, local copies, waits for them, and re-layouts: 0.92 us -> none
  transfers between devices with their start and end apart: 11 -> 11, of which waited for: 2 -> 2; matrix products, arithmetic and copies ran while one was open for 0% -> 0% of each run, Pallas kernels for 38% -> 37%
where the time goes in v3:
time: 59.5 us; the launch traced here: 59.2 us
  Pallas kernels  26.9 us (45%)
  starting transfers between devices  17.1 us (29%)
  waiting for transfers between devices  14.4 us (24%)
  between operations  0.76 us (1%)
    pallas_call x1, Pallas kernels, per_device(): pl.pallas_call(functools.partial(before_forcing, n, strip_rows), out_shap...  13.4 us
    ppermute x3, waiting for transfers between devices, per_device(): lax.ppermute(controls[k], 'gy', ring(k))  10 us
    pallas_call x1, Pallas kernels, per_device(): pl.pallas_call(after_forcing, out_shape=f32(2 * LAYERS, TILE, TILE), in_s...  6.25 us
    ppermute x3, starting transfers between devices, per_device(): lax.ppermute(controls[k], 'gy', ring(k))  4.66 us
    ppermute x1, waiting for transfers between devices, per_device(): below = lax.ppermute(rows_down, 'gx', line(size_x, -1))  4.37 us
    ppermute x1, starting transfers between devices, per_device(): above = lax.ppermute(rows_up, 'gx', line(size_x, 1))  4.06 us
    pallas_call x1, Pallas kernels, per_device(): pl.pallas_call(functools.partial(pack_kernel, n, strip_rows), out_shape=[...  3.86 us
    ppermute x3, starting transfers between devices, per_device(): lax.ppermute(sent[k - 1], 'gy', ring(k))  3.26 us
  transfers between devices with their start and end apart: 11, of which 2 were waited for; matrix products, arithmetic and copies ran while one was open for 0% of the time, Pallas kernels for 37%

profile of v3, /device:TPU:1, one launch (start us, length us, event | category | flops | bytes accessed | tf_op | source)
XLA Modules:
  0.0 59.2 jit_solution(6829963577876752121)
XLA Ops:
  0.6 3.9 %shard_map.95 = (f32[184,128]{1,0:T(8,128)S(1)}, f32[312,128]{1,0:T(8,128)S(1)}, f32[184,128]{1,0:T(8,128)S(1)}, f32[312,128]{1,0:T(8,128)S(1)}, f32[8,3,272,128...) custom-call(s32[2,2]{1,0:T(2,128)} %mask.5, f32[64,1024]{1,0:T(8,128)} %logf.1, ...), custom_call_target="tpu_custom_call" | custom-call | tf_op jit(solution)/shard_map/pallas_call | solution.py:569
  4.5 2.2 %collective-permute-start = (f32[312,128]{1,0:T(8,128)S(1)}, f32[312,128]{1,0:T(8,128)S(1)}, u32[]{:S(2)}, u32[]{:S(2)}) collective-permute-start(f32[312,128]{1,0:T(8,128)S(1)} %get-tuple-element.50), channel_id=1, source_target_pairs={{0,1},{1,2},{2,3},{3,0},{4,5},{5,6},{6,7},{7,4},{8,9},{9,10},{10,1... | collective-permute-start | bytes 479240 | tf_op jit(solution)/shard_map/ppermute | solution.py:601
  6.7 2.1 %collective-permute-start.2 = (f32[312,128]{1,0:T(8,128)S(1)}, f32[312,128]{1,0:T(8,128)S(1)}, u32[]{:S(2)}, u32[]{:S(2)}) collective-permute-start(f32[312,128]{1,0:T(8,128)S(1)} %get-tuple-element.52), channel_id=1, source_target_pairs={{0,3},{1,0},{2,1},{3,2},{4,7},{5,4},{6,5},{7,6},{8,11},{9,8},{10,9... | collective-permute-start | bytes 479240 | tf_op jit(solution)/shard_map/ppermute | solution.py:601
  8.8 0.4 collective-permute-start.1
  9.2 1.5 %shard_map.96 = (f32[4,2,64,128]{3,2,1,0:T(8,128)S(1)}, f32[4,2,64,128]{3,2,1,0:T(8,128)S(1)}, f32[4,2,64,128]{3,2,1,0:T(8,128)S(1)}, f32[4,2,64,128]{3,2,1,0:T(8,128)S(1)}) custom-call(f32[2,64,1024]{2,1,0:T(8,128)} %obs.2, f32[2,64,1024]{2,1,0:T(8,128)} %weight.2), custom_call_target="tpu_custom_call" | custom-call | tf_op jit(solution)/shard_map/pallas_call | solution.py:592
  10.7 10.0 %collective-permute-done.1.rest_2_ = f32[184,128]{1,0:T(8,128)S(1)} collective-permute-done((f32[184,128]{1,0:T(8,128)S(1)}, f32[184,128]{1,0:T(8,128)S(1)}, u32[]{:S(2)}, u32[]{:S(2)}) %collective-permute-start.1) | collective-permute-done | bytes 94240 | tf_op jit(solution)/shard_map/ppermute | solution.py:601
  20.7 0.0 collective-permute-done.rest_1_
  20.7 0.0 collective-permute-done.2.rest_3_
  20.7 0.0 collective-permute-start.5
  20.8 0.4 collective-permute-start.6
  21.1 2.9 %collective-permute-start.7 = (f32[4,2,64,128]{3,2,1,0:T(8,128)S(1)}, f32[4,2,64,128]{3,2,1,0:T(8,128)S(1)}, u32[]{:S(2)}, u32[]{:S(2)}) collective-permute-start(f32[4,2,64,128]{3,2,1,0:T(8,128)S(1)} %get-tuple-element.70), channel_id=1, source_target_pairs={{0,3},{1,0},{2,1},{3,2},{4,7},{5,4},{6,5},{7,6},{8,11},{9,8},{10,9... | collective-permute-start | bytes 786440 | tf_op jit(solution)/shard_map/ppermute | solution.py:603
  24.0 1.0 %shard_map.97 = (f32[10,3,8,128]{3,2,1,0:T(8,128)S(1)}, f32[10,3,8,128]{3,2,1,0:T(8,128)S(1)}) custom-call(s32[2,2]{1,0:T(2,128)} %mask.5, f32[8,3,272,128]{3,2,1,0:T(8,128)S(1)} %get-tuple-element.42.state.state_in, f32[4,3,272,128]{3,2,1,0:T(8,128)S(1)} %get-tuple-element.43.visc.visc_in, f32[2,3,272,128]{3,2,1,0:T(8,128)S(1)} %get-tuple-element.44.surf.surf_in, ...), custom_call_target="tpu_custom_call" | custom-call | tf_op jit(solution)/shard_map/pallas_call | solution.py:605
  25.0 4.1 %collective-permute-start.3 = (f32[10,3,8,128]{3,2,1,0:T(8,128)S(1)}, f32[10,3,8,128]{3,2,1,0:T(8,128)S(1)}, u32[]{:S(2)}, u32[]{:S(2)}) collective-permute-start(f32[10,3,8,128]{3,2,1,0:T(8,128)S(1)} %get-tuple-element.62), channel_id=1, source_target_pairs={{0,4},{4,8},{8,12},{12,16},{16,20},{20,24},{24,28},{1,5},{5,9},{9,... | collective-permute-start | bytes 368648 | tf_op jit(solution)/shard_map/ppermute | solution.py:613
  29.1 2.1 %collective-permute-start.4 = (f32[10,3,8,128]{3,2,1,0:T(8,128)S(1)}, f32[10,3,8,128]{3,2,1,0:T(8,128)S(1)}, u32[]{:S(2)}, u32[]{:S(2)}) collective-permute-start(f32[10,3,8,128]{3,2,1,0:T(8,128)S(1)} %get-tuple-element.63), channel_id=1, source_target_pairs={{4,0},{8,4},{12,8},{16,12},{20,16},{24,20},{28,24},{5,1},{9,5},{13... | collective-permute-start | bytes 368648 | tf_op jit(solution)/shard_map/ppermute | solution.py:614
  31.2 0.0 collective-permute-done.3.above
  31.2 4.4 %collective-permute-done.4.below = f32[10,3,8,128]{3,2,1,0:T(8,128)S(1)} collective-permute-done((f32[10,3,8,128]{3,2,1,0:T(8,128)S(1)}, f32[10,3,8,128]{3,2,1,0:T(8,128)S(1)}, u32[]{:S(2)}, u32[]{:S(2)}) %collective-permute-start.4) | collective-permute-done | bytes 122912 | tf_op jit(solution)/shard_map/ppermute | solution.py:614
  35.6 13.4 %shard_map.98 = (f32[8,3,272,128]{3,2,1,0:T(8,128)S(1)}, f32[4,3,272,128]{3,2,1,0:T(8,128)S(1)}, f32[2,3,272,128]{3,2,1,0:T(8,128)S(1)}, f32[4,9,3,272,128]{4,3,...) custom-call(s32[2,2]{1,0:T(2,128)} %mask.5, ...), custom_call_target="tpu_custom_call", output_to_operand_aliasing={{0}: (1, {}), {1}: (2, {}), {2}: (3, {})} | custom-call | tf_op jit(solution)/shard_map/pallas_call | solution.py:616
  49.0 0.0 collective-permute-done.5.rest_1_
  49.0 0.0 collective-permute-done.6.rest_2_
  49.0 0.0 collective-permute-done.7.rest_3_
  49.0 0.2 shard_map.99
  49.2 0.4 collective-permute-start.8
  49.6 1.2 %collective-permute-start.9 = (f32[2,64,128]{2,1,0:T(8,128)S(1)}, f32[2,64,128]{2,1,0:T(8,128)S(1)}, u32[]{:S(2)}, u32[]{:S(2)}) collective-permute-start(f32[2,64,128]{2,1,0:T(8,128)S(1)} %get-tuple-element.73), channel_id=1, source_target_pairs={{0,2},{1,3},{2,0},{3,1},{4,6},{5,7},{6,4},{7,5},{8,10},{9,11},{10,... | collective-permute-start | bytes 196616 | tf_op jit(solution)/shard_map/ppermute | solution.py:653
  50.8 1.4 %collective-permute-start.10 = (f32[2,64,128]{2,1,0:T(8,128)S(1)}, f32[2,64,128]{2,1,0:T(8,128)S(1)}, u32[]{:S(2)}, u32[]{:S(2)}) collective-permute-start(f32[2,64,128]{2,1,0:T(8,128)S(1)} %get-tuple-element.74), channel_id=1, source_target_pairs={{0,1},{1,2},{2,3},{3,0},{4,5},{5,6},{6,7},{7,4},{8,9},{9,10},{10,1... | collective-permute-start | bytes 196616 | tf_op jit(solution)/shard_map/ppermute | solution.py:653
  52.2 6.3 %shard_map.101 = f32[8,256,256]{2,1,0:T(8,128)} custom-call(f32[4,9,3,272,128]{4,3,2,1,0:T(8,128)S(1)} %get-tuple-element.75.coef, f32[8,3,272,128]{3,2,1,0:T(8,128)S(1)} %get-tuple-element.76.s1, f32[8,3,272,128]{3,2,1,0:T(8,128)S(1)} %get-tuple-element.77.s2, f32[8,3,272,128]{3,2,1,0:T(8,128)S(1)} %get-tuple-element.78.s3, ...), custom_call_target="tpu_custom_call" | custom-call | tf_op jit(solution)/shard_map/pallas_call | solution.py:655
  58.4 0.0 collective-permute-done.8.refs_1_
  58.4 0.0 collective-permute-done.9.refs_2_
  58.4 0.0 collective-permute-done.10.refs_3_
  58.4 0.7 %shard_map.100 = f32[64,1024]{1,0:T(8,128)} custom-call(f32[2,64,128]{2,1,0:T(8,128)S(1)} %get-tuple-element.71.refs_0_, f32[2,64,128]{2,1,0:T(8,128)S(1)} %collective-permute-done.8.refs_1_, f32[2,64,128]{2,1,0:T(8,128)S(1)} %collective-permute-done.9.refs_2_, f32[2,64,128]{2,1,0:T(8,128)S(1)} %collective-permute-done.10.refs_3_), custom_call_target="tpu_custom_call" | custom-call | tf_op jit(solution)/shard_map/pallas_call | solution.py:670
Async XLA Ops:
  4.5 16.2 %collective-permute-start = (f32[312,128]{1,0:T(8,128)S(1)}, f32[312,128]{1,0:T(8,128)S(1)}, u32[]{:S(2)}, u32[]{:S(2)}) collective-permute-start(f32[312,128]{1,0:T(8,128)S(1)} %get-tuple-element.50), channel_id=1, source_target_pairs={{0,1},{1,2},{2,3},{3,0},{4,5},{5,6},{6,7},{7,4},{8,9},{9,10},{10,1... | collective-permute-start | bytes 479240 | tf_op jit(solution)/shard_map/ppermute | solution.py:601
  6.7 14.1 %collective-permute-start.2 = (f32[312,128]{1,0:T(8,128)S(1)}, f32[312,128]{1,0:T(8,128)S(1)}, u32[]{:S(2)}, u32[]{:S(2)}) collective-permute-start(f32[312,128]{1,0:T(8,128)S(1)} %get-tuple-element.52), channel_id=1, source_target_pairs={{0,3},{1,0},{2,1},{3,2},{4,7},{5,4},{6,5},{7,6},{8,11},{9,8},{10,9... | collective-permute-start | bytes 479240 | tf_op jit(solution)/shard_map/ppermute | solution.py:601
  8.8 12.0 %collective-permute-start.1 = (f32[184,128]{1,0:T(8,128)S(1)}, f32[184,128]{1,0:T(8,128)S(1)}, u32[]{:S(2)}, u32[]{:S(2)}) collective-permute-start(f32[184,128]{1,0:T(8,128)S(1)} %get-tuple-element.51), channel_id=1, source_target_pairs={{0,2},{1,3},{2,0},{3,1},{4,6},{5,7},{6,4},{7,5},{8,10},{9,11},{10,... | collective-permute-start | bytes 282632 | tf_op jit(solution)/shard_map/ppermute | solution.py:601
  20.7 28.2 %collective-permute-start.5 = (f32[4,2,64,128]{3,2,1,0:T(8,128)S(1)}, f32[4,2,64,128]{3,2,1,0:T(8,128)S(1)}, u32[]{:S(2)}, u32[]{:S(2)}) collective-permute-start(f32[4,2,64,128]{3,2,1,0:T(8,128)S(1)} %get-tuple-element.68), channel_id=1, source_target_pairs={{0,1},{1,2},{2,3},{3,0},{4,5},{5,6},{6,7},{7,4},{8,9},{9,10},{10,1... | collective-permute-start | bytes 786440 | tf_op jit(solution)/shard_map/ppermute | solution.py:603
  20.8 28.2 %collective-permute-start.6 = (f32[4,2,64,128]{3,2,1,0:T(8,128)S(1)}, f32[4,2,64,128]{3,2,1,0:T(8,128)S(1)}, u32[]{:S(2)}, u32[]{:S(2)}) collective-permute-start(f32[4,2,64,128]{3,2,1,0:T(8,128)S(1)} %get-tuple-element.69), channel_id=1, source_target_pairs={{0,2},{1,3},{2,0},{3,1},{4,6},{5,7},{6,4},{7,5},{8,10},{9,11},{10,... | collective-permute-start | bytes 786440 | tf_op jit(solution)/shard_map/ppermute | solution.py:603
  21.1 27.9 %collective-permute-start.7 = (f32[4,2,64,128]{3,2,1,0:T(8,128)S(1)}, f32[4,2,64,128]{3,2,1,0:T(8,128)S(1)}, u32[]{:S(2)}, u32[]{:S(2)}) collective-permute-start(f32[4,2,64,128]{3,2,1,0:T(8,128)S(1)} %get-tuple-element.70), channel_id=1, source_target_pairs={{0,3},{1,0},{2,1},{3,2},{4,7},{5,4},{6,5},{7,6},{8,11},{9,8},{10,9... | collective-permute-start | bytes 786440 | tf_op jit(solution)/shard_map/ppermute | solution.py:603
  25.0 6.2 %collective-permute-start.3 = (f32[10,3,8,128]{3,2,1,0:T(8,128)S(1)}, f32[10,3,8,128]{3,2,1,0:T(8,128)S(1)}, u32[]{:S(2)}, u32[]{:S(2)}) collective-permute-start(f32[10,3,8,128]{3,2,1,0:T(8,128)S(1)} %get-tuple-element.62), channel_id=1, source_target_pairs={{0,4},{4,8},{8,12},{12,16},{16,20},{20,24},{24,28},{1,5},{5,9},{9,... | collective-permute-start | bytes 368648 | tf_op jit(solution)/shard_map/ppermute | solution.py:613
  29.1 6.5 %collective-permute-start.4 = (f32[10,3,8,128]{3,2,1,0:T(8,128)S(1)}, f32[10,3,8,128]{3,2,1,0:T(8,128)S(1)}, u32[]{:S(2)}, u32[]{:S(2)}) collective-permute-start(f32[10,3,8,128]{3,2,1,0:T(8,128)S(1)} %get-tuple-element.63), channel_id=1, source_target_pairs={{4,0},{8,4},{12,8},{16,12},{20,16},{24,20},{28,24},{5,1},{9,5},{13... | collective-permute-start | bytes 368648 | tf_op jit(solution)/shard_map/ppermute | solution.py:614
  49.2 9.2 %collective-permute-start.8 = (f32[2,64,128]{2,1,0:T(8,128)S(1)}, f32[2,64,128]{2,1,0:T(8,128)S(1)}, u32[]{:S(2)}, u32[]{:S(2)}) collective-permute-start(f32[2,64,128]{2,1,0:T(8,128)S(1)} %get-tuple-element.72), channel_id=1, source_target_pairs={{0,3},{1,0},{2,1},{3,2},{4,7},{5,4},{6,5},{7,6},{8,11},{9,8},{10,9... | collective-permute-start | bytes 196616 | tf_op jit(solution)/shard_map/ppermute | solution.py:653
  49.6 8.9 %collective-permute-start.9 = (f32[2,64,128]{2,1,0:T(8,128)S(1)}, f32[2,64,128]{2,1,0:T(8,128)S(1)}, u32[]{:S(2)}, u32[]{:S(2)}) collective-permute-start(f32[2,64,128]{2,1,0:T(8,128)S(1)} %get-tuple-element.73), channel_id=1, source_target_pairs={{0,2},{1,3},{2,0},{3,1},{4,6},{5,7},{6,4},{7,5},{8,10},{9,11},{10,... | collective-permute-start | bytes 196616 | tf_op jit(solution)/shard_map/ppermute | solution.py:653
  50.8 7.7 %collective-permute-start.10 = (f32[2,64,128]{2,1,0:T(8,128)S(1)}, f32[2,64,128]{2,1,0:T(8,128)S(1)}, u32[]{:S(2)}, u32[]{:S(2)}) collective-permute-start(f32[2,64,128]{2,1,0:T(8,128)S(1)} %get-tuple-element.74), channel_id=1, source_target_pairs={{0,1},{1,2},{2,3},{3,0},{4,5},{5,6},{6,7},{7,4},{8,9},{9,10},{10,1... | collective-permute-start | bytes 196616 | tf_op jit(solution)/shard_map/ppermute | solution.py:653

commit v4 on v3

--- a/solution.py
+++ b/solution.py
@@ -249,7 +249,15 @@
 E_, N_, S_, U_, V_, K0_, K1_, I0_, I1_ = range(9)
 
 
-def coefficients(coef, visc, ice, fric, lane):
+def over_blocks(step, count, ends):
+    if ends:
+        for i in (0, count - 1):
+            step(i, 0)
+    else:
+        lax.fori_loop(0, count, step, 0, unroll=True)
+
+
+def coefficients(coef, visc, ice, fric, lane, ends):
     def step(i, carry):
         r = FIRST + i * ROWS
         rows, east, west = pl.ds(r, ROWS), pl.ds(r + 1, ROWS), pl.ds(r - 1, ROWS)
@@ -287,10 +295,10 @@
                     coef[l, K0_ + c_, t, rows, :] = cells[t] - own * inverse
         return carry
 
-    lax.fori_loop(0, STEPS, step, 0, unroll=STEPS)
-
-
-def sweep_layer(coef, old, new, l, lane, force=None, last=False):
+    over_blocks(step, STEPS, ends)
+
+
+def sweep_layer(coef, old, new, l, lane, force=None, last=False, ends=False):
     first, steps, tiles = (ROWS, BLOCKS, 2) if last else (FIRST, STEPS, 3)
 
     def step(i, carry):
@@ -329,80 +337,63 @@
                 )
         return carry
 
-    lax.fori_loop(0, steps, step, 0, unroll=steps)
+    over_blocks(step, steps, ends)
+
+
+GROUP = 4
+
+
+def sweep_reached(coef, work, old, new, l, lane, force=None, last=False):
+    first, steps, tiles = (ROWS, BLOCKS, 2) if last else (FIRST, STEPS, 3)
+
+    def along_y(i, carry):
+        rows = pl.ds(i * ROWS, ROWS)
+        for c in range(2):
+            m = [old(c, l)[t, rows, :] for t in range(3)]
+            mn, ms = after(m, lane), before(m, lane)
+            for t in range(tiles):
+                y = coef[l, N_, t, rows, :] * mn[t] + coef[l, S_, t, rows, :] * ms[t]
+                work[0, c, t, rows, :] = 4.0 * y if c else y
+                work[1, c, t, rows, :] = mn[t] - ms[t]
+        return carry
+
+    lax.fori_loop(0, FRAME // ROWS, along_y, 0, unroll=True)
+
+    def block(i):
+        r = first + i * ROWS
+        rows, east, west = pl.ds(r, ROWS), pl.ds(r + 1, ROWS), pl.ds(r - 1, ROWS)
+        for t in range(tiles):
+            e, w = coef[l, E_, t, rows, :], coef[l, E_, t, west, :]
+            for c in range(2):
+                x = e * old(c, l)[t, east, :] + w * old(c, l)[t, west, :]
+                total = (x if c else 4.0 * x) + work[0, c, t, rows, :]
+                if l < LAYERS - 1:
+                    total = total + coef[l, U_, t, rows, :] * old(c, l + 1)[t, rows, :]
+                if l > 0:
+                    total = total + coef[l - 1, U_, t, rows, :] * old(c, l - 1)[t, rows, :]
+                if force is not None:
+                    total = total + force[c, t, rows, :]
+                mixed = work[1, 1 - c, t, east, :] - work[1, 1 - c, t, west, :]
+                total = total + coef[l, V_, t, rows, :] * mixed
+                value = coef[l, K0_ + c, t, rows, :] * old(c, l)[t, rows, :] + coef[l, I0_ + c, t, rows, :] * total
+                yield c, t, rows, value
+
+    for start in range(0, steps, GROUP):
+        results = [result for i in range(start, min(start + GROUP, steps)) for result in block(i)]
+        for c, t, rows, value in results:
+            new(c, l)[t, rows, :] = value
 
 
 def layers_of(ref):
     return lambda c, l: ref.at[c * LAYERS + l]
 
 
-def before_forcing(n, strip_rows, mask, state_in, visc_in, surf_in, base, above, below, *rest):
-    controls = rest[:n]
-    s0, visc, surf, coef, s1, s2, s3, bottom, terms, reach, force = rest[n : n + 11]
-    ice, logf, fric, bed, sems = rest[n + 11 :]
+def gradient_terms(n, coef, logf, fric, bed, bottom, terms, reach, lane, ends):
     me, mx = lax.axis_index("gy"), lax.axis_index("gx")
     size_x = lax.axis_size("gx")
-    lane = lane_index()
-    blocks = strip_rows // ROWS
-    copies = start_copies(sems, [(base.at[:, :, pl.ds(t * LANES, LANES)], bed.at[:, t]) for t in range(2)])
-
-    for h in range(2):
-        for t in range(2):
-            ice[t, pl.ds(ROWS + h * HALF, HALF), :] = jnp.full((HALF, LANES), mask[h, t].astype(jnp.float32))
-    for message, row in ((above, 0), (below, ROWS + TILE)):
-        rows = pl.ds(row, ROWS)
-        for t in range(3):
-            for a in range(8):
-                s0[a, t, rows, :] = rim_rows(message, a, t)
-            for a in range(4):
-                visc[a, t, rows, :] = rim_rows(message, 8 + a, t)
-            ice[t, rows, :] = rim_rows(message, 14, t)
-            logf[t, rows, :] = rim_rows(message, 15, t)
-            for c in range(2):
-                difference = rim_rows(message, 16 + c, t) - rim_rows(message, 12 + c, t)
-                force[c, t, rows, :] = rim_rows(message, 18 + c, t) * difference
-
-    def sides(r, carry):
-        left, right = sides_at(n, strip_rows, controls, r * ROWS)
-        for h in range(2):
-            to = pl.ds(pl.multiple_of(ROWS + h * HALF + r * ROWS, ROWS), ROWS)
-            for a in range(TILE_FIELDS):
-                value = side_columns(lane, left, right, h * TILE_FIELDS + a)
-                if a == TILE_FIELDS - 1:
-                    ice[2, to, :] = value
-                else:
-                    tile_field(a, s0, visc, surf)[2, to, :] = value
-        return carry
-
-    lax.fori_loop(0, HALF // ROWS, sides, 0, unroll=8)
-    for k in range(n):
-        source = lax.rem(me - k + n, n)
-        for b in range(blocks):
-            to = pl.ds(pl.multiple_of(ROWS + source * strip_rows + b * ROWS, ROWS), ROWS)
-            for t in range(2):
-                logf[t, to, :] = controls[k][pl.ds(t * strip_rows + b * ROWS, ROWS), :]
-            values = []
-            for a in range(5):
-                part, slot = rim_slot(a, b, blocks)
-                packed = controls[k][pl.ds(2 * strip_rows + EDGE_ROWS + part * ROWS, ROWS), :]
-                values.append(strip_columns(lane, packed, slot))
-            logf[2, to, :] = values[0]
-            for c in range(2):
-                force[c, 2, to, :] = values[3 + c] * (values[1 + c] - surf[c, 2, to, :])
-    for i in range(FRAME // ROWS):
-        rows = pl.ds(i * ROWS, ROWS)
-        for t in range(3):
-            fric[t, rows, :] = jnp.exp(logf[t, rows, :])
-    coefficients(coef, visc, ice, fric, lane)
-    steps = [layers_of(s) for s in (s0, s1, s2, s3)] + [lambda c, l: bottom.at[c]]
-    for sweep in range(SWEEPS):
-        for l in range(LAYERS - sweep):
-            sweep_layer(coef, steps[sweep], steps[sweep + 1], l, lane, last=sweep == SWEEPS - 1)
-    for copy in copies:
-        copy.wait()
 
     def finish(i, carry):
-        r = pl.multiple_of(i * ROWS, ROWS)
+        r = i * ROWS
         rows, east, west = pl.ds(r + ROWS, ROWS), pl.ds(r + ROWS + 1, ROWS), pl.ds(r + ROWS - 1, ROWS)
         centre = [logf[t, rows, :] for t in range(3)]
         north, south = after(centre, lane), before(centre, lane)
@@ -430,7 +421,92 @@
             terms[0, t, inner, :] = total
         return carry
 
-    lax.fori_loop(0, BLOCKS, finish, 0, unroll=8)
+    over_blocks(finish, BLOCKS, ends)
+
+
+def sweeps_without_forcing(coef, s0, s1, s2, s3, bottom, lane, ends):
+    steps = [layers_of(s) for s in (s0, s1, s2, s3)] + [lambda c, l: bottom.at[c]]
+    for sweep in range(SWEEPS):
+        for l in range(LAYERS - sweep):
+            sweep_layer(coef, steps[sweep], steps[sweep + 1], l, lane, last=sweep == SWEEPS - 1, ends=ends)
+
+
+def before_forcing(n, strip_rows, mask, state_in, visc_in, surf_in, base, *rest):
+    controls = rest[:n]
+    s0, visc, surf, coef, s1, s2, s3, bottom, terms, reach, force, ice, logf, fric, bed, sems = rest[n:]
+    me = lax.axis_index("gy")
+    lane = lane_index()
+    blocks = strip_rows // ROWS
+    copies = start_copies(sems, [(base.at[:, :, pl.ds(t * LANES, LANES)], bed.at[:, t]) for t in range(2)])
+
+    for h in range(2):
+        for t in range(2):
+            ice[t, pl.ds(ROWS + h * HALF, HALF), :] = jnp.full((HALF, LANES), mask[h, t].astype(jnp.float32))
+    zero = jnp.zeros((ROWS, LANES), jnp.float32)
+    for row in (0, ROWS + TILE):
+        rows = pl.ds(row, ROWS)
+        for t in range(3):
+            for a in range(12):
+                tile_field(a, s0, visc, surf)[t, rows, :] = zero
+            ice[t, rows, :] = zero
+            logf[t, rows, :] = zero
+
+    def sides(r, carry):
+        left, right = sides_at(n, strip_rows, controls, r * ROWS)
+        for h in range(2):
+            to = pl.ds(pl.multiple_of(ROWS + h * HALF + r * ROWS, ROWS), ROWS)
+            for a in range(TILE_FIELDS):
+                value = side_columns(lane, left, right, h * TILE_FIELDS + a)
+                if a == TILE_FIELDS - 1:
+                    ice[2, to, :] = value
+                else:
+                    tile_field(a, s0, visc, surf)[2, to, :] = value
+        return carry
+
+    lax.fori_loop(0, HALF // ROWS, sides, 0, unroll=8)
+    for k in range(n):
+        source = lax.rem(me - k + n, n)
+        for b in range(blocks):
+            to = pl.ds(pl.multiple_of(ROWS + source * strip_rows + b * ROWS, ROWS), ROWS)
+            for t in range(2):
+                logf[t, to, :] = controls[k][pl.ds(t * strip_rows + b * ROWS, ROWS), :]
+            values = []
+            for a in range(5):
+                part, slot = rim_slot(a, b, blocks)
+                packed = controls[k][pl.ds(2 * strip_rows + EDGE_ROWS + part * ROWS, ROWS), :]
+                values.append(strip_columns(lane, packed, slot))
+            logf[2, to, :] = values[0]
+            for c in range(2):
+                force[c, 2, to, :] = values[3 + c] * (values[1 + c] - surf[c, 2, to, :])
+    for i in range(FRAME // ROWS):
+        rows = pl.ds(i * ROWS, ROWS)
+        for t in range(3):
+            fric[t, rows, :] = jnp.exp(logf[t, rows, :])
+    coefficients(coef, visc, ice, fric, lane, False)
+    sweeps_without_forcing(coef, s0, s1, s2, s3, bottom, lane, False)
+    for copy in copies:
+        copy.wait()
+    gradient_terms(n, coef, logf, fric, bed, bottom, terms, reach, lane, False)
+
+
+def at_edges(n, bed, above, below, *rest):
+    s0, visc, coef, s1, s2, s3, bottom, terms, reach, force, ice, logf, fric = rest[13:]
+    lane = lane_index()
+    for message, row in ((above, 0), (below, ROWS + TILE)):
+        rows = pl.ds(row, ROWS)
+        for t in range(3):
+            for a in range(12):
+                tile_field(a, s0, visc, None)[t, rows, :] = rim_rows(message, a, t)
+            ice[t, rows, :] = rim_rows(message, 14, t)
+            value = rim_rows(message, 15, t)
+            logf[t, rows, :] = value
+            fric[t, rows, :] = jnp.exp(value)
+            for c in range(2):
+                difference = rim_rows(message, 16 + c, t) - rim_rows(message, 12 + c, t)
+                force[c, t, rows, :] = rim_rows(message, 18 + c, t) * difference
+    coefficients(coef, visc, ice, fric, lane, True)
+    sweeps_without_forcing(coef, s0, s1, s2, s3, bottom, lane, True)
+    gradient_terms(n, coef, logf, fric, bed, bottom, terms, reach, lane, True)
 
 
 def gradient_kernel(n, strip_rows, terms, surf, rims, *rest):
@@ -452,7 +528,7 @@
                 grads[k][t, part, :] = total
 
 
-def after_forcing(coef, s1, s2, s3, bottom, reach, force, out, n1, n2, n3, n4, sems):
+def after_forcing(coef, s1, s2, s3, bottom, reach, force, out, n1, n2, n3, n4, work, sems):
     lane = lane_index()
     copies = []
 
@@ -495,11 +571,11 @@
     def third(c, l):
         return n3.at[3 * c + l - 1] if l >= 1 else s3.at[c * LAYERS + l]
 
-    sweep_layer(coef, first, second, 3, lane, force)
-    sweep_layer(coef, second, third, 2, lane)
-    sweep_layer(coef, second, third, 3, lane, force)
+    sweep_reached(coef, work, first, second, 3, lane, force)
+    sweep_reached(coef, work, second, third, 2, lane)
+    sweep_reached(coef, work, second, third, 3, lane, force)
     for l in (1, 2, 3):
-        sweep_layer(coef, third, layers_of(n4), l, lane, force if l == 3 else None, last=True)
+        sweep_reached(coef, work, third, layers_of(n4), l, lane, force if l == 3 else None, last=True)
         send(l)
     for copy in copies:
         copy.wait()
@@ -523,7 +599,7 @@
 
 
 def frames(*leading):
-    return vmem_f32(*leading, 3, FRAME, LANES)
+    return vmem_f32(*leading, 3, FRAME + ROWS, LANES)
 
 
 def in_vmem(x):
@@ -613,34 +689,38 @@
     above = lax.ppermute(rows_up, "gx", line(size_x, 1))
     below = lax.ppermute(rows_down, "gx", line(size_x, -1))
 
-    _, _, surf, *held, force = pl.pallas_call(
+    held_shapes = [
+        frames(LAYERS, 9),
+        frames(2 * LAYERS),
+        frames(2 * LAYERS),
+        frames(2 * LAYERS),
+        vmem_f32(2, 2, FRAME, LANES),
+        vmem_f32(3, 2, TILE, LANES),
+        vmem_f32(2, 2, TILE, LANES),
+        frames(2),
+        frames(),
+        frames(),
+        frames(),
+    ]
+    state, visc, surf, *held, bed = pl.pallas_call(
         functools.partial(before_forcing, n, strip_rows),
-        out_shape=[
-            frames(2 * LAYERS),
-            frames(LAYERS),
-            frames(2),
-            frames(LAYERS, 9),
-            frames(2 * LAYERS),
-            frames(2 * LAYERS),
-            frames(2 * LAYERS),
-            vmem_f32(2, 2, FRAME, LANES),
-            vmem_f32(3, 2, TILE, LANES),
-            vmem_f32(2, 2, TILE, LANES),
-            frames(2),
-        ],
-        in_specs=[smem] + [vmem] * 3 + [anywhere] + [vmem] * (2 + n),
-        out_specs=[vmem] * 11,
-        scratch_shapes=[
-            frames(),
-            frames(),
-            frames(),
-            vmem_f32(2, 2, TILE, LANES),
-            pltpu.SemaphoreType.DMA((2,)),
-        ],
+        out_shape=[frames(2 * LAYERS), frames(LAYERS), frames(2)] + held_shapes + [vmem_f32(2, 2, TILE, LANES)],
+        in_specs=[smem] + [vmem] * 3 + [anywhere] + [vmem] * n,
+        out_specs=[vmem] * 15,
+        scratch_shapes=[pltpu.SemaphoreType.DMA((2,))],
         input_output_aliases={1: 0, 2: 1, 3: 2},
-        compiler_params=params(12),
-    )(ice_mask, state, visc, surf, in_hbm(base_velocity), above, below, *controls)
-    coef, s1, s2, s3, bottom, terms, reach = [in_vmem(x) for x in held]
+        compiler_params=params(6),
+    )(ice_mask, state, visc, surf, in_hbm(base_velocity), *controls)
+    edge_shapes = [frames(2 * LAYERS), frames(LAYERS)] + held_shapes
+    _, _, *held = pl.pallas_call(
+        functools.partial(at_edges, n),
+        out_shape=edge_shapes,
+        in_specs=[vmem] * (3 + len(edge_shapes)),
+        out_specs=[vmem] * len(edge_shapes),
+        input_output_aliases={3 + i: i for i in range(len(edge_shapes))},
+        compiler_params=params(4),
+    )(in_vmem(bed), above, below, *[in_vmem(x) for x in [state, visc] + held])
+    coef, s1, s2, s3, bottom, terms, reach, force = [in_vmem(x) for x in held[:8]]
 
     force, *grads = pl.pallas_call(
         functools.partial(gradient_kernel, n, strip_rows),
@@ -662,9 +742,10 @@
             frames(4),
             frames(6),
             vmem_f32(2 * LAYERS, 2, FRAME, LANES),
+            frames(2, 2),
             pltpu.SemaphoreType.DMA((16,)),
         ],
-        compiler_params=params(12),
+        compiler_params=params(18),
     )(coef, s1, s2, s3, bottom, reach, in_vmem(force))
 
     gradient = pl.pallas_call(

time: 59.5 us -> 58.8 us (0.988); the launches traced: 59.2 us -> 57.7 us
  waiting for transfers between devices: 14.4 us -> 10.1 us
  Pallas kernels: 26.9 us -> 29.5 us
    ppermute x1, waiting for transfers between devices: 4.37 us -> 0.01 us  [per_device(): below = lax.ppermute(rows_down, 'gx', line(size_x, -1))]
    pallas_call x1, Pallas kernels: 13.4 us -> 14.7 us  [per_device(): pl.pallas_call(functools.partial(before_forcing, n, strip_rows), out_shap...]
    pallas_call x0 -> x1, Pallas kernels: none -> 0.86 us  [per_device(): pl.pallas_call(functools.partial(at_edges, n), out_shape=edge_shapes, in_...]
  transfers between devices with their start and end apart: 11 -> 11, of which waited for: 2 -> 1; matrix products, arithmetic and copies ran while one was open for 0% -> 0% of each run, Pallas kernels for 37% -> 43%
where the time goes in v4:
time: 58.8 us; the launch traced here: 57.7 us
  Pallas kernels  29.5 us (50%)
  starting transfers between devices  17.4 us (30%)
  waiting for transfers between devices  10.1 us (17%)
  between operations  0.77 us (1%)
    pallas_call x1, Pallas kernels, per_device(): pl.pallas_call(functools.partial(before_forcing, n, strip_rows), out_shap...  14.7 us
    ppermute x3, waiting for transfers between devices, per_device(): lax.ppermute(controls[k], 'gy', ring(k))  10 us
    pallas_call x1, Pallas kernels, per_device(): pl.pallas_call(after_forcing, out_shape=f32(2 * LAYERS, TILE, TILE), in_s...  6.64 us
    ppermute x3, starting transfers between devices, per_device(): lax.ppermute(controls[k], 'gy', ring(k))  4.66 us
    ppermute x1, starting transfers between devices, per_device(): above = lax.ppermute(rows_up, 'gx', line(size_x, 1))  4.06 us
    pallas_call x1, Pallas kernels, per_device(): pl.pallas_call(functools.partial(pack_kernel, n, strip_rows), out_shape=[...  3.86 us
    ppermute x3, starting transfers between devices, per_device(): lax.ppermute(grads[k], 'gy', ring(n - k))  3.49 us
    ppermute x3, starting transfers between devices, per_device(): lax.ppermute(sent[k - 1], 'gy', ring(k))  3.26 us
  transfers between devices with their start and end apart: 11, of which 1 were waited for; matrix products, arithmetic and copies ran while one was open for 0% of the time, Pallas kernels for 43%

profile of v4, /device:TPU:1, one launch (start us, length us, event | category | flops | bytes accessed | tf_op | source)
XLA Modules:
  0.0 57.7 jit_solution(10918826508464128014)
XLA Ops:
  0.6 3.9 %shard_map.95 = (f32[184,128]{1,0:T(8,128)S(1)}, f32[312,128]{1,0:T(8,128)S(1)}, f32[184,128]{1,0:T(8,128)S(1)}, f32[312,128]{1,0:T(8,128)S(1)}, f32[8,3,280,128...) custom-call(s32[2,2]{1,0:T(2,128)} %mask.5, f32[64,1024]{1,0:T(8,128)} %logf.1, ...), custom_call_target="tpu_custom_call" | custom-call | tf_op jit(solution)/shard_map/pallas_call | solution.py:645
  4.5 2.2 %collective-permute-start = (f32[312,128]{1,0:T(8,128)S(1)}, f32[312,128]{1,0:T(8,128)S(1)}, u32[]{:S(2)}, u32[]{:S(2)}) collective-permute-start(f32[312,128]{1,0:T(8,128)S(1)} %get-tuple-element.64), channel_id=1, source_target_pairs={{0,1},{1,2},{2,3},{3,0},{4,5},{5,6},{6,7},{7,4},{8,9},{9,10},{10,1... | collective-permute-start | bytes 479240 | tf_op jit(solution)/shard_map/ppermute | solution.py:677
  6.7 2.1 %collective-permute-start.2 = (f32[312,128]{1,0:T(8,128)S(1)}, f32[312,128]{1,0:T(8,128)S(1)}, u32[]{:S(2)}, u32[]{:S(2)}) collective-permute-start(f32[312,128]{1,0:T(8,128)S(1)} %get-tuple-element.66), channel_id=1, source_target_pairs={{0,3},{1,0},{2,1},{3,2},{4,7},{5,4},{6,5},{7,6},{8,11},{9,8},{10,9... | collective-permute-start | bytes 479240 | tf_op jit(solution)/shard_map/ppermute | solution.py:677
  8.8 0.4 collective-permute-start.1
  9.2 1.5 %shard_map.96 = (f32[4,2,64,128]{3,2,1,0:T(8,128)S(1)}, f32[4,2,64,128]{3,2,1,0:T(8,128)S(1)}, f32[4,2,64,128]{3,2,1,0:T(8,128)S(1)}, f32[4,2,64,128]{3,2,1,0:T(8,128)S(1)}) custom-call(f32[2,64,1024]{2,1,0:T(8,128)} %obs.2, f32[2,64,1024]{2,1,0:T(8,128)} %weight.2), custom_call_target="tpu_custom_call" | custom-call | tf_op jit(solution)/shard_map/pallas_call | solution.py:668
  10.7 10.0 %collective-permute-done.1.rest_2_ = f32[184,128]{1,0:T(8,128)S(1)} collective-permute-done((f32[184,128]{1,0:T(8,128)S(1)}, f32[184,128]{1,0:T(8,128)S(1)}, u32[]{:S(2)}, u32[]{:S(2)}) %collective-permute-start.1) | collective-permute-done | bytes 94240 | tf_op jit(solution)/shard_map/ppermute | solution.py:677
  20.7 0.0 collective-permute-done.rest_1_
  20.7 0.0 collective-permute-done.2.rest_3_
  20.7 0.0 collective-permute-start.5
  20.8 0.4 collective-permute-start.6
  21.1 2.9 %collective-permute-start.7 = (f32[4,2,64,128]{3,2,1,0:T(8,128)S(1)}, f32[4,2,64,128]{3,2,1,0:T(8,128)S(1)}, u32[]{:S(2)}, u32[]{:S(2)}) collective-permute-start(f32[4,2,64,128]{3,2,1,0:T(8,128)S(1)} %get-tuple-element.98), channel_id=1, source_target_pairs={{0,3},{1,0},{2,1},{3,2},{4,7},{5,4},{6,5},{7,6},{8,11},{9,8},{10,9... | collective-permute-start | bytes 786440 | tf_op jit(solution)/shard_map/ppermute | solution.py:679
  24.0 1.0 %shard_map.98 = (f32[10,3,8,128]{3,2,1,0:T(8,128)S(1)}, f32[10,3,8,128]{3,2,1,0:T(8,128)S(1)}) custom-call(s32[2,2]{1,0:T(2,128)} %mask.5, f32[8,3,280,128]{3,2,1,0:T(8,128)S(1)} %get-tuple-element.56.state_in.state, f32[4,3,280,128]{3,2,1,0:T(8,128)S(1)} %get-tuple-element.57.visc_in.visc, f32[2,3,280,128]{3,2,1,0:T(8,128)S(1)} %get-tuple-element.58.surf_in.surf, ...), custom_call_target="tpu_custom_call" | custom-call | tf_op jit(solution)/shard_map/pallas_call | solution.py:681
  25.0 4.1 %collective-permute-start.3 = (f32[10,3,8,128]{3,2,1,0:T(8,128)S(1)}, f32[10,3,8,128]{3,2,1,0:T(8,128)S(1)}, u32[]{:S(2)}, u32[]{:S(2)}) collective-permute-start(f32[10,3,8,128]{3,2,1,0:T(8,128)S(1)} %get-tuple-element.77), channel_id=1, source_target_pairs={{0,4},{4,8},{8,12},{12,16},{16,20},{20,24},{24,28},{1,5},{5,9},{9,... | collective-permute-start | bytes 368648 | tf_op jit(solution)/shard_map/ppermute | solution.py:689
  29.1 1.9 %collective-permute-start.4 = (f32[10,3,8,128]{3,2,1,0:T(8,128)S(1)}, f32[10,3,8,128]{3,2,1,0:T(8,128)S(1)}, u32[]{:S(2)}, u32[]{:S(2)}) collective-permute-start(f32[10,3,8,128]{3,2,1,0:T(8,128)S(1)} %get-tuple-element.78), channel_id=1, source_target_pairs={{4,0},{8,4},{12,8},{16,12},{20,16},{24,20},{28,24},{5,1},{9,5},{13... | collective-permute-start | bytes 368648 | tf_op jit(solution)/shard_map/ppermute | solution.py:690
  31.0 14.7 %shard_map.97 = (f32[8,3,280,128]{3,2,1,0:T(8,128)S(1)}, f32[4,3,280,128]{3,2,1,0:T(8,128)S(1)}, f32[2,3,280,128]{3,2,1,0:T(8,128)S(1)}, f32[4,9,3,280,128]{4,3,...) custom-call(s32[2,2]{1,0:T(2,128)} %mask.5, ...), custom_call_target="tpu_custom_call", output_to_operand_aliasing={{0}: (1, {}), {1}: (2, {}), {2}: (3, {})} | custom-call | tf_op jit(solution)/shard_map/pallas_call | solution.py:705
  45.7 0.0 collective-permute-done.3.above
  45.7 0.0 collective-permute-done.4.below
  45.7 0.9 %shard_map.99 = (f32[8,3,280,128]{3,2,1,0:T(8,128)S(1)}, f32[4,3,280,128]{3,2,1,0:T(8,128)S(1)}, f32[4,9,3,280,128]{4,3,2,1,0:T(8,128)S(1)}, f32[8,3,280,128]{3,...) custom-call(f32[2,2,256,128]{3,2,1,0:T(8,128)S(1)} %get-tuple-elemen, ...), custom_call_target="tpu_custom_call", output_to_operand_aliasing={{0}: (3, {}), {1}: (4, {}), {2}: (5, {}), {3}: (6, {}), {4}... | custom-call | tf_op jit(solution)/shard_map/pallas_call | solution.py:715
  46.6 0.0 collective-permute-done.5.rest_1_
  46.6 0.0 collective-permute-done.6.rest_2_
  46.6 0.0 collective-permute-done.7.rest_3_
  46.6 0.2 shard_map.100
  46.8 0.6 %collective-permute-start.8 = (f32[2,64,128]{2,1,0:T(8,128)S(1)}, f32[2,64,128]{2,1,0:T(8,128)S(1)}, u32[]{:S(2)}, u32[]{:S(2)}) collective-permute-start(f32[2,64,128]{2,1,0:T(8,128)S(1)} %get-tuple-element.100), channel_id=1, source_target_pairs={{0,3},{1,0},{2,1},{3,2},{4,7},{5,4},{6,5},{7,6},{8,11},{9,8},{10,9... | collective-permute-start | bytes 196616 | tf_op jit(solution)/shard_map/ppermute | solution.py:733
  47.4 1.5 %collective-permute-start.9 = (f32[2,64,128]{2,1,0:T(8,128)S(1)}, f32[2,64,128]{2,1,0:T(8,128)S(1)}, u32[]{:S(2)}, u32[]{:S(2)}) collective-permute-start(f32[2,64,128]{2,1,0:T(8,128)S(1)} %get-tuple-element.101), channel_id=1, source_target_pairs={{0,2},{1,3},{2,0},{3,1},{4,6},{5,7},{6,4},{7,5},{8,10},{9,11},{10,... | collective-permute-start | bytes 196616 | tf_op jit(solution)/shard_map/ppermute | solution.py:733
  48.9 1.4 %collective-permute-start.10 = (f32[2,64,128]{2,1,0:T(8,128)S(1)}, f32[2,64,128]{2,1,0:T(8,128)S(1)}, u32[]{:S(2)}, u32[]{:S(2)}) collective-permute-start(f32[2,64,128]{2,1,0:T(8,128)S(1)} %get-tuple-element.102), channel_id=1, source_target_pairs={{0,1},{1,2},{2,3},{3,0},{4,5},{5,6},{6,7},{7,4},{8,9},{9,10},{10,1... | collective-permute-start | bytes 196616 | tf_op jit(solution)/shard_map/ppermute | solution.py:733
  50.3 6.6 %shard_map.102 = f32[8,256,256]{2,1,0:T(8,128)} custom-call(f32[4,9,3,280,128]{4,3,2,1,0:T(8,128)S(1)} %get-tuple-element.103.coef, f32[8,3,280,128]{3,2,1,0:T(8,128)S(1)} %get-tuple-element.104.s1, f32[8,3,280,128]{3,2,1,0:T(8,128)S(1)} %get-tuple-element.105.s2, f32[8,3,280,128]{3,2,1,0:T(8,128)S(1)} %get-tuple-element.106.s3, ...), custom_call_target="tpu_custom_call" | custom-call | tf_op jit(solution)/shard_map/pallas_call | solution.py:735
  57.0 0.0 collective-permute-done.8.refs_1_
  57.0 0.0 collective-permute-done.9.refs_2_
  57.0 0.0 collective-permute-done.10.refs_3_
  57.0 0.7 %shard_map.101 = f32[64,1024]{1,0:T(8,128)} custom-call(f32[2,64,128]{2,1,0:T(8,128)S(1)} %get-tuple-element.99.refs_0_, f32[2,64,128]{2,1,0:T(8,128)S(1)} %collective-permute-done.8.refs_1_, f32[2,64,128]{2,1,0:T(8,128)S(1)} %collective-permute-done.9.refs_2_, f32[2,64,128]{2,1,0:T(8,128)S(1)} %collective-permute-done.10.refs_3_), custom_call_target="tpu_custom_call" | custom-call | tf_op jit(solution)/shard_map/pallas_call | solution.py:751
Async XLA Ops:
  4.5 16.2 %collective-permute-start = (f32[312,128]{1,0:T(8,128)S(1)}, f32[312,128]{1,0:T(8,128)S(1)}, u32[]{:S(2)}, u32[]{:S(2)}) collective-permute-start(f32[312,128]{1,0:T(8,128)S(1)} %get-tuple-element.64), channel_id=1, source_target_pairs={{0,1},{1,2},{2,3},{3,0},{4,5},{5,6},{6,7},{7,4},{8,9},{9,10},{10,1... | collective-permute-start | bytes 479240 | tf_op jit(solution)/shard_map/ppermute | solution.py:677
  6.7 14.1 %collective-permute-start.2 = (f32[312,128]{1,0:T(8,128)S(1)}, f32[312,128]{1,0:T(8,128)S(1)}, u32[]{:S(2)}, u32[]{:S(2)}) collective-permute-start(f32[312,128]{1,0:T(8,128)S(1)} %get-tuple-element.66), channel_id=1, source_target_pairs={{0,3},{1,0},{2,1},{3,2},{4,7},{5,4},{6,5},{7,6},{8,11},{9,8},{10,9... | collective-permute-start | bytes 479240 | tf_op jit(solution)/shard_map/ppermute | solution.py:677
  8.8 12.0 %collective-permute-start.1 = (f32[184,128]{1,0:T(8,128)S(1)}, f32[184,128]{1,0:T(8,128)S(1)}, u32[]{:S(2)}, u32[]{:S(2)}) collective-permute-start(f32[184,128]{1,0:T(8,128)S(1)} %get-tuple-element.65), channel_id=1, source_target_pairs={{0,2},{1,3},{2,0},{3,1},{4,6},{5,7},{6,4},{7,5},{8,10},{9,11},{10,... | collective-permute-start | bytes 282632 | tf_op jit(solution)/shard_map/ppermute | solution.py:677
  20.7 25.9 %collective-permute-start.5 = (f32[4,2,64,128]{3,2,1,0:T(8,128)S(1)}, f32[4,2,64,128]{3,2,1,0:T(8,128)S(1)}, u32[]{:S(2)}, u32[]{:S(2)}) collective-permute-start(f32[4,2,64,128]{3,2,1,0:T(8,128)S(1)} %get-tuple-element.96), channel_id=1, source_target_pairs={{0,1},{1,2},{2,3},{3,0},{4,5},{5,6},{6,7},{7,4},{8,9},{9,10},{10,1... | collective-permute-start | bytes 786440 | tf_op jit(solution)/shard_map/ppermute | solution.py:679
  20.8 25.9 %collective-permute-start.6 = (f32[4,2,64,128]{3,2,1,0:T(8,128)S(1)}, f32[4,2,64,128]{3,2,1,0:T(8,128)S(1)}, u32[]{:S(2)}, u32[]{:S(2)}) collective-permute-start(f32[4,2,64,128]{3,2,1,0:T(8,128)S(1)} %get-tuple-element.97), channel_id=1, source_target_pairs={{0,2},{1,3},{2,0},{3,1},{4,6},{5,7},{6,4},{7,5},{8,10},{9,11},{10,... | collective-permute-start | bytes 786440 | tf_op jit(solution)/shard_map/ppermute | solution.py:679
  21.1 25.5 %collective-permute-start.7 = (f32[4,2,64,128]{3,2,1,0:T(8,128)S(1)}, f32[4,2,64,128]{3,2,1,0:T(8,128)S(1)}, u32[]{:S(2)}, u32[]{:S(2)}) collective-permute-start(f32[4,2,64,128]{3,2,1,0:T(8,128)S(1)} %get-tuple-element.98), channel_id=1, source_target_pairs={{0,3},{1,0},{2,1},{3,2},{4,7},{5,4},{6,5},{7,6},{8,11},{9,8},{10,9... | collective-permute-start | bytes 786440 | tf_op jit(solution)/shard_map/ppermute | solution.py:679
  25.0 20.7 %collective-permute-start.3 = (f32[10,3,8,128]{3,2,1,0:T(8,128)S(1)}, f32[10,3,8,128]{3,2,1,0:T(8,128)S(1)}, u32[]{:S(2)}, u32[]{:S(2)}) collective-permute-start(f32[10,3,8,128]{3,2,1,0:T(8,128)S(1)} %get-tuple-element.77), channel_id=1, source_target_pairs={{0,4},{4,8},{8,12},{12,16},{16,20},{20,24},{24,28},{1,5},{5,9},{9,... | collective-permute-start | bytes 368648 | tf_op jit(solution)/shard_map/ppermute | solution.py:689
  29.1 16.7 %collective-permute-start.4 = (f32[10,3,8,128]{3,2,1,0:T(8,128)S(1)}, f32[10,3,8,128]{3,2,1,0:T(8,128)S(1)}, u32[]{:S(2)}, u32[]{:S(2)}) collective-permute-start(f32[10,3,8,128]{3,2,1,0:T(8,128)S(1)} %get-tuple-element.78), channel_id=1, source_target_pairs={{4,0},{8,4},{12,8},{16,12},{20,16},{24,20},{28,24},{5,1},{9,5},{13... | collective-permute-start | bytes 368648 | tf_op jit(solution)/shard_map/ppermute | solution.py:690
  46.8 10.1 %collective-permute-start.8 = (f32[2,64,128]{2,1,0:T(8,128)S(1)}, f32[2,64,128]{2,1,0:T(8,128)S(1)}, u32[]{:S(2)}, u32[]{:S(2)}) collective-permute-start(f32[2,64,128]{2,1,0:T(8,128)S(1)} %get-tuple-element.100), channel_id=1, source_target_pairs={{0,3},{1,0},{2,1},{3,2},{4,7},{5,4},{6,5},{7,6},{8,11},{9,8},{10,9... | collective-permute-start | bytes 196616 | tf_op jit(solution)/shard_map/ppermute | solution.py:733
  47.4 9.5 %collective-permute-start.9 = (f32[2,64,128]{2,1,0:T(8,128)S(1)}, f32[2,64,128]{2,1,0:T(8,128)S(1)}, u32[]{:S(2)}, u32[]{:S(2)}) collective-permute-start(f32[2,64,128]{2,1,0:T(8,128)S(1)} %get-tuple-element.101), channel_id=1, source_target_pairs={{0,2},{1,3},{2,0},{3,1},{4,6},{5,7},{6,4},{7,5},{8,10},{9,11},{10,... | collective-permute-start | bytes 196616 | tf_op jit(solution)/shard_map/ppermute | solution.py:733
  48.9 8.1 %collective-permute-start.10 = (f32[2,64,128]{2,1,0:T(8,128)S(1)}, f32[2,64,128]{2,1,0:T(8,128)S(1)}, u32[]{:S(2)}, u32[]{:S(2)}) collective-permute-start(f32[2,64,128]{2,1,0:T(8,128)S(1)} %get-tuple-element.102), channel_id=1, source_target_pairs={{0,1},{1,2},{2,3},{3,0},{4,5},{5,6},{6,7},{7,4},{8,9},{9,10},{10,1... | collective-permute-start | bytes 196616 | tf_op jit(solution)/shard_map/ppermute | solution.py:733
